TPU v7x, 128 devices: a whole 4x4x4 slice. The times are simulated.
128 devices in a mesh: lat: 16 (over x, z_hi, core), lon: 8 (over z_lo, y).
Axes of the slice: x: 4, y: 4, z: 4 (z_hi: 2, z_lo: 2; z = z_hi * 2 + z_lo), core: 2. Of those that a mesh axis runs over, the one named last changes fastest.
Arguments:
- fields: bfloat16 [3, 64, 128, 512], P(None, 'lat', 'lon'), may hold values from -6 to 6
- land_sea: int32 [64, 128], P('lat', 'lon'), may hold values 0 or 1
- surface_embed: bfloat16 [2, 512], replicated, may hold values from -4 to 4
- norm_gains: float32 [2, 512], replicated, may hold values from 0.1 to 1.9
- w_qkv: bfloat16 [512, 1536], replicated, may hold values from -0.25 to 0.25
- head_scales: float32 [8], replicated, may hold values from 2 to 20
- w_out: bfloat16 [512, 512], replicated, may hold values from -0.25 to 0.25
- w_up: bfloat16 [512, 2048], replicated, may hold values from -0.25 to 0.25
- w_down: bfloat16 [2048, 512], replicated, may hold values from -0.125 to 0.125
- cotangent: bfloat16 [3, 64, 128, 512], P(None, 'lat', 'lon'), may hold values from -6 to 6
Outputs:
- layer_out: bfloat16 [3, 64, 128, 512], P(None, 'lat', 'lon')
- grad_fields: bfloat16 [3, 64, 128, 512], P(None, 'lat', 'lon')
- grad_qkv: float32 [512, 1536], P(('lat', 'lon'))
- grad_out: float32 [512, 512], P(('lat', 'lon'))
- grad_up: float32 [512, 2048], P(('lat', 'lon'))
- grad_down: float32 [2048, 512], P(('lat', 'lon'))
- grad_gains: float32 [2, 512], P(None, ('lat', 'lon'))
Inputs may be any that keep to these rules, and one draw needn't show every extreme that they name: `land_sea`: 1 marks land, 0 sea.
All inputs are finite; a program needn't handle non-finite values. No bound on the sum of `land_sea` on one device may be relied on, other than what follows from the above.
Results may differ from a plain program's by a relative error of at most 0.025.
Values may be sent and summed in bfloat16 or wider, within the bound.
No kernel may reach another device: no remote copies, remote signals or barrier semaphores. Data moves between devices by JAX's collectives and lax.ppermute only.
A program may use at most 128 MiB of HBM per device.

v0:
```python
from functools import partial
import math

import jax
import jax.numpy as jnp
from jax import lax
from jax.sharding import PartitionSpec as P


def with_halo(array, sides, width):
    for axis, dim in sides:
        devices, length = (lax.axis_size(axis), array.shape[dim])
        up = [(i, (i + 1) % devices) for i in range(devices - 1)]
        down = [(j, i) for i, j in up]
        last = lax.slice_in_dim(array, length - width, length, axis=dim)
        initial = lax.slice_in_dim(array, 0, width, axis=dim)
        before = lax.ppermute(last, axis, up)
        after = lax.ppermute(initial, axis, down)
        array = jnp.concatenate([before, array, after], axis=dim)
    return array


def layer_norm(values, gain_row):
    row_mean = jnp.mean(values, axis=-1, keepdims=True)
    centred = values - row_mean
    variance = jnp.mean(centred * centred, axis=-1, keepdims=True)
    return centred * lax.rsqrt(variance + 1e-05) * gain_row


def unit_heads(values, head_count):
    shaped = values.reshape(values.shape[:-1] + (head_count, values.shape[-1] // head_count))
    scaled = shaped * lax.rsqrt(jnp.sum(shaped * shaped, axis=-1, keepdims=True) + 1e-06)
    return scaled.reshape(values.shape)


def attend(query_block, key_block, value_block, key_valid, head_scales):
    scores = (
        jnp.einsum("qhe,khe->hqk", query_block, key_block, preferred_element_type=jnp.float32)
        * head_scales[:, None, None]
    )
    exp_scores = jnp.exp(scores) * key_valid[None, None, :]
    inverse = 1.0 / jnp.sum(exp_scores, axis=2)
    attn_probs = (exp_scores * inverse[:, :, None]).astype(jnp.bfloat16)
    attended = jnp.einsum(
        "hqk,khe->qhe", attn_probs, value_block, preferred_element_type=jnp.float32
    ).astype(jnp.bfloat16)
    return (attended, attn_probs)


def attend_back(query_block, key_block, value_block, attn_probs, attended, grad_block, head_scales):
    row_delta = jnp.sum(grad_block.astype(jnp.float32) * attended.astype(jnp.float32), axis=2).T
    grad_probs = jnp.einsum(
        "qhe,khe->hqk", grad_block, value_block, preferred_element_type=jnp.float32
    )
    grad_scores = (
        attn_probs.astype(jnp.float32)
        * (grad_probs - row_delta[:, :, None])
        * head_scales[:, None, None]
    ).astype(jnp.bfloat16)
    grad_query = jnp.einsum(
        "hqk,khe->qhe", grad_scores, key_block, preferred_element_type=jnp.float32
    )
    grad_key = jnp.einsum(
        "hqk,qhe->khe", grad_scores, query_block, preferred_element_type=jnp.float32
    )
    grad_value = jnp.einsum(
        "hqk,qhe->khe", attn_probs, grad_block, preferred_element_type=jnp.float32
    )
    return (grad_query, grad_key, grad_value)


def fold_rims(grad_rows_ext, moved_rims, half_window, own_rows):
    inner_rows = grad_rows_ext[:, :, half_window : half_window + own_rows]
    upper_part = inner_rows[:, :, :half_window] + moved_rims[:, :, :half_window]
    lower_part = inner_rows[:, :, half_window:] + moved_rims[:, :, 3 * half_window :]
    return jnp.concatenate([upper_part, lower_part], axis=2)


def rim_rows_of(grad_rows_ext, half_window, own_rows):
    return jnp.concatenate(
        [grad_rows_ext[:, :, :half_window], grad_rows_ext[:, :, 2 * own_rows - half_window :]],
        axis=2,
    )


def shards(
    fields, land_sea, surface_embed, norm_gains, w_qkv, head_scales, w_out, w_up, w_down, cotangent
):
    levels, own_rows, own_cols, width = fields.shape
    token_count = levels * own_rows * own_cols
    lat_devices = lax.axis_size("lat")
    lon_devices = lax.axis_size("lon")
    all_cols = own_cols * lon_devices
    half_window = own_rows // 2
    head_count = head_scales.shape[0]
    head_width = width // head_count
    chosen = jnp.where(
        land_sea[None, :, :, None] == 1,
        surface_embed[1].astype(jnp.float32),
        surface_embed[0].astype(jnp.float32),
    )
    hidden = (fields.astype(jnp.float32) + chosen).astype(jnp.bfloat16)
    hidden_wide = hidden.reshape(token_count, width).astype(jnp.float32)
    normed_wide, norm_back_one = jax.vjp(layer_norm, hidden_wide, norm_gains[0])
    normed = normed_wide.astype(jnp.bfloat16)
    projected = jnp.dot(normed, w_qkv, preferred_element_type=jnp.float32)
    unit_fn = partial(unit_heads, head_count=head_count)
    query_wide, query_back = jax.vjp(unit_fn, projected[:, :width])
    key_wide, key_back = jax.vjp(unit_fn, projected[:, width : 2 * width])
    query_unit = query_wide.astype(jnp.bfloat16)
    key_value = jnp.stack(
        [key_wide.astype(jnp.bfloat16), projected[:, 2 * width :].astype(jnp.bfloat16)]
    )
    key_value = key_value.reshape(2, levels, own_rows, own_cols, width)
    wide_rows = lax.all_gather(key_value, "lon", axis=3, tiled=True)
    key_value_ext = with_halo(wide_rows, (("lat", 2),), half_window)
    first_row = lax.axis_index("lat") * own_rows - half_window
    ext_index = first_row + jnp.arange(2 * own_rows, dtype=jnp.int32)
    row_valid = ((ext_index >= 0) & (ext_index < own_rows * lat_devices)).astype(jnp.float32)
    query_grid = query_unit.reshape(levels, own_rows, own_cols, head_count, head_width)
    query_blocks = []
    key_blocks = []
    value_blocks = []
    prob_blocks = []
    attended_blocks = []
    for window_index in range(2):
        query_block = query_grid[
            :, window_index * half_window : (window_index + 1) * half_window
        ].reshape(-1, head_count, head_width)
        rows_slice = key_value_ext[:, :, window_index * own_rows : (window_index + 1) * own_rows]
        key_block = rows_slice[0].reshape(-1, head_count, head_width)
        value_block = rows_slice[1].reshape(-1, head_count, head_width)
        valid_rows = row_valid[window_index * own_rows : (window_index + 1) * own_rows]
        key_valid = jnp.broadcast_to(
            valid_rows[None, :, None], (levels, own_rows, all_cols)
        ).reshape(-1)
        attended_block, attn_probs = attend(
            query_block, key_block, value_block, key_valid, head_scales
        )
        query_blocks.append(query_block)
        key_blocks.append(key_block)
        value_blocks.append(value_block)
        prob_blocks.append(attn_probs)
        attended_blocks.append(attended_block)
    attended_grid = jnp.concatenate(
        [block.reshape(levels, half_window, own_cols, width) for block in attended_blocks], axis=1
    )
    attended = attended_grid.reshape(token_count, width)
    mixed = (hidden_wide + jnp.dot(attended, w_out, preferred_element_type=jnp.float32)).astype(
        jnp.bfloat16
    )
    mixed_wide = mixed.astype(jnp.float32)
    normed_two_wide, norm_back_two = jax.vjp(layer_norm, mixed_wide, norm_gains[1])
    normed_two = normed_two_wide.astype(jnp.bfloat16)
    pre_act = jnp.dot(normed_two, w_up, preferred_element_type=jnp.float32)
    act_wide, gelu_back = jax.vjp(jax.nn.gelu, pre_act)
    activated = act_wide.astype(jnp.bfloat16)
    layer_out = (
        mixed_wide + jnp.dot(activated, w_down, preferred_element_type=jnp.float32)
    ).astype(jnp.bfloat16)
    grad_rows = cotangent.reshape(token_count, width)
    grad_act = jnp.einsum("nd,fd->nf", grad_rows, w_down, preferred_element_type=jnp.float32)
    grad_pre = gelu_back(grad_act)[0].astype(jnp.bfloat16)
    grad_normed_two = jnp.einsum("nf,df->nd", grad_pre, w_up, preferred_element_type=jnp.float32)
    grad_mixed_part, grad_gain_two = norm_back_two(grad_normed_two)
    grad_mixed = grad_rows.astype(jnp.float32) + grad_mixed_part
    grad_mixed_low = grad_mixed.astype(jnp.bfloat16)
    grad_attended = jnp.einsum(
        "ne,de->nd", grad_mixed_low, w_out, preferred_element_type=jnp.float32
    ).astype(jnp.bfloat16)
    grad_attended_grid = grad_attended.reshape(levels, own_rows, own_cols, head_count, head_width)
    grad_query_blocks = []
    grad_kv_blocks = []
    for window_index in range(2):
        grad_block = grad_attended_grid[
            :, window_index * half_window : (window_index + 1) * half_window
        ].reshape(-1, head_count, head_width)
        grad_query, grad_key, grad_value = attend_back(
            query_blocks[window_index],
            key_blocks[window_index],
            value_blocks[window_index],
            prob_blocks[window_index],
            attended_blocks[window_index],
            grad_block,
            head_scales,
        )
        grad_query_blocks.append(grad_query.reshape(levels, half_window, own_cols, width))
        grad_kv_blocks.append(
            jnp.stack([grad_key, grad_value]).reshape(2, levels, own_rows, all_cols, width)
        )
    grad_query_rows = jnp.concatenate(grad_query_blocks, axis=1).reshape(token_count, width)
    grad_kv_ext = jnp.concatenate(grad_kv_blocks, axis=2)
    moved_rims = with_halo(
        rim_rows_of(grad_kv_ext, half_window, own_rows).astype(jnp.bfloat16),
        (("lat", 2),),
        half_window,
    ).astype(jnp.float32)
    joined = fold_rims(grad_kv_ext, moved_rims, half_window, own_rows)
    grad_kv = lax.psum_scatter(
        joined.astype(jnp.bfloat16), "lon", scatter_dimension=3, tiled=True
    ).astype(jnp.float32)
    grad_key_rows = grad_kv[0].reshape(token_count, width)
    grad_value_rows = grad_kv[1].reshape(token_count, width)
    grad_projected = jnp.concatenate(
        [query_back(grad_query_rows)[0], key_back(grad_key_rows)[0], grad_value_rows], axis=1
    ).astype(jnp.bfloat16)
    grad_normed = jnp.einsum("ne,de->nd", grad_projected, w_qkv, preferred_element_type=jnp.float32)
    grad_hidden_part, grad_gain_one = norm_back_one(grad_normed)
    grad_fields = (grad_mixed + grad_hidden_part).astype(jnp.bfloat16).reshape(fields.shape)
    part_qkv = jnp.einsum("nd,ne->de", normed, grad_projected, preferred_element_type=jnp.float32)
    part_out = jnp.einsum("nd,ne->de", attended, grad_mixed_low, preferred_element_type=jnp.float32)
    part_up = jnp.einsum("nd,nf->df", normed_two, grad_pre, preferred_element_type=jnp.float32)
    part_down = jnp.einsum("nf,nd->fd", activated, grad_rows, preferred_element_type=jnp.float32)
    part_gains = jnp.stack([grad_gain_one, grad_gain_two])
    summed = (
        lax.psum_scatter(part_qkv, ("lat", "lon"), scatter_dimension=0, tiled=True),
        lax.psum_scatter(part_out, ("lat", "lon"), scatter_dimension=0, tiled=True),
        lax.psum_scatter(part_up, ("lat", "lon"), scatter_dimension=0, tiled=True),
        lax.psum_scatter(part_down, ("lat", "lon"), scatter_dimension=0, tiled=True),
        lax.psum_scatter(part_gains, ("lat", "lon"), scatter_dimension=1, tiled=True),
    )
    grad_scale = 1.0 / math.sqrt(token_count * lat_devices * lon_devices)
    return (
        layer_out.reshape(fields.shape),
        grad_fields,
        summed[0] * grad_scale,
        summed[1] * grad_scale,
        summed[2] * grad_scale,
        summed[3] * grad_scale,
        summed[4] * grad_scale,
    )


def solution(mesh):
    in_specs = (
        P(None, "lat", "lon", None),
        P("lat", "lon"),
        P(),
        P(),
        P(),
        P(),
        P(),
        P(),
        P(),
        P(None, "lat", "lon", None),
    )
    out_specs = (
        P(None, "lat", "lon", None),
        P(None, "lat", "lon", None),
        P(("lat", "lon"), None),
        P(("lat", "lon"), None),
        P(("lat", "lon"), None),
        P(("lat", "lon"), None),
        P(None, ("lat", "lon")),
    )
    return jax.shard_map(shards, mesh=mesh, in_specs=in_specs, out_specs=out_specs, check_vma=False)
```

profile of v0, /device:TPU:1, one launch (start us, length us, event | category | flops | bytes accessed | tf_op | source)
XLA Modules:
  0.0 1153.4 jit_solution(12139094471652305055)
XLA Ops:
  29.9 44.6 %all-gather.2.cloned.1.call-done = bf16[2,3,4,128,512]{4,3,2,1,0:T(8,128)(2,1)} async-done(((bf16[2,3,4,16,512]{4,3,2,1,0:T(8,128)(2,1)}), bf16[2,3,4,128,512]{4,3,2,1,0:T(8,128)(2,1)}) %all-gather.2.cloned.1.call-update) | async-done | bytes 3145744 | tf_op jit(solution)/shard_map/all_gather | solution.py:115
  74.5 3.9 fusion.36
  78.4 8.1 collective-permute-start
  89.4 3.6 fusion.45
  93.0 28.0 %collective-permute-done = bf16[2,3,2,128,512]{4,3,2,1,0:T(8,128)(2,1)} collective-permute-done((bf16[2,3,2,128,512]{4,3,2,1,0:T(8,128)(2,1)}, bf16[2,3,2,128,512]{4,3,2,1,0:T(8,128)(2,1)}, u32[]{:S(2)}, u32[]{:S(2)}) %collective-permute-start) | collective-permute-done | bytes 1572896 | tf_op jit(solution)/shard_map/ppermute | solution.py:17
  126.9 3.8 copy.68
  130.7 3.8 reshape_squeeze.17
  134.5 3.8 copy.65
  138.3 3.8 reshape_squeeze.16
  144.8 3.9 fusion.35
  148.7 3.8 copy.72
  152.6 3.9 reshape_squeeze.19
  156.4 3.9 copy.71
  160.3 3.8 reshape_squeeze.18
  186.9 4.1 convolution_bitcast_fusion
  199.7 4.9 stack.38
  204.6 4.9 copy.90
  209.5 4.9 stack.39
  214.4 4.9 copy.91
  219.2 3.7 multiply_convert_fusion.1
  222.9 3.9 convolution_bitcast_fusion.3
  226.9 3.2 stack.35
  230.0 3.1 copy.86
  233.1 4.9 stack.36
  238.0 5.0 copy.87
  244.8 6.0 collective-permute-start.2
  253.2 31.8 %collective-permute-done.2 = bf16[2,3,2,128,512]{4,3,2,1,0:T(8,128)(2,1)S(1)} collective-permute-done((bf16[2,3,2,128,512]{4,3,2,1,0:T(8,128)(2,1)S(1)}, bf16[2,3,2,128,512]{4,3,2,1,0:T(8,128)(2,1)S(1)}, u32[]{:S(2)}, u32[]{:S(2)}) %collective-permute-start.2) | collective-permute-done | bytes 1572896 | tf_op jit(solution)/shard_map/ppermute | solution.py:17
  296.6 3.1 convolution_bitcast_fusion.5
  306.5 23.0 %reduce-scatter.4.cloned.1.call-done = bf16[2,3,4,16,512]{4,3,2,1,0:T(8,128)(2,1)} async-done(((bf16[2,3,4,128,512]{4,3,2,1,0:T(8,128)(2,1)}), bf16[2,3,4,16,512]{4,3,2,1,0:T(8,128)(2,1)}) %reduce-scatter.4.cloned.1.call-update) | async-done | bytes 393232 | tf_op jit(solution)/shard_map/reduce_scatter | solution.py:199
  344.6 68.4 %all-reduce.3 = f32[2,512]{1,0:T(2,128)S(1)} all-reduce(f32[2,512]{1,0:T(2,128)S(1)} %pad_maximum_fusion.11), channel_id=7, replica_groups=mesh['lat'=16,'lon'=8] {'lat','lon'}, use_global_device_ids=true, to_apply=%region_23.24.clone | all-reduce | flops 1024 | bytes 8192
  414.5 549.3 %reduce-scatter.6.cloned.1.call-done = f32[16,512]{1,0:T(8,128)} async-done(((f32[2048,512]{1,0:T(8,128)}), f32[16,512]{1,0:T(8,128)}) %reduce-scatter.6.cloned.1.call-update) | async-done | bytes 32784 | tf_op jit(solution)/shard_map/reduce_scatter | solution.py:219
  965.1 177.6 %all-reduce.7.cloned.1.call-done = (f32[512,1536]{1,0:T(8,128)}, f32[512,512]{1,0:T(8,128)}, f32[512,2048]{1,0:T(8,128)}) async-done(((f32[512,1536]{1,0:T(8,128)}, f32[512,512]{1,0:T(8,128)}, f32[512,2048]{1,0:T(8,128)}), (f32[512,1536]{1,0:T(8,128)}, f32[512,512]{1,0:T(8,128)}, f32[512,2048]{1,0:T(8,128)})) %all-reduce.7.cloned.1.call-update) | async-done | bytes 8388624
  (278 shorter events, 109.2 us)
Async XLA Ops:
  7.2 173.0 %copy-start = (bf16[512,2048]{1,0:T(8,128)(2,1)S(1)}, bf16[512,2048]{1,0:T(8,128)(2,1)}, u32[]{:S(2)}) copy-start(bf16[512,2048]{1,0:T(8,128)(2,1)} %param.17) | copy-start | bytes 6291460
  7.2 67.3 %all-gather.2.cloned.1.call-start = ((), (), s32[]{:S(2)}) async-start(), calls=%async_computation.2 | async-start | bytes 3538944 | tf_op jit(solution)/shard_map/all_gather | solution.py:115
  9.6 3.8 copy-start.60
  13.4 13.7 %copy-start.14 = (f32[192,1536]{1,0:T(8,128)}, f32[192,1536]{1,0:T(8,128)S(1)}, u32[]{:S(2)}) copy-start(f32[192,1536]{1,0:T(8,128)S(1)} %fusion.29) | copy-start | bytes 3538948
  18.2 6.0 copy-start.58
  25.0 4.0 copy-start.56
  29.8 58.9 %copy-start.57 = (bf16[192,512]{1,0:T(8,128)(2,1)S(1)}, bf16[192,512]{1,0:T(8,128)(2,1)}, u32[]{:S(2)}) copy-start(bf16[192,512]{1,0:T(8,128)(2,1)} %get-tuple-element.30) | copy-start | bytes 589828
  29.9 299.6 %reduce-scatter.4.cloned.1.call-start = ((), (), s32[]{:S(2)}) async-start(), calls=%async_computation.3 | async-start | bytes 3538944 | tf_op jit(solution)/shard_map/reduce_scatter | solution.py:199
  78.4 11.0 copy-start.29
  78.4 42.7 %collective-permute-start = (bf16[2,3,2,128,512]{4,3,2,1,0:T(8,128)(2,1)}, bf16[2,3,2,128,512]{4,3,2,1,0:T(8,128)(2,1)}, u32[]{:S(2)}, u32[]{:S(2)}) collective-permute-start(bf16[2,3,2,128,512]{4,3,2,1,0:T(8,128)(2,1)} %get-tuple-element.26), channel_id=1, source_target_pairs={{0,8},{8,16},{16,24},{24,32},{32,40},{40,48},{48,56},{56,64},{64,7... | collective-permute-start | bytes 4718600 | tf_op jit(solution)/shard_map/ppermute | solution.py:17
  86.6 55.6 %collective-permute-start.1 = (bf16[2,3,2,128,512]{4,3,2,1,0:T(8,128)(2,1)}, bf16[2,3,2,128,512]{4,3,2,1,0:T(8,128)(2,1)}, u32[]{:S(2)}, u32[]{:S(2)}) collective-permute-start(bf16[2,3,2,128,512]{4,3,2,1,0:T(8,128)(2,1)} %get-tuple-element.27), channel_id=1, source_target_pairs={{8,0},{16,8},{24,16},{32,24},{40,32},{48,40},{56,48},{64,56},{72,6... | collective-permute-start | bytes 4718600 | tf_op jit(solution)/shard_map/ppermute | solution.py:18
  89.4 74.8 %copy-start.44 = (bf16[96,8,64]{0,2,1:T(8,128)(2,1)}, bf16[96,8,64]{0,2,1:T(8,128)(2,1)S(1)}, u32[]{:S(2)}) copy-start(bf16[96,8,64]{0,2,1:T(8,128)(2,1)S(1)} %copy.73) | copy-start | bytes 294916
  93.0 29.6 %copy-start.13 = (bf16[2,3,4,128,512]{4,3,2,1,0:T(8,128)(2,1)S(1)}, bf16[2,3,4,128,512]{4,3,2,1,0:T(8,128)(2,1)}, u32[]{:S(2)}) copy-start(bf16[2,3,4,128,512]{4,3,2,1,0:T(8,128)(2,1)} %all-gather.2.cloned.1.call-done) | copy-start | bytes 9437188
  160.3 3.8 copy-start.72
  171.1 3.5 copy-start.46
  180.1 4.1 copy-start.62
  186.9 4.3 copy-start.49
  186.9 4.3 copy-start.3
  193.5 4.0 copy-start.45
  238.0 5.0 copy-start.4
  243.0 7.8 copy-start.6
  243.0 7.8 copy-start.7
  244.8 40.2 %collective-permute-start.2 = (bf16[2,3,2,128,512]{4,3,2,1,0:T(8,128)(2,1)S(1)}, bf16[2,3,2,128,512]{4,3,2,1,0:T(8,128)(2,1)S(1)}, u32[]{:S(2)}, u32[]{:S(2)}) collective-permute-start(bf16[2,3,2,128,512]{4,3,2,1,0:T(8,128)(2,1)S(1)} %fusion.1), channel_id=1, source_target_pairs={{0,8},{8,16},{16,24},{24,32},{32,40},{40,48},{48,56},{56,64},{64,7... | collective-permute-start | bytes 4718600 | tf_op jit(solution)/shard_map/ppermute | solution.py:17
  250.8 34.1 %copy-start.5 = (f32[1,3,4,128,512]{4,3,2,1,0:T(8,128)S(1)}, f32[1,3,4,128,512]{4,3,2,1,0:T(8,128)}, u32[]{:S(2)}) copy-start(f32[1,3,4,128,512]{4,3,2,1,0:T(8,128)} %copy.91) | copy-start | bytes 9437188
  251.1 33.9 %collective-permute-start.3 = (bf16[2,3,2,128,512]{4,3,2,1,0:T(8,128)(2,1)S(1)}, bf16[2,3,2,128,512]{4,3,2,1,0:T(8,128)(2,1)S(1)}, u32[]{:S(2)}, u32[]{:S(2)}) collective-permute-start(bf16[2,3,2,128,512]{4,3,2,1,0:T(8,128)(2,1)S(1)} %fusion.7), channel_id=1, source_target_pairs={{8,0},{16,8},{24,16},{32,24},{40,32},{48,40},{56,48},{64,56},{72,6... | collective-permute-start | bytes 4718600 | tf_op jit(solution)/shard_map/ppermute | solution.py:18
  288.0 675.7 %reduce-scatter.6.cloned.1.call-start = ((), (), s32[]{:S(2)}) async-start(), calls=%async_computation.4 | async-start | bytes 4227072 | tf_op jit(solution)/shard_map/reduce_scatter | solution.py:219
  292.3 850.4 %all-reduce.7.cloned.1.call-start = ((), (), s32[]{:S(2)}) async-start(), calls=%async_computation.5 | async-start | bytes 16777216
  306.5 25.9 %copy-start.19 = (f32[192,512]{0,1:T(8,128)S(1)}, f32[192,512]{0,1:T(8,128)}, u32[]{:S(2)}) copy-start(f32[192,512]{0,1:T(8,128)} %copy.63) | copy-start | bytes 1179652
  343.4 70.2 %copy-start.31 = (bf16[3,4,16,512]{3,2,1,0:T(8,128)(2,1)S(1)}, bf16[3,4,16,512]{3,2,1,0:T(8,128)(2,1)}, u32[]{:S(2)}) copy-start(bf16[3,4,16,512]{3,2,1,0:T(8,128)(2,1)} %param.19) | copy-start | bytes 589828
  343.4 70.2 %copy-start.69 = (f32[192]{0:T(256)S(1)}, f32[192]{0:T(256)}, u32[]{:S(2)}) copy-start(f32[192]{0:T(256)} %copy-done.68) | copy-start | bytes 2308
  343.4 803.5 %copy-start.1 = (bf16[512,2048]{1,0:T(8,128)(2,1)S(1)}, bf16[512,2048]{1,0:T(8,128)(2,1)}, u32[]{:S(2)}) copy-start(bf16[512,2048]{1,0:T(8,128)(2,1)} %param.17) | copy-start | bytes 6291460
  344.2 69.4 %copy-start.28 = (f32[192,512]{1,0:T(8,128)S(1)}, f32[192,512]{1,0:T(8,128)}, u32[]{:S(2)}) copy-start(f32[192,512]{1,0:T(8,128)} %copy-done.27) | copy-start | bytes 1179652
  (51 other events, 94.2 us)
Sparse Core Ops, SparseCore 0:
  30.0 44.4 all-gather.1
  288.1 41.3 reduce-scatter.3
  331.8 631.8 reduce-scatter.5
  970.0 172.5 all-reduce.6
where the time goes:
time: 1160 us; the launch traced here: 1150 us
  waiting for transfers between devices  854 us (74%)
  local copies, waits for them, and re-layouts  113 us (10%)
  blocking collectives  68.4 us (6%)
  matrix products  56.3 us (5%)
  other arithmetic  27.8 us (2%)
  starting transfers between devices  18.5 us (2%)
  between operations  14.8 us (1%)
    reduce_scatter x1, waiting for transfers between devices, shards(): lax.psum_scatter(part_down, ('lat', 'lon'), scatter_dimension=0, tiled=True)  549 us
    unnamed x5, waiting for transfers between devices  178 us
    unnamed x1, blocking collectives  68.4 us
    ppermute x2, waiting for transfers between devices, with_halo(): before = lax.ppermute(last, axis, up)  59.8 us
    all_gather x1, waiting for transfers between devices, shards(): wide_rows = lax.all_gather(key_value, 'lon', axis=3, tiled=True)  44.6 us
    another operation x8, local copies, waits for them, and re-layouts, shards(): jnp.stack([grad_key, grad_value])  35.5 us
  transfers between devices with their start and end apart: 8, of which 6 were waited for; matrix products, arithmetic and copies ran while one was open for 5% of the time, Pallas kernels for 0%

commit v1 on v0

v1 whole, which is shorter than its diff:
```python
import math

import jax
import jax.numpy as jnp
from jax import lax
from jax.experimental import pallas as pl
from jax.experimental.pallas import tpu as pltpu
from jax.sharding import Mesh
from jax.sharding import PartitionSpec as P

LAT = ("x", "zh", "c")
LON = ("zl", "y")
ALL = LAT + LON
AXIS_SIZES = (4, 2, 2, 2, 4)

HEADS = 8
HEAD = 64
D = 512
FF = 2048
HALF = 96
ROWS = 768
OWN = 2 * HALF
QT = 256

F32 = jnp.float32
BF16 = jnp.bfloat16
NT = (((1,), (1,)), ((), ()))
TN = (((0,), (0,)), ((), ()))


def dot(a, b):
    return jnp.dot(a, b, preferred_element_type=F32)


def dot_nt(a, b):
    return lax.dot_general(a, b, NT, preferred_element_type=F32)


def dot_tn(a, b):
    return lax.dot_general(a, b, TN, preferred_element_type=F32)


def norm_stats(values):
    centred = values - jnp.mean(values, axis=-1, keepdims=True)
    variance = jnp.mean(centred * centred, axis=-1, keepdims=True)
    inverse = lax.rsqrt(variance + 1e-05)
    return centred * inverse, inverse


def norm_back(grad, unit, inverse, gain):
    scaled = grad * gain
    first = jnp.mean(scaled, axis=-1, keepdims=True)
    second = jnp.mean(scaled * unit, axis=-1, keepdims=True)
    return inverse * (scaled - first - unit * second)


def unit_rows(values):
    inverse = lax.rsqrt(jnp.sum(values * values, axis=-1, keepdims=True) + 1e-06)
    return values * inverse, inverse


def unit_back(grad, unit, inverse):
    return inverse * (grad - unit * jnp.sum(grad * unit, axis=-1, keepdims=True))


def pack_head(array, column):
    cols = slice(column, column + HEAD)
    return [array[:HALF, cols], array[HALF:, cols]]


def unpack_heads(ref, lane):
    return jnp.concatenate([ref[h, :, lane : lane + HEAD] for h in range(HEADS)], axis=1)


def project_kernel(low_ref, up_ref, gain_ref, w_ref, normed_ref, packed_ref):
    hidden = jnp.concatenate([low_ref[...], up_ref[...]], axis=0).astype(F32)
    unit, _ = norm_stats(hidden)
    normed = (unit * gain_ref[0:1, :]).astype(BF16)
    normed_ref[0] = normed[:HALF]
    normed_ref[1] = normed[HALF:]
    projected = dot(normed, w_ref[...]).astype(BF16)
    for h in range(HEADS):
        pieces = []
        for part in range(3):
            pieces += pack_head(projected, part * D + h * HEAD)
        packed_ref[h] = jnp.concatenate(pieces, axis=1)


def load_heads(x_ref, offset, half):
    start = offset + half * HEAD
    return x_ref[:, start : start + HEAD]


def lane_ones(count):
    lanes = lax.broadcasted_iota(jnp.int32, (ROWS, HEAD), 1)
    return jnp.where(lanes < count, 1.0, 0.0).astype(BF16)


def attend_kernel(scal_ref, x_ref, att_ref, inv_ref, q_s, k_s, v_s):
    factor = scal_ref[0]
    other = scal_ref[2].astype(BF16)
    for a in range(2):
        rows = slice(a * ROWS, (a + 1) * ROWS)
        q_s[rows] = unit_rows(load_heads(x_ref, 0, a).astype(F32))[0].astype(BF16)
        k_s[rows] = unit_rows(load_heads(x_ref, 128, a).astype(F32))[0].astype(BF16)
        wide = jnp.concatenate([load_heads(x_ref, 256, a), lane_ones(1)], axis=1)
        v_s[a, rows] = wide
        v_s[1 - a, rows] = wide * other
    for t in range(2 * ROWS // QT):
        rows = slice(t * QT, (t + 1) * QT)
        a, inner = divmod(t * QT, ROWS)
        weights = jnp.exp2(dot_nt(q_s[rows], k_s[...]) * factor).astype(BF16)
        total = dot(weights, v_s[a])
        inverse = 1.0 / total[:, HEAD : HEAD + 1]
        inv_ref[rows] = inverse
        att_ref[inner : inner + QT, a * HEAD : (a + 1) * HEAD] = (
            total[:, :HEAD] * inverse
        ).astype(BF16)


def attend_back_kernel(
    scal_ref, x_ref, grad_ref, att_ref, inv_ref, normed_ref, out_ref, gw_ref,
    q_s, k_s, kt_s, v_s, g_s, gv_s, dq_s, dk_s, dv_s,
):
    factor = scal_ref[0]
    scale = scal_ref[1]
    other = scal_ref[2].astype(BF16)
    for a in range(2):
        rows = slice(a * ROWS, (a + 1) * ROWS)
        q_s[rows] = unit_rows(load_heads(x_ref, 0, a).astype(F32))[0].astype(BF16)
        key_unit = unit_rows(load_heads(x_ref, 128, a).astype(F32))[0].astype(BF16)
        k_s[rows] = key_unit
        kt_s[:, rows] = key_unit.astype(F32).T.astype(BF16)
        wide = jnp.concatenate([load_heads(x_ref, 256, a), lane_ones(2)], axis=1)
        v_s[a, rows] = wide
        v_s[1 - a, rows] = wide * other
        grad = load_heads(grad_ref, 0, a).astype(F32)
        inverse = inv_ref[rows]
        delta = jnp.sum(grad * load_heads(att_ref, 0, a).astype(F32), axis=-1, keepdims=True)
        delta = delta * inverse
        delta_high = delta.astype(BF16)
        delta_low = (delta - delta_high.astype(F32)).astype(BF16)
        grad_low = (grad * inverse).astype(BF16)
        lanes = lax.broadcasted_iota(jnp.int32, (ROWS, HEAD), 1)
        tail = jnp.where(
            lanes == 0,
            -delta_high.astype(F32),
            jnp.where(lanes == 1, -delta_low.astype(F32), 0.0),
        ).astype(BF16)
        g_s[rows] = jnp.concatenate([grad_low, tail], axis=1)
        gv_s[0, rows] = grad_low
        gv_s[1, rows] = grad_low * other
    dk_s[...] = jnp.zeros_like(dk_s)
    dv_s[...] = jnp.zeros_like(dv_s)
    for t in range(2 * ROWS // QT):
        rows = slice(t * QT, (t + 1) * QT)
        a = t * QT // ROWS
        query = q_s[rows]
        weights = jnp.exp2(dot_nt(k_s[...], query) * factor)
        grad_weights = dot_nt(v_s[a], g_s[rows])
        grad_scores = (weights * grad_weights).astype(BF16)
        weights = weights.astype(BF16)
        for b in range(2):
            keys = slice(b * ROWS, (b + 1) * ROWS)
            dv_s[keys] += dot(weights[keys], gv_s[abs(a - b), rows])
        dk_s[...] += dot(grad_scores, query)
        dq_s[rows] = dot(kt_s[...], grad_scores).T
    part = None
    for a in range(2):
        rows = slice(a * ROWS, (a + 1) * ROWS)
        unit, inverse = unit_rows(load_heads(x_ref, 0, a).astype(F32))
        dq = unit_back(dq_s[rows] * scale, unit, inverse).astype(BF16)
        unit, inverse = unit_rows(load_heads(x_ref, 128, a).astype(F32))
        dk = unit_back(dk_s[rows] * scale, unit, inverse).astype(BF16)
        dv = dv_s[rows].astype(BF16)
        for place, piece in enumerate((dq, dk, dv)):
            start = place * 128 + a * HEAD
            out_ref[:, start : start + HEAD] = piece
        grads = jnp.concatenate([dq, dk, dv], axis=1)
        normed = jnp.concatenate([normed_ref[i, a] for i in range(8)], axis=0)
        term = dot_tn(normed, grads)
        part = term if part is None else part + term
    gw_ref[...] = part.astype(BF16)


def middle_kernel(
    core_ref, att_ref, low_ref, up_ref, clow_ref, cup_ref, gain_ref, w_out_ref, w_up_ref,
    w_down_ref, out_low_ref, out_up_ref, packed_ref, gm_ref, mine_ref, other_ref,
):
    attended = jnp.concatenate([unpack_heads(att_ref, 0), unpack_heads(att_ref, HEAD)], axis=0)
    hidden = jnp.concatenate([low_ref[...], up_ref[...]], axis=0).astype(F32)
    cot = jnp.concatenate([clow_ref[...], cup_ref[...]], axis=0)
    gain = gain_ref[1:2, :]
    mixed = (hidden + dot(attended, w_out_ref[...])).astype(BF16).astype(F32)
    unit, inverse = norm_stats(mixed)
    normed = (unit * gain).astype(BF16)
    pre = dot(normed, w_up_ref[...])
    root = math.sqrt(2.0 / math.pi)
    square = pre * pre
    bend = jnp.tanh(root * pre * (1.0 + 0.044715 * square))
    half_up = 0.5 * (1.0 + bend)
    activated = (pre * half_up).astype(BF16)
    slope = half_up + 0.5 * pre * (1.0 - bend * bend) * root * (1.0 + 3 * 0.044715 * square)
    layer_out = (mixed + dot(activated, w_down_ref[...])).astype(BF16)
    out_low_ref[...] = layer_out[:HALF]
    out_up_ref[...] = layer_out[HALF:]
    grad_pre = (dot_nt(cot, w_down_ref[...]) * slope).astype(BF16)
    grad_normed = dot_nt(grad_pre, w_up_ref[...])
    grad_mixed = cot.astype(F32) + norm_back(grad_normed, unit, inverse, gain)
    gm_ref[...] = grad_mixed
    grad_low = grad_mixed.astype(BF16)
    grad_attended = dot_nt(grad_low, w_out_ref[...]).astype(BF16)
    for h in range(HEADS):
        packed_ref[h] = jnp.concatenate(pack_head(grad_attended, h * HEAD), axis=1)
    first = core_ref[0] == 0

    def put(product, start, width, step, blocks):
        for g in range(8):
            at = g * 2 * step
            zero = product[at : at + step]
            one = product[at + step : at + 2 * step]
            mine = jnp.where(first, zero, one).astype(BF16)
            other = jnp.where(first, one, zero).astype(BF16)
            for s in range(blocks):
                rows = slice(s * 32, (s + 1) * 32)
                cols = slice(start + s * width, start + (s + 1) * width)
                mine_ref[g, :, cols] = mine[rows]
                other_ref[g, :, cols] = other[rows]

    put(dot_tn(attended, grad_low), 0, D, 32, 1)
    put(dot_tn(normed, grad_pre), D, FF, 32, 1)
    put(dot_tn(activated, cot), D + FF, D, 128, 4)


def input_grad_kernel(packed_ref, low_ref, up_ref, gain_ref, gm_ref, w_ref, glow_ref, gup_ref):
    halves = []
    for a in range(2):
        parts = [unpack_heads(packed_ref, place * 128 + a * HEAD) for place in range(3)]
        halves.append(jnp.concatenate(parts, axis=1))
    grad_projected = jnp.concatenate(halves, axis=0)
    grad_normed = dot_nt(grad_projected, w_ref[...])
    hidden = jnp.concatenate([low_ref[...], up_ref[...]], axis=0).astype(F32)
    unit, inverse = norm_stats(hidden)
    grad = gm_ref[...] + norm_back(grad_normed, unit, inverse, gain_ref[0:1, :])
    grad = grad.astype(BF16)
    glow_ref[...] = grad[:HALF]
    gup_ref[...] = grad[HALF:]


VMEM = pl.BlockSpec(memory_space=pltpu.VMEM)
SMEM = pl.BlockSpec(memory_space=pltpu.SMEM)


def call(kernel, outs, specs, scratch=(), flops=0):
    shapes = tuple(jax.ShapeDtypeStruct(shape, dtype) for shape, dtype in outs)
    return pl.pallas_call(
        kernel,
        out_shape=shapes,
        in_specs=specs,
        out_specs=tuple(VMEM for _ in outs),
        scratch_shapes=list(scratch),
        compiler_params=pltpu.CompilerParams(vmem_limit_bytes=52 * 1024 * 1024),
        cost_estimate=pl.CostEstimate(flops=flops, bytes_accessed=8_000_000, transcendentals=0),
    )


def shards(
    fields, land_sea, surface_embed, norm_gains, w_qkv, head_scales, w_out, w_up, w_down, cotangent
):
    lat = lax.axis_index(LAT)
    lon = lax.axis_index(LON)
    device = lax.axis_index(ALL)
    forward = [(i, (i + 1) % 16) for i in range(16)]
    backward = [(j, i) for i, j in forward]
    chosen = jnp.where(
        land_sea[None, :, :, None] == 1,
        surface_embed[1].astype(F32),
        surface_embed[0].astype(F32),
    )
    hidden = (fields.astype(F32) + chosen).astype(BF16)
    low = lax.ppermute(hidden[:, 2:].reshape(HALF, D), LAT, forward)
    up = hidden[:, :2].reshape(HALF, D)
    cot_low = lax.ppermute(cotangent[:, 2:].reshape(HALF, D), LAT, forward)
    cot_up = cotangent[:, :2].reshape(HALF, D)

    scale = head_scales[lon]
    valid = jnp.where(lat == 0, 0.0, 1.0)
    scal = jnp.stack([scale * math.log2(math.e), scale, valid]).astype(F32)

    normed, packed = call(
        project_kernel,
        [((2, HALF, D), BF16), ((HEADS, HALF, 384), BF16)],
        [VMEM] * 4,
        flops=2 * OWN * D * 3 * D,
    )(low, up, norm_gains, w_qkv)
    normed_all = lax.all_gather(normed, LON, axis=0, tiled=False)
    heads = lax.all_to_all(packed, LON, 0, 0, tiled=True).reshape(ROWS, 384)

    wide = 2 * ROWS
    att, inv = call(
        attend_kernel,
        [((ROWS, 128), BF16), ((wide, 1), F32)],
        [SMEM, VMEM],
        [
            pltpu.VMEM((wide, HEAD), BF16),
            pltpu.VMEM((wide, HEAD), BF16),
            pltpu.VMEM((2, wide, 128), BF16),
        ],
        flops=4 * wide * wide * HEAD,
    )(scal, heads)
    att_rows = lax.all_to_all(att.reshape(HEADS, HALF, 128), LON, 0, 0, tiled=True)

    core = lax.axis_index("c").astype(jnp.int32).reshape(1)
    out_low, out_up, packed_grad, grad_mixed, mine, other = call(
        middle_kernel,
        [
            ((HALF, D), BF16),
            ((HALF, D), BF16),
            ((HEADS, HALF, 128), BF16),
            ((OWN, D), F32),
            ((8, 32, 9 * D), BF16),
            ((8, 32, 9 * D), BF16),
        ],
        [SMEM] + [VMEM] * 9,
        flops=6 * OWN * D * (2 * FF + D),
    )(core, att_rows, low, up, cot_low, cot_up, norm_gains, w_out, w_up, w_down)
    theirs = lax.ppermute(other, "c", [(0, 1), (1, 0)])
    out_back = lax.ppermute(out_low, LAT, backward)
    grad_heads = lax.all_to_all(packed_grad, LON, 0, 0, tiled=True).reshape(ROWS, 128)
    pair = (mine.astype(F32) + theirs.astype(F32)).astype(BF16)
    part = lax.psum_scatter(pair, "x", scatter_dimension=0, tiled=True)

    packed_back, part_qkv = call(
        attend_back_kernel,
        [((ROWS, 384), BF16), ((D, 192), BF16)],
        [SMEM] + [VMEM] * 5,
        [
            pltpu.VMEM((wide, HEAD), BF16),
            pltpu.VMEM((wide, HEAD), BF16),
            pltpu.VMEM((HEAD, wide), BF16),
            pltpu.VMEM((2, wide, 128), BF16),
            pltpu.VMEM((wide, 128), BF16),
            pltpu.VMEM((2, wide, HEAD), BF16),
            pltpu.VMEM((wide, HEAD), F32),
            pltpu.VMEM((wide, HEAD), F32),
            pltpu.VMEM((wide, HEAD), F32),
        ],
        flops=10 * wide * wide * HEAD,
    )(scal, heads, grad_heads, att, inv, normed_all)
    grad_packed = lax.all_to_all(
        packed_back.reshape(HEADS, HALF, 384), LON, 0, 0, tiled=True
    )
    grad_low, grad_up = call(
        input_grad_kernel,
        [((HALF, D), BF16), ((HALF, D), BF16)],
        [VMEM] * 6,
        flops=2 * OWN * D * 3 * D,
    )(grad_packed, low, up, norm_gains, grad_mixed, w_qkv)
    grad_back = lax.ppermute(grad_low, LAT, backward)

    got = lax.all_to_all(part_qkv.reshape(128, 6, 128), ALL, 0, 0, tiled=True)
    got = jnp.sum(got.astype(F32).reshape(16, 8, 6 * 128), axis=0)
    sum_qkv = got.reshape(HEADS, 4, 3, HEAD).transpose(1, 2, 0, 3).reshape(4, 3 * D)
    down_part = part[:, :, 5 * D :].reshape(2, 32, 4, D).transpose(0, 2, 1, 3)
    joined = jnp.concatenate(
        [
            part[:, :, :D].reshape(16, 4 * D),
            part[:, :, D : 5 * D].reshape(16, 4 * FF),
            down_part.reshape(16, 16 * D),
        ],
        axis=1,
    )
    rest = lax.all_to_all(joined.reshape(16, 144, 128), ("zh",) + LON, 0, 0, tiled=True)
    rest = jnp.sum(rest.astype(F32), axis=0).reshape(-1)
    sum_out = rest[: 4 * D].reshape(4, D)
    sum_up = rest[4 * D : 4 * D + 4 * FF].reshape(4, FF)
    sum_down = rest[4 * D + 4 * FF :].reshape(16, D)

    grad_scale = 1.0 / math.sqrt(OWN * 128)
    grad_qkv = sum_qkv * grad_scale
    grad_up_w = sum_up * grad_scale
    rows_qkv = lax.dynamic_slice_in_dim(w_qkv, device * 4, 4, axis=0).astype(F32)
    rows_up = lax.dynamic_slice_in_dim(w_up, device * 4, 4, axis=0).astype(F32)
    gains = lax.dynamic_slice_in_dim(norm_gains, device * 4, 4, axis=1)
    grad_gains = (
        jnp.stack([jnp.sum(rows_qkv * grad_qkv, axis=1), jnp.sum(rows_up * grad_up_w, axis=1)])
        / gains
    )

    def place(own, moved):
        shape = (3, 2, 16, D)
        return jnp.concatenate([own.reshape(shape), moved.reshape(shape)], axis=1)

    return (
        place(out_up, out_back),
        place(grad_up, grad_back),
        grad_qkv,
        sum_out * grad_scale,
        grad_up_w,
        sum_down * grad_scale,
        grad_gains,
    )


def solution(mesh):
    fine = Mesh(mesh.devices.reshape(AXIS_SIZES), ALL)
    grid = P(None, LAT, LON, None)
    in_specs = (grid, P(LAT, LON), P(), P(), P(), P(), P(), P(), P(), grid)
    rows = P(ALL, None)
    out_specs = (grid, grid, rows, rows, rows, rows, P(None, ALL))
    return jax.shard_map(shards, mesh=fine, in_specs=in_specs, out_specs=out_specs, check_vma=False)
```

time: 1160 us -> 182 us (0.16)
  waiting for transfers between devices: 854 us -> 51 us
  local copies, waits for them, and re-layouts: 113 us -> 7.41 us
  matrix products: 56.3 us -> 0 us
  blocking collectives: 68.4 us -> 12.9 us
  Pallas kernels: 0 us -> 37.2 us
  starting transfers between devices: 18.5 us -> 44.8 us
  other arithmetic: 27.8 us -> 11.7 us
    reduce_scatter x2 -> x1, waiting for transfers between devices: 572 us -> 0.03 us  [shards(): part = lax.psum_scatter(pair, 'x', scatter_dimension=0, tiled=True)]
    unnamed x5 -> x2, waiting for transfers between devices: 178 us -> 0.03 us
    unnamed x1 -> x0, blocking collectives: 68.4 us -> none
    dot_general x24 -> x0, matrix products: 56.3 us -> none  [the longest x2 6.32 us: attend_back(): jnp.einsum('qhe,khe->hqk', grad_block, value_block, preferred_element_typ...]
    another operation x16 -> x0, local copies, waits for them, and re-layouts: 51.9 us -> none  [the longest x8 35.5 us: shards(): jnp.stack([grad_key, grad_value])]
    ppermute x4 -> x5, waiting for transfers between devices: 59.9 us -> 14.3 us  [the longest x1 6.61 us: shards(): grad_back = lax.ppermute(grad_low, LAT, backward)]
    pallas_call x0 -> x5, Pallas kernels: none -> 37.2 us  [the longest x1 17.6 us: shards(): call(attend_back_kernel, [((ROWS, 384), BF16), ((D, 192), BF16)], [SMEM]...]
    all_gather x1, waiting for transfers between devices: 44.6 us -> 12.2 us  [shards(): normed_all = lax.all_gather(normed, LON, axis=0, tiled=False)]
  transfers between devices with their start and end apart: 8 -> 12, of which waited for: 6 -> 8; matrix products, arithmetic and copies ran while one was open for 5% -> 7% of each run, Pallas kernels for 0% -> 11%
where the time goes in v1:
time: 182 us; the launch traced here: 181 us
  waiting for transfers between devices  51 us (28%)
  starting transfers between devices  44.8 us (25%)
  Pallas kernels  37.2 us (20%)
  between operations  16.4 us (9%)
  blocking collectives  12.9 us (7%)
  other arithmetic  11.7 us (6%)
  local copies, waits for them, and re-layouts  7.41 us (4%)
    pallas_call x1, Pallas kernels, shards(): call(attend_back_kernel, [((ROWS, 384), BF16), ((D, 192), BF16)], [SMEM]...  17.6 us
    all_to_all x1, blocking collectives, shards(): lax.all_to_all(packed_grad, LON, 0, 0, tiled=True).reshape(ROWS, 128)  12.9 us
    all_gather x1, waiting for transfers between devices, shards(): normed_all = lax.all_gather(normed, LON, axis=0, tiled=False)  12.2 us
    all_to_all x1, starting transfers between devices, shards(): got = lax.all_to_all(part_qkv.reshape(128, 6, 128), ALL, 0, 0, tiled=True)  11.5 us
    all_to_all x1, waiting for transfers between devices, shards(): got = lax.all_to_all(part_qkv.reshape(128, 6, 128), ALL, 0, 0, tiled=True)  10.1 us
    pallas_call x1, Pallas kernels, shards(): call(middle_kernel, [((HALF, D), BF16), ((HALF, D), BF16), ((HEADS, HALF,...  9.1 us
    all_to_all x1, waiting for transfers between devices, shards(): lax.all_to_all(packed_back.reshape(HEADS, HALF, 384), LON, 0, 0, tiled=True)  8.3 us
    ppermute x1, waiting for transfers between devices, shards(): grad_back = lax.ppermute(grad_low, LAT, backward)  6.61 us
  transfers between devices with their start and end apart: 12, of which 8 were waited for; matrix products, arithmetic and copies ran while one was open for 7% of the time, Pallas kernels for 11%

profile of v1, /device:TPU:1, one launch (start us, length us, event | category | flops | bytes accessed | tf_op | source)
XLA Modules:
  0.0 181.4 jit_solution(7030549406485718533)
XLA Ops:
  9.5 1.0 add_convert_fusion.1
  10.5 5.1 %collective-permute-start = (bf16[96,512]{1,0:T(8,128)(2,1)S(1)}, bf16[96,512]{1,0:T(8,128)(2,1)S(1)}, u32[]{:S(2)}, u32[]{:S(2)}) collective-permute-start(bf16[96,512]{1,0:T(8,128)(2,1)S(1)} %bitcast.48), channel_id=1, source_target_pairs={{0,8},{8,16},{16,24},{24,32},{32,40},{40,48},{48,56},{56,64},{64,7... | collective-permute-start | bytes 294920 | tf_op jit(solution)/shard_map/ppermute | solution.py:281
  15.6 1.6 collective-permute-done.low_ref
  17.9 3.0 %shard_map.153 = (bf16[2,96,512]{2,1,0:T(8,128)(2,1)}, bf16[8,96,384]{2,1,0:T(8,128)(2,1)}) custom-call(bf16[96,512]{1,0:T(8,128)(2,1)S(1)} %collective-permute-done.low_ref, bf16[96,512]{1,0:T(8,128)(2,1)S(1)} %bitcast.34, f32[2,512]{1,0:T(2,128)S(1)} %copy-done, bf16[512,1536]{1,0:T(8,128)(2,1)} %w_ref.3), custom_call_target="tpu_custom_call" | custom-call | flops 301989888 | bytes 8000000 | tf_op jit(solution)/shard_map/pallas_call | solution.py:290
  20.9 4.8 %all-to-all-start = ((bf16[8,96,384]{2,1,0:T(8,128)(2,1)}), bf16[8,96,384]{2,1,0:T(8,128)(2,1)S(1)}, u32[]{:S(2)}, u32[]{:S(2)}) async-start(bf16[8,96,384]{2,1,0:T(8,128)(2,1)} %get-tuple-element.21), calls=%async_computation | async-start | bytes 1179648 | tf_op jit(solution)/shard_map/all_to_all | solution.py:297
  27.7 6.0 %all-to-all-done = bf16[8,96,384]{2,1,0:T(8,128)(2,1)S(1)} async-done(((bf16[8,96,384]{2,1,0:T(8,128)(2,1)}), bf16[8,96,384]{2,1,0:T(8,128)(2,1)S(1)}, u32[]{:S(2)}, u32[]{:S(2)}) %all-to-all-start) | async-done | bytes 589856 | tf_op jit(solution)/shard_map/all_to_all | solution.py:297
  33.7 5.3 %shard_map.154 = (bf16[768,128]{1,0:T(8,128)(2,1)}, f32[1536,1]{1,0:T(8,128)S(1)}) custom-call(f32[3]{0:T(128)S(1)} %pad_maximum_fusion.2.scal_ref, bf16[768,384]{1,0:T(8,128)(2,1)S(1)} %bitcast.37), custom_call_target="tpu_custom_call" | custom-call | flops 603979776 | bytes 8000000 | tf_op jit(solution)/shard_map/pallas_call | solution.py:300
  39.0 0.9 copy-done.3
  39.9 3.4 %all-to-all-start.1 = ((bf16[8,96,128]{2,1,0:T(8,128)(2,1)}), bf16[8,96,128]{2,1,0:T(8,128)(2,1)S(1)}, u32[]{:S(2)}, u32[]{:S(2)}) async-start(bf16[8,96,128]{2,1,0:T(8,128)(2,1)} %bitcast.7), calls=%async_computation.1 | async-start | bytes 393216 | tf_op jit(solution)/shard_map/all_to_all | solution.py:311
  43.4 5.9 %collective-permute-start.1 = (bf16[96,512]{1,0:T(8,128)(2,1)S(1)}, bf16[96,512]{1,0:T(8,128)(2,1)S(1)}, u32[]{:S(2)}, u32[]{:S(2)}) collective-permute-start(bf16[96,512]{1,0:T(8,128)(2,1)S(1)} %bitcast.49), channel_id=1, source_target_pairs={{0,8},{8,16},{16,24},{24,32},{32,40},{40,48},{48,56},{56,64},{64,7... | collective-permute-start | bytes 294920 | tf_op jit(solution)/shard_map/ppermute | solution.py:283
  49.3 1.6 collective-permute-done.1.clow_ref
  50.9 9.1 %shard_map.155 = (bf16[96,512]{1,0:T(8,128)(2,1)S(1)}, bf16[96,512]{1,0:T(8,128)(2,1)S(1)}, bf16[8,96,128]{2,1,0:T(8,128)(2,1)S(1)}, f32[192,512]{1,0:T(8,128)S(...) custom-call(s32[1]{0:T(128)} %bitcast.core_ref, bf16[8,96,128]{2,1,0:T(8,128)(2,1)S(1)} %all-to-all-done.1.att_ref, ...), custom_call_target="tpu_custom_call" | custom-call | flops 2717908992 | bytes 8000000 | tf_op jit(solution)/shard_map/pallas_call | solution.py:314
  60.0 5.0 %collective-permute-start.4 = (bf16[8,32,4608]{2,1,0:T(8,128)(2,1)}, bf16[8,32,4608]{2,1,0:T(8,128)(2,1)}, u32[]{:S(2)}, u32[]{:S(2)}) collective-permute-start(bf16[8,32,4608]{2,1,0:T(8,128)(2,1)} %get-tuple-element.34), channel_id=1, source_target_pairs={{0,8},{8,0},{1,9},{9,1},{2,10},{10,2},{3,11},{11,3},{4,12},{12,4},... | collective-permute-start | bytes 7077896 | tf_op jit(solution)/shard_map/ppermute | solution.py:327
  65.1 4.4 %collective-permute-done.4 = bf16[8,32,4608]{2,1,0:T(8,128)(2,1)} collective-permute-done((bf16[8,32,4608]{2,1,0:T(8,128)(2,1)}, bf16[8,32,4608]{2,1,0:T(8,128)(2,1)}, u32[]{:S(2)}, u32[]{:S(2)}) %collective-permute-start.4) | collective-permute-done | bytes 2359328 | tf_op jit(solution)/shard_map/ppermute | solution.py:327
  69.6 4.5 %add_convert_fusion = bf16[8,32,4608]{2,1,0:T(8,128)(2,1)} fusion(bf16[8,32,4608]{2,1,0:T(8,128)(2,1)} %collective-permute-done.4, bf16[8,32,4608]{2,1,0:T(8,128)(2,1)} %get-tuple-element.33), kind=kLoop, calls=%fused_computation | loop fusion | flops 4718592 | bytes 7077888 | tf_op jit(solution)/shard_map/convert_element_type | solution.py:330
  74.1 12.9 %all_to_all.30 = bf16[8,96,128]{2,1,0:T(8,128)(2,1)S(1)} all-to-all(bf16[8,96,128]{2,1,0:T(8,128)(2,1)S(1)} %get-tuple-element.25), channel_id=1, replica_groups=mesh['x'=4,'zh'=2,'c'=2,'zl'=2,'y'=4] {'zl','y'}, dimensions={0} | all-to-all | bytes 393216 | tf_op jit(solution)/shard_map/all_to_all | solution.py:329
  86.9 12.2 %all-gather.3.cloned.1.call-done = bf16[16,96,512]{2,1,0:T(8,128)(2,1)} async-done(((bf16[2,96,512]{2,1,0:T(8,128)(2,1)}), bf16[16,96,512]{2,1,0:T(8,128)(2,1)}) %all-gather.3.cloned.1.call-update) | async-done | bytes 1572880 | tf_op jit(solution)/shard_map/all_gather | solution.py:296
  99.2 17.6 %shard_map.156 = (bf16[768,384]{1,0:T(8,128)(2,1)}, bf16[512,192]{1,0:T(8,128)(2,1)S(1)}) custom-call(f32[3]{0:T(128)S(1)} %pad_maximum_fusion.2.scal_ref, bf16[768,384]{1,0:T(8,128)(2,1)S(1)} %bitcast.38, bf16[768,128]{1,0:T(8,128)(2,1)S(1)} %bitcast.39, bf16[768,128]{1,0:T(8,128)(2,1)} %get-tuple-element.22.att_ref, f32[1536,1]{1,0:T(8,128)} %copy-done.3, ...), custom_call_target="tpu_custom_call" | custom-call | flops 1509949440 | bytes 8000000 | tf_op jit(solution)/shard_map/pallas_call | solution.py:333
  116.7 1.0 reshape.125
  117.8 11.5 %all-to-all-start.4 = ((bf16[128,6,128]{2,1,0:T(8,128)(2,1)}), bf16[128,6,128]{2,1,0:T(8,128)(2,1)S(1)}, u32[]{:S(2)}, u32[]{:S(2)}) async-start(bf16[128,6,128]{2,1,0:T(8,128)(2,1)} %reshape.125), calls=%async_computation.4 | async-start | bytes 524288 | tf_op jit(solution)/shard_map/all_to_all | solution.py:361
  129.3 1.1 collective-permute-start.2
  130.4 10.1 %all-to-all-done.4 = bf16[128,6,128]{2,1,0:T(8,128)(2,1)S(1)} async-done(((bf16[128,6,128]{2,1,0:T(8,128)(2,1)}), bf16[128,6,128]{2,1,0:T(8,128)(2,1)S(1)}, u32[]{:S(2)}, u32[]{:S(2)}) %all-to-all-start.4) | async-done | bytes 196640 | tf_op jit(solution)/shard_map/all_to_all | solution.py:361
  140.5 3.5 %all-to-all-start.3 = ((bf16[8,96,384]{2,1,0:T(8,128)(2,1)}), bf16[8,96,384]{2,1,0:T(8,128)(2,1)S(1)}, u32[]{:S(2)}, u32[]{:S(2)}) async-start(bf16[8,96,384]{2,1,0:T(8,128)(2,1)} %bitcast.14), calls=%async_computation.3 | async-start | bytes 1179648 | tf_op jit(solution)/shard_map/all_to_all | solution.py:350
  144.1 1.1 fusion
  145.7 0.9 copy.23
  146.6 8.3 %all-to-all-done.3.packed_ref = bf16[8,96,384]{2,1,0:T(8,128)(2,1)S(1)} async-done(((bf16[8,96,384]{2,1,0:T(8,128)(2,1)}), bf16[8,96,384]{2,1,0:T(8,128)(2,1)S(1)}, u32[]{:S(2)}, u32[]{:S(2)}) %all-to-all-start.3) | async-done | bytes 589856 | tf_op jit(solution)/shard_map/all_to_all | solution.py:350
  154.9 3.6 %all-to-all-start.5 = ((bf16[16,144,128]{2,1,0:T(8,128)(2,1)}), bf16[16,144,128]{2,1,0:T(8,128)(2,1)S(1)}, u32[]{:S(2)}, u32[]{:S(2)}) async-start(bf16[16,144,128]{2,1,0:T(8,128)(2,1)} %bitcast.26), calls=%async_computation.6 | async-start | bytes 1179648 | tf_op jit(solution)/shard_map/all_to_all | solution.py:373
  159.7 2.2 %shard_map.157 = (bf16[96,512]{1,0:T(8,128)(2,1)S(1)}, bf16[96,512]{1,0:T(8,128)(2,1)S(1)}) custom-call(bf16[8,96,384]{2,1,0:T(8,128)(2,1)S(1)} %all-to-all-done.3.packed_ref, bf16[96,512]{1,0:T(8,128)(2,1)S(1)} %collective-permute-done.low_ref, bf16[96,512]{1,0:T(8,128)(2,1)S(1)} %bitcast.36, f32[2,512]{1,0:T(2,128)S(1)} %copy-done.1, ...), custom_call_target="tpu_custom_call" | custom-call | flops 301989888 | bytes 8000000 | tf_op jit(solution)/shard_map/pallas_call | solution.py:353
  162.0 0.9 collective-permute-start.3
  162.9 0.9 multiply_reduce_fusion.1
  163.7 6.6 %collective-permute-done.3 = bf16[96,512]{1,0:T(8,128)(2,1)S(1)} collective-permute-done((bf16[96,512]{1,0:T(8,128)(2,1)S(1)}, bf16[96,512]{1,0:T(8,128)(2,1)S(1)}, u32[]{:S(2)}, u32[]{:S(2)}) %collective-permute-start.3) | collective-permute-done | bytes 98336 | tf_op jit(solution)/shard_map/ppermute | solution.py:359
  172.4 0.9 multiply_reduce_fusion
  (52 shorter events, 8.0 us)
Async XLA Ops:
  8.0 17.7 %copy-start.7 = (f32[8]{0:T(128)S(1)}, f32[8]{0:T(128)}, u32[]{:S(2)}) copy-start(f32[8]{0:T(128)} %param.15) | copy-start | bytes 100
  10.5 6.7 %collective-permute-start = (bf16[96,512]{1,0:T(8,128)(2,1)S(1)}, bf16[96,512]{1,0:T(8,128)(2,1)S(1)}, u32[]{:S(2)}, u32[]{:S(2)}) collective-permute-start(bf16[96,512]{1,0:T(8,128)(2,1)S(1)} %bitcast.48), channel_id=1, source_target_pairs={{0,8},{8,16},{16,24},{24,32},{32,40},{40,48},{48,56},{56,64},{64,7... | collective-permute-start | bytes 294920 | tf_op jit(solution)/shard_map/ppermute | solution.py:281
  17.2 0.7 copy-start
  20.9 22.4 %copy-start.4 = (bf16[3,4,16,512]{3,2,1,0:T(8,128)(2,1)S(1)}, bf16[3,4,16,512]{3,2,1,0:T(8,128)(2,1)}, u32[]{:S(2)}) copy-start(bf16[3,4,16,512]{3,2,1,0:T(8,128)(2,1)} %param.19) | copy-start | bytes 589828
  20.9 30.0 %copy-start.1 = (f32[2,512]{1,0:T(2,128)S(1)}, f32[2,512]{1,0:T(2,128)}, u32[]{:S(2)}) copy-start(f32[2,512]{1,0:T(2,128)} %gain_ref.5) | copy-start | bytes 12292
  20.9 30.0 %copy-start.2 = (bf16[512,512]{1,0:T(8,128)(2,1)S(1)}, bf16[512,512]{1,0:T(8,128)(2,1)}, u32[]{:S(2)}) copy-start(bf16[512,512]{1,0:T(8,128)(2,1)} %w_out_ref.1) | copy-start | bytes 1572868
  20.9 12.8 %all-to-all-start = ((bf16[8,96,384]{2,1,0:T(8,128)(2,1)}), bf16[8,96,384]{2,1,0:T(8,128)(2,1)S(1)}, u32[]{:S(2)}, u32[]{:S(2)}) async-start(bf16[8,96,384]{2,1,0:T(8,128)(2,1)} %get-tuple-element.21), calls=%async_computation | async-start | bytes 1179648 | tf_op jit(solution)/shard_map/all_to_all | solution.py:297
  39.0 0.9 copy-start.3
  39.9 11.0 %all-to-all-start.1 = ((bf16[8,96,128]{2,1,0:T(8,128)(2,1)}), bf16[8,96,128]{2,1,0:T(8,128)(2,1)S(1)}, u32[]{:S(2)}, u32[]{:S(2)}) async-start(bf16[8,96,128]{2,1,0:T(8,128)(2,1)} %bitcast.7), calls=%async_computation.1 | async-start | bytes 393216 | tf_op jit(solution)/shard_map/all_to_all | solution.py:311
  43.3 55.9 %all-gather.3.cloned.1.call-start = ((), (), s32[]{:S(2)}) async-start(), calls=%async_computation.8 | async-start | bytes 1769472 | tf_op jit(solution)/shard_map/all_gather | solution.py:296
  43.4 7.5 %collective-permute-start.1 = (bf16[96,512]{1,0:T(8,128)(2,1)S(1)}, bf16[96,512]{1,0:T(8,128)(2,1)S(1)}, u32[]{:S(2)}, u32[]{:S(2)}) collective-permute-start(bf16[96,512]{1,0:T(8,128)(2,1)S(1)} %bitcast.49), channel_id=1, source_target_pairs={{0,8},{8,16},{16,24},{24,32},{32,40},{40,48},{48,56},{56,64},{64,7... | collective-permute-start | bytes 294920 | tf_op jit(solution)/shard_map/ppermute | solution.py:283
  60.0 9.5 %collective-permute-start.4 = (bf16[8,32,4608]{2,1,0:T(8,128)(2,1)}, bf16[8,32,4608]{2,1,0:T(8,128)(2,1)}, u32[]{:S(2)}, u32[]{:S(2)}) collective-permute-start(bf16[8,32,4608]{2,1,0:T(8,128)(2,1)} %get-tuple-element.34), channel_id=1, source_target_pairs={{0,8},{8,0},{1,9},{9,1},{2,10},{10,2},{3,11},{11,3},{4,12},{12,4},... | collective-permute-start | bytes 7077896 | tf_op jit(solution)/shard_map/ppermute | solution.py:327
  65.1 79.0 %reduce-scatter.2.cloned.1.call-start = ((), (), s32[]{:S(2)}) async-start(), calls=%async_computation.7 | async-start | bytes 2949120 | tf_op jit(solution)/shard_map/reduce_scatter | solution.py:331
  117.8 22.7 %all-to-all-start.4 = ((bf16[128,6,128]{2,1,0:T(8,128)(2,1)}), bf16[128,6,128]{2,1,0:T(8,128)(2,1)S(1)}, u32[]{:S(2)}, u32[]{:S(2)}) async-start(bf16[128,6,128]{2,1,0:T(8,128)(2,1)} %reshape.125), calls=%async_computation.4 | async-start | bytes 524288 | tf_op jit(solution)/shard_map/all_to_all | solution.py:361
  129.3 29.3 %collective-permute-start.2 = (bf16[96,512]{1,0:T(8,128)(2,1)S(1)}, bf16[96,512]{1,0:T(8,128)(2,1)S(1)}, u32[]{:S(2)}, u32[]{:S(2)}) collective-permute-start(bf16[96,512]{1,0:T(8,128)(2,1)S(1)} %get-tuple-element.24), channel_id=1, source_target_pairs={{8,0},{16,8},{24,16},{32,24},{40,32},{48,40},{56,48},{64,56},{72,6... | collective-permute-start | bytes 294920 | tf_op jit(solution)/shard_map/ppermute | solution.py:328
  140.5 14.4 %all-to-all-start.3 = ((bf16[8,96,384]{2,1,0:T(8,128)(2,1)}), bf16[8,96,384]{2,1,0:T(8,128)(2,1)S(1)}, u32[]{:S(2)}, u32[]{:S(2)}) async-start(bf16[8,96,384]{2,1,0:T(8,128)(2,1)} %bitcast.14), calls=%async_computation.3 | async-start | bytes 1179648 | tf_op jit(solution)/shard_map/all_to_all | solution.py:350
  144.1 1.5 slice-start
  154.9 16.1 %all-to-all-start.5 = ((bf16[16,144,128]{2,1,0:T(8,128)(2,1)}), bf16[16,144,128]{2,1,0:T(8,128)(2,1)S(1)}, u32[]{:S(2)}, u32[]{:S(2)}) async-start(bf16[16,144,128]{2,1,0:T(8,128)(2,1)} %bitcast.26), calls=%async_computation.6 | async-start | bytes 1179648 | tf_op jit(solution)/shard_map/all_to_all | solution.py:373
  159.7 13.6 %copy-start.6 = (f32[4,1536]{1,0:T(4,128)}, f32[4,1536]{1,0:T(4,128)S(1)}, u32[]{:S(2)}) copy-start(f32[4,1536]{1,0:T(4,128)S(1)} %mul.82) | copy-start | bytes 73732
  162.0 8.4 %collective-permute-start.3 = (bf16[96,512]{1,0:T(8,128)(2,1)S(1)}, bf16[96,512]{1,0:T(8,128)(2,1)S(1)}, u32[]{:S(2)}, u32[]{:S(2)}) collective-permute-start(bf16[96,512]{1,0:T(8,128)(2,1)S(1)} %get-tuple-element.31), channel_id=1, source_target_pairs={{8,0},{16,8},{24,16},{32,24},{40,32},{48,40},{56,48},{64,56},{72,6... | collective-permute-start | bytes 294920 | tf_op jit(solution)/shard_map/ppermute | solution.py:359
  172.4 1.6 copy-start.5
Sparse Core Ops, SparseCore 0:
  65.2 33.9 all-gather.2
Sparse Core Ops, SparseCore 1:
  74.1 29.1 reduce-scatter.1

commit v2 on v1

v2 whole, which is shorter than its diff:
```python
import math

import jax
import jax.numpy as jnp
from jax import lax
from jax.experimental import pallas as pl
from jax.experimental.pallas import tpu as pltpu
from jax.sharding import Mesh
from jax.sharding import PartitionSpec as P

LAT = ("x", "zh", "c")
LON = ("zl", "y")
ALL = LAT + LON
AXIS_SIZES = (4, 2, 2, 2, 4)

HEADS = 8
HEAD = 64
D = 512
FF = 2048
HALF = 96
ROWS = 768
OWN = 2 * HALF
QT = 256

F32 = jnp.float32
BF16 = jnp.bfloat16
NT = (((1,), (1,)), ((), ()))
TN = (((0,), (0,)), ((), ()))


def dot(a, b):
    return jnp.dot(a, b, preferred_element_type=F32)


def dot_nt(a, b):
    return lax.dot_general(a, b, NT, preferred_element_type=F32)


def dot_tn(a, b):
    return lax.dot_general(a, b, TN, preferred_element_type=F32)


def norm_stats(values):
    centred = values - jnp.mean(values, axis=-1, keepdims=True)
    variance = jnp.mean(centred * centred, axis=-1, keepdims=True)
    inverse = lax.rsqrt(variance + 1e-05)
    return centred * inverse, inverse


def norm_back(grad, unit, inverse, gain):
    scaled = grad * gain
    first = jnp.mean(scaled, axis=-1, keepdims=True)
    second = jnp.mean(scaled * unit, axis=-1, keepdims=True)
    return inverse * (scaled - first - unit * second)


def swap(pair):
    return pltpu.roll(pair, HEAD, axis=1)


def is_left(rows):
    return lax.broadcasted_iota(jnp.int32, (rows, 2 * HEAD), 1) < HEAD


def pair_sum(values):
    row = lax.broadcasted_iota(jnp.int32, (4 * HEAD, 2 * HEAD), 0) >> 6
    column = lax.broadcasted_iota(jnp.int32, (4 * HEAD, 2 * HEAD), 1) >> 6
    ones = jnp.where((row & 1) == column, 1.0, 0.0).astype(BF16)
    high = values.astype(BF16)
    low = (values - high.astype(F32)).astype(BF16)
    return dot(jnp.concatenate([high, low], axis=1), ones)


def unit_pair(x_ref, offset):
    values = x_ref[:, offset : offset + 2 * HEAD].astype(F32)
    inverse = lax.rsqrt(pair_sum(values * values) + 1e-06)
    return values * inverse, inverse


def unit_back(grad, unit, inverse):
    return inverse * (grad - unit * pair_sum(grad * unit))


def spread(pair):
    swapped = swap(pair)
    left = is_left(ROWS)
    return jnp.where(left, pair, swapped), jnp.where(left, swapped, pair)


def put_spread(ref, pair):
    zero, one = spread(pair)
    ref[:ROWS] = zero.astype(BF16)
    ref[ROWS:] = one.astype(BF16)


def pack_head(array, column):
    cols = slice(column, column + HEAD)
    return [array[:HALF, cols], array[HALF:, cols]]


def unpack_heads(ref, lane):
    return jnp.concatenate([ref[h, :, lane : lane + HEAD] for h in range(HEADS)], axis=1)


def project_kernel(low_ref, up_ref, gain_ref, w_ref, normed_ref, packed_ref):
    hidden = jnp.concatenate([low_ref[:HALF], up_ref[...]], axis=0).astype(F32)
    unit, _ = norm_stats(hidden)
    normed = (unit * gain_ref[0:1, :]).astype(BF16)
    normed_ref[0] = normed[:HALF]
    normed_ref[1] = normed[HALF:]
    projected = dot(normed, w_ref[...]).astype(BF16)
    for h in range(HEADS):
        pieces = []
        for part in range(3):
            pieces += pack_head(projected, part * D + h * HEAD)
        packed_ref[h] = jnp.concatenate(pieces, axis=1)


def value_rows(x_ref):
    values = x_ref[:, 4 * HEAD :].astype(F32)
    swapped = swap(values)
    left = is_left(ROWS)
    return [
        [jnp.where(left, values, 1.0), jnp.where(left, swapped, 1.0)],
        [jnp.where(left, 1.0, swapped), jnp.where(left, 1.0, values)],
    ]


def attend_kernel(scal_ref, x_ref, att_ref, inv_ref, q_s, k_s, v_s):
    factor = scal_ref[0]
    other = scal_ref[2]
    put_spread(q_s, unit_pair(x_ref, 0)[0])
    put_spread(k_s, unit_pair(x_ref, 2 * HEAD)[0])
    values = value_rows(x_ref)
    for a in range(2):
        for b in range(2):
            block = values[a][b] if a == b else values[a][b] * other
            v_s[a, b * ROWS : (b + 1) * ROWS] = block.astype(BF16)
    left = is_left(QT)
    for t in range(ROWS // QT):
        totals = []
        for a in range(2):
            start = a * ROWS + t * QT
            scores = dot_nt(q_s[start : start + QT], k_s[...])
            totals.append(dot(jnp.exp2(scores * factor).astype(BF16), v_s[a]))
        inverse = 1.0 / swap(jnp.where(left, totals[1], totals[0]))
        rows = slice(t * QT, (t + 1) * QT)
        inv_ref[rows] = inverse
        att_ref[rows] = (jnp.where(left, totals[0], totals[1]) * inverse).astype(BF16)


def attend_back_kernel(
    scal_ref, core_ref, x_ref, grad_ref, att_ref, inv_ref, normed_ref, out_ref, mine_ref,
    other_ref, q_s, k_s, v_s, g_s, gd_s,
):
    factor = scal_ref[0]
    scale = scal_ref[1]
    other = scal_ref[2]
    left = is_left(ROWS)
    query_unit, query_inverse = unit_pair(x_ref, 0)
    key_unit, key_inverse = unit_pair(x_ref, 2 * HEAD)
    put_spread(q_s, query_unit)
    key_wide = spread(key_unit)
    k_s[:ROWS] = key_wide[0].astype(BF16)
    k_s[ROWS:] = key_wide[1].astype(BF16)
    values = value_rows(x_ref)
    for a in range(2):
        for b in range(2):
            v_s[a, b * ROWS : (b + 1) * ROWS] = values[a][b].astype(BF16)
    grad = grad_ref[...].astype(F32)
    inverse = inv_ref[...]
    delta = swap(pair_sum(grad * att_ref[...].astype(F32)) * inverse)
    high = delta.astype(BF16).astype(F32)
    grad = grad * inverse
    lanes = lax.broadcasted_iota(jnp.int32, (ROWS, 2 * HEAD), 1) & (HEAD - 1)
    tail = jnp.where(lanes == 0, -high, jnp.where(lanes == 1, high - delta, 0.0))
    grad_rows = [jnp.where(left, grad, tail), jnp.where(left, tail, grad)]
    grad_wide = spread(grad)
    for a in range(2):
        rows = slice(a * ROWS, (a + 1) * ROWS)
        for b in range(2):
            mask = 1.0 if a == b else other
            g_s[b, rows] = (grad_rows[a] * mask).astype(BF16)
            gd_s[b, rows] = (grad_wide[a] * mask).astype(BF16)
    dq = [None, None]
    dk = [None, None]
    dv = [None, None]

    def add(sums, place, term):
        sums[place] = term if sums[place] is None else sums[place] + term

    for b in range(2):
        keys = slice(b * ROWS, (b + 1) * ROWS)
        key = k_s[keys]
        key_flat = key_wide[b].T.astype(BF16)
        for a in range(2):
            rows = slice(a * ROWS, (a + 1) * ROWS)
            query = q_s[rows]
            weights = jnp.exp2(dot_nt(key, query) * factor)
            grad_weights = dot_nt(v_s[a, keys], g_s[b, rows])
            grad_scores = (weights * grad_weights).astype(BF16)
            add(dv, b, dot(weights.astype(BF16), gd_s[b, rows]))
            add(dk, b, dot(grad_scores, query))
            add(dq, a, dot(key_flat, grad_scores))
    dq_pair = jnp.where(left, dq[0].T, dq[1].T) * scale
    dk_pair = jnp.where(left, dk[0], dk[1]) * scale
    out_ref[:, : 2 * HEAD] = unit_back(dq_pair, query_unit, query_inverse).astype(BF16)
    out_ref[:, 2 * HEAD : 4 * HEAD] = unit_back(dk_pair, key_unit, key_inverse).astype(BF16)
    out_ref[:, 4 * HEAD :] = jnp.where(left, dv[0], dv[1]).astype(BF16)
    product = None
    for a in range(2):
        pieces = []
        for part in range(3):
            start = part * 2 * HEAD + a * HEAD
            pieces.append(out_ref[:, start : start + HEAD])
        normed = jnp.concatenate([normed_ref[i, a] for i in range(8)], axis=0)
        term = dot_tn(normed, jnp.concatenate(pieces, axis=1))
        product = term if product is None else product + term
    first = core_ref[0] == 0
    for g in range(8):
        zero = product[g * 64 : g * 64 + 32]
        one = product[g * 64 + 32 : g * 64 + 64]
        mine_ref[g] = jnp.where(first, zero, one).astype(BF16)
        other_ref[g] = jnp.where(first, one, zero).astype(BF16)


def pair_kernel(x_ref, mine_ref, theirs_ref, zero_ref, one_ref, two_ref, three_ref):
    for k, ref in enumerate((zero_ref, one_ref, two_ref, three_ref)):
        block = pl.ds(((x_ref[0] + k) & 3) * 2, 2)
        ref[...] = (mine_ref[block].astype(F32) + theirs_ref[block].astype(F32)).astype(BF16)


def join_kernel(part_ref, zero_ref, one_ref, two_ref, three_ref, out_ref):
    for z in range(2):
        narrow = part_ref[z, :, : 5 * D].astype(F32)
        qkv = zero_ref[z].astype(F32)
        for ref in (one_ref, two_ref, three_ref):
            qkv = qkv + ref[z].astype(F32)
        for j in range(8):
            rows = slice(4 * j, 4 * j + 4)
            out_ref[z * 8 + j, :, : 5 * D] = narrow[rows].astype(BF16)
            start = 5 * D + D * (j // 2)
            down = part_ref[z, 16 * (j % 2) : 16 * (j % 2) + 16, start : start + D].astype(F32)
            for s in range(4):
                cols = slice((5 + s) * D, (6 + s) * D)
                out_ref[z * 8 + j, :, cols] = down[4 * s : 4 * s + 4].astype(BF16)
            padded = jnp.concatenate([qkv[rows], jnp.zeros((4, HEAD), F32)], axis=1)
            out_ref[z * 8 + j, :, 9 * D :] = padded.astype(BF16)


def last_kernel(
    got_ref, qkv_rows_ref, up_rows_ref, gains_ref, qkv_ref, out_ref, up_ref, down_ref, gain_ref
):
    grad_scale = 1.0 / math.sqrt(OWN * 128)
    total = got_ref[0, :, : 9 * D].astype(F32)
    for i in range(1, 16):
        total = total + got_ref[i, :, : 9 * D].astype(F32)
    total = total * grad_scale
    out_ref[...] = total[:, :D]
    up = total[:, D : 5 * D]
    up_ref[...] = up
    for s in range(4):
        down_ref[4 * s : 4 * s + 4] = total[:, (5 + s) * D : (6 + s) * D]
    heads = []
    for h in range(HEADS):
        pair = got_ref[h, :, 9 * D :].astype(F32) + got_ref[8 + h, :, 9 * D :].astype(F32)
        heads.append(pair * grad_scale)
    pieces = [heads[h][:, p * HEAD : (p + 1) * HEAD] for p in range(3) for h in range(HEADS)]
    qkv = jnp.concatenate(pieces, axis=1)
    qkv_ref[...] = qkv
    eye = lax.broadcasted_iota(jnp.int32, (4, 4), 0) == lax.broadcasted_iota(
        jnp.int32, (4, 4), 1
    )
    products = (qkv * qkv_rows_ref[...].astype(F32), up * up_rows_ref[...].astype(F32))
    for i, product in enumerate(products):
        column = jnp.sum(product, axis=1, keepdims=True)
        row = jnp.sum(jnp.where(eye, column, 0.0), axis=0, keepdims=True)
        gain_ref[i : i + 1] = row / gains_ref[i : i + 1]


def enter_kernel(
    field_ref, mask_ref, embed_ref, cot_ref, low_ref, up_ref, cup_ref
):
    sea = embed_ref[0:1].astype(F32)
    land = embed_ref[1:2].astype(F32)
    mask = (mask_ref[...] == 1).astype(F32)
    eye = lax.broadcasted_iota(jnp.int32, (16, 16), 0) == lax.broadcasted_iota(
        jnp.int32, (16, 16), 1
    )
    for row in range(4):
        column = jnp.sum(jnp.where(eye, mask[row : row + 1], 0.0), axis=1, keepdims=True)
        chosen = jnp.where(column > 0.5, land, sea)
        hidden_ref, grad_ref = (up_ref, cup_ref) if row < 2 else (low_ref, low_ref)
        offset = 0 if row < 2 else HALF
        for level in range(3):
            start = (level * 2 + row % 2) * 16
            rows = slice(start, start + 16)
            hidden_ref[rows] = (field_ref[level, row].astype(F32) + chosen).astype(BF16)
            grad_ref[offset + start : offset + start + 16] = cot_ref[level, row]


def core_columns(array, width, core):
    pieces = [
        array[:, (2 * g + core) * width : (2 * g + core + 1) * width] for g in range(8)
    ]
    return jnp.concatenate(pieces, axis=1)


def middle_kernel(
    core_ref, att_ref, low_ref, up_ref, cup_ref, gain_ref, w_out_ref, w_up_ref, w_down_ref,
    out_low_ref, out_up_ref, packed_ref, gm_ref, send_ref, keep_ref,
):
    first = core_ref[0] == 0
    attended = jnp.concatenate([unpack_heads(att_ref, 0), unpack_heads(att_ref, HEAD)], axis=0)
    hidden = jnp.concatenate([low_ref[:HALF], up_ref[...]], axis=0).astype(F32)
    cot = jnp.concatenate([low_ref[HALF:], cup_ref[...]], axis=0)
    gain = gain_ref[1:2, :]
    mixed = (hidden + dot(attended, w_out_ref[...])).astype(BF16).astype(F32)
    unit, inverse = norm_stats(mixed)
    normed = (unit * gain).astype(BF16)
    pre = dot(normed, w_up_ref[...])
    root = math.sqrt(2.0 / math.pi)
    square = pre * pre
    bend = jnp.tanh(root * pre * (1.0 + 0.044715 * square))
    half_up = 0.5 * (1.0 + bend)
    activated = (pre * half_up).astype(BF16)
    slope = half_up + 0.5 * pre * (1.0 - bend * bend) * root * (1.0 + 3 * 0.044715 * square)
    grad_pre = (dot_nt(cot, w_down_ref[...]) * slope).astype(BF16)
    grad_normed = dot_nt(grad_pre, w_up_ref[...])
    grad_mixed = cot.astype(F32) + norm_back(grad_normed, unit, inverse, gain)
    gm_ref[...] = grad_mixed
    grad_low = grad_mixed.astype(BF16)
    grad_attended = dot_nt(grad_low, w_out_ref[...]).astype(BF16)
    for h in range(HEADS):
        packed_ref[h] = jnp.concatenate(pack_head(grad_attended, h * HEAD), axis=1)
    layer_out = (mixed + dot(activated, w_down_ref[...])).astype(BF16)
    out_low_ref[...] = layer_out[:HALF]
    out_up_ref[...] = layer_out[HALF:]
    start = 0
    for array, width in ((activated, 128), (normed, 32), (attended, 32)):
        zero = core_columns(array, width, 0)
        one = core_columns(array, width, 1)
        cols = slice(start, start + 8 * width)
        keep_ref[:, cols] = jnp.where(first, zero, one)
        send_ref[:, cols] = jnp.where(first, one, zero)
        start += 8 * width
    for array in (cot, grad_pre, grad_low):
        send_ref[:, start : start + array.shape[1]] = array
        start += array.shape[1]


def partial_kernel(keep_ref, sent_ref, got_ref, out_ref):
    def both(own_ref, start, width):
        cols = slice(start, start + width)
        return jnp.concatenate([own_ref[:, cols], got_ref[:, cols]], axis=0)

    product = dot_tn(both(keep_ref, 0, 2 * D), both(sent_ref, 3 * D, D)).astype(BF16)
    for g in range(8):
        for s in range(4):
            at = g * 128 + s * 32
            out_ref[g, :, (5 + s) * D : (6 + s) * D] = product[at : at + 32]
    product = dot_tn(both(keep_ref, 2 * D, D // 2), both(sent_ref, 4 * D, FF)).astype(BF16)
    for g in range(8):
        out_ref[g, :, D : 5 * D] = product[g * 32 : g * 32 + 32]
    product = dot_tn(both(keep_ref, 5 * D // 2, D // 2), both(sent_ref, 8 * D, D)).astype(BF16)
    for g in range(8):
        out_ref[g, :, :D] = product[g * 32 : g * 32 + 32]


def input_grad_kernel(
    packed_ref, low_ref, up_ref, gain_ref, gm_ref, w_ref, glow_ref, gup_ref
):
    halves = []
    for a in range(2):
        parts = [unpack_heads(packed_ref, place * 128 + a * HEAD) for place in range(3)]
        halves.append(jnp.concatenate(parts, axis=1))
    grad_projected = jnp.concatenate(halves, axis=0)
    hidden = jnp.concatenate([low_ref[:HALF], up_ref[...]], axis=0).astype(F32)
    unit, inverse = norm_stats(hidden)
    grad_normed = dot_nt(grad_projected, w_ref[...])
    grad = gm_ref[...] + norm_back(grad_normed, unit, inverse, gain_ref[0:1, :])
    grad = grad.astype(BF16)
    glow_ref[...] = grad[:HALF]
    gup_ref[...] = grad[HALF:]


VMEM = pl.BlockSpec(memory_space=pltpu.VMEM)
SMEM = pl.BlockSpec(memory_space=pltpu.SMEM)


def call(kernel, outs, specs, scratch=(), vmem=12, cost=0):
    shapes = tuple(jax.ShapeDtypeStruct(shape, dtype) for shape, dtype in outs)
    return pl.pallas_call(
        kernel,
        out_shape=shapes,
        in_specs=specs,
        out_specs=(VMEM,) * len(outs),
        scratch_shapes=list(scratch),
        compiler_params=pltpu.CompilerParams(vmem_limit_bytes=vmem * 1024 * 1024),
        cost_estimate=pl.CostEstimate(flops=0, bytes_accessed=cost, transcendentals=0),
    )


def shards(
    fields, land_sea, surface_embed, norm_gains, w_qkv, head_scales, w_out, w_up, w_down, cotangent
):
    lat = lax.axis_index(LAT)
    lon = lax.axis_index(LON)
    device = lax.axis_index(ALL)
    core = lax.axis_index("c").astype(jnp.int32).reshape(1)
    x_index = lax.axis_index("x").astype(jnp.int32).reshape(1)
    forward = [(i, (i + 1) % 16) for i in range(16)]
    backward = [(j, i) for i, j in forward]
    across = [(0, 1), (1, 0)]
    half = ((HALF, D), BF16)
    low, up, cot_up = call(enter_kernel, [((OWN, D), BF16), half, half], [VMEM] * 4, cost=20_000_000)(
        fields, land_sea, surface_embed, cotangent
    )
    low = lax.ppermute(low, LAT, forward)

    scale = head_scales[lon]
    valid = jnp.where(lat == 0, 0.0, 1.0)
    scal = jnp.stack([scale * (0.5 * math.log2(math.e)), scale, valid]).astype(F32)
    rows_qkv = lax.dynamic_slice_in_dim(w_qkv, device * 4, 4, axis=0)
    rows_up = lax.dynamic_slice_in_dim(w_up, device * 4, 4, axis=0)
    gains = lax.dynamic_slice_in_dim(norm_gains, device * 4, 4, axis=1)
    scal, rows_qkv, rows_up, gains = lax.optimization_barrier((scal, rows_qkv, rows_up, gains))

    normed, packed = call(
        project_kernel,
        [((2, HALF, D), BF16), ((HEADS, HALF, 384), BF16)],
        [VMEM] * 4,
        vmem=12,
        cost=8_000_000,
    )(low, up, norm_gains, w_qkv)
    normed_all = lax.all_gather(normed, LON, axis=0, tiled=False)
    heads = lax.all_to_all(packed, LON, 0, 0, tiled=True).reshape(ROWS, 384)

    wide = 2 * ROWS
    att, inv = call(
        attend_kernel,
        [((ROWS, 128), BF16), ((ROWS, 128), F32)],
        [SMEM, VMEM],
        [
            pltpu.VMEM((wide, 128), BF16),
            pltpu.VMEM((wide, 128), BF16),
            pltpu.VMEM((2, wide, 128), BF16),
        ],
        vmem=20,
        cost=20_000_000,
    )(scal, heads)
    att_rows = lax.all_to_all(att.reshape(HEADS, HALF, 128), LON, 0, 0, tiled=True)

    out_low, out_up, packed_grad, grad_mixed, sent, keep = call(
        middle_kernel,
        [
            half,
            half,
            ((HEADS, HALF, 128), BF16),
            ((OWN, D), F32),
            ((OWN, 9 * D), BF16),
            ((OWN, 3 * D), BF16),
        ],
        [SMEM] + [VMEM] * 8,
        vmem=24,
    )(core, att_rows, low, up, cot_up, norm_gains, w_out, w_up, w_down)
    grad_heads = lax.all_to_all(packed_grad, LON, 0, 0, tiled=True).reshape(ROWS, 128)
    received = lax.ppermute(sent, "c", across)
    out_back = lax.ppermute(out_low, LAT, backward)
    (pair,) = call(partial_kernel, [((8, 32, 9 * D), BF16)], [VMEM] * 3, vmem=24)(
        keep, sent, received
    )
    part = lax.psum_scatter(pair, "x", scatter_dimension=0, tiled=True)

    block = ((8, 32, 192), BF16)
    packed_back, mine, other = call(
        attend_back_kernel,
        [((ROWS, 384), BF16), block, block],
        [SMEM] * 2 + [VMEM] * 5,
        [
            pltpu.VMEM((wide, 128), BF16),
            pltpu.VMEM((wide, 128), BF16),
            pltpu.VMEM((2, wide, 128), BF16),
            pltpu.VMEM((2, wide, 128), BF16),
            pltpu.VMEM((2, wide, 128), BF16),
        ],
        vmem=32,
        cost=1_000_000_000,
    )(scal, core, heads, grad_heads, att, inv, normed_all)
    grad_packed = lax.all_to_all(
        packed_back.reshape(HEADS, HALF, 384), LON, 0, 0, tiled=True
    )
    theirs = lax.ppermute(other, "c", across)
    blocks = call(pair_kernel, [((2, 32, 192), BF16)] * 4, [SMEM, VMEM, VMEM])(
        x_index, mine, theirs
    )
    blocks = [blocks[0]] + [
        lax.ppermute(blocks[k], "x", [(i, (i + k) % 4) for i in range(4)]) for k in (1, 2, 3)
    ]
    grad_low, grad_up = call(
        input_grad_kernel,
        [half] * 2,
        [VMEM] * 6,
        vmem=12,
    )(grad_packed, low, up, norm_gains, grad_mixed, w_qkv)

    part, grad_low, grad_up = lax.optimization_barrier((part, grad_low, grad_up))
    grad_back = lax.ppermute(grad_low, LAT, backward)
    (joined,) = call(join_kernel, [((16, 4, 9 * D + 256), BF16)], [VMEM] * 5)(part, *blocks)
    got = lax.all_to_all(joined, ("zh",) + LON, 0, 0, tiled=True)
    grad_qkv, grad_out, grad_up_w, grad_down, grad_gains = call(
        last_kernel,
        [
            ((4, 3 * D), F32),
            ((4, D), F32),
            ((4, FF), F32),
            ((16, D), F32),
            ((2, 4), F32),
        ],
        [VMEM] * 4,
    )(got, rows_qkv, rows_up, gains)

    def place(own, moved):
        shape = (3, 2, 16, D)
        return jnp.concatenate([own.reshape(shape), moved.reshape(shape)], axis=1)

    return (
        place(out_up, out_back),
        place(grad_up, grad_back),
        grad_qkv,
        grad_out,
        grad_up_w,
        grad_down,
        grad_gains,
    )


def solution(mesh):
    fine = Mesh(mesh.devices.reshape(AXIS_SIZES), ALL)
    grid = P(None, LAT, LON, None)
    in_specs = (grid, P(LAT, LON), P(), P(), P(), P(), P(), P(), P(), grid)
    rows = P(ALL, None)
    out_specs = (grid, grid, rows, rows, rows, rows, P(None, ALL))
    return jax.shard_map(shards, mesh=fine, in_specs=in_specs, out_specs=out_specs, check_vma=False)
```

time: 182 us -> 139 us (0.76)
  waiting for transfers between devices: 51 us -> 27 us
  Pallas kernels: 37.2 us -> 22.6 us
  other arithmetic: 11.7 us -> 2.11 us
  local copies, waits for them, and re-layouts: 7.41 us -> 17 us
  starting transfers between devices: 44.8 us -> 35.4 us
  blocking collectives: 12.9 us -> 17.8 us
    all_to_all x3 -> x1, starting transfers between devices: 18.4 us -> 3.59 us  [shards(): got = lax.all_to_all(joined, ('zh',) + LON, 0, 0, tiled=True)]
    pallas_call x4 -> x9, Pallas kernels: 34.2 us -> 21 us  [the longest x1 8.45 us: shards(): call(attend_back_kernel, [((ROWS, 384), BF16), block, block], [SMEM] * 2...]
    unnamed x17 -> x46, local copies, waits for them, and re-layouts: 2.58 us -> 15.6 us
    all_gather x1, waiting for transfers between devices: 12.2 us -> 0.01 us  [shards(): normed_all = lax.all_gather(normed, LON, axis=0, tiled=False)]
    all_to_all x3 -> x1, waiting for transfers between devices: 10.1 us -> 0.01 us  [shards(): got = lax.all_to_all(joined, ('zh',) + LON, 0, 0, tiled=True)]
    all_to_all x0 -> x1, blocking collectives: none -> 9.4 us  [shards(): lax.all_to_all(att.reshape(HEADS, HALF, 128), LON, 0, 0, tiled=True)]
    ppermute x1, waiting for transfers between devices: 0.01 us -> 8.27 us  [shards(): out_back = lax.ppermute(out_low, LAT, backward)]
    convert_element_type x3 -> x0, other arithmetic: 6.2 us -> none  [the longest x1 4.47 us: shards(): pair = (mine.astype(F32) + theirs.astype(F32)).astype(BF16)]
  transfers between devices with their start and end apart: 12 -> 13, of which waited for: 8 -> 7; matrix products, arithmetic and copies ran while one was open for 7% -> 3% of each run, Pallas kernels for 11% -> 14%
where the time goes in v2:
time: 139 us; the launch traced here: 138 us
  starting transfers between devices  35.4 us (25%)
  waiting for transfers between devices  27 us (19%)
  Pallas kernels  22.6 us (16%)
  blocking collectives  17.8 us (13%)
  local copies, waits for them, and re-layouts  17 us (12%)
  between operations  16.4 us (12%)
  other arithmetic  2.11 us (2%)
    unnamed x46, local copies, waits for them, and re-layouts  15.6 us
    ppermute x1, starting transfers between devices, shards(): received = lax.ppermute(sent, 'c', across)  9.92 us
    all_to_all x1, blocking collectives, shards(): lax.all_to_all(att.reshape(HEADS, HALF, 128), LON, 0, 0, tiled=True)  9.4 us
    pallas_call x1, Pallas kernels, shards(): call(attend_back_kernel, [((ROWS, 384), BF16), block, block], [SMEM] * 2...  8.45 us
    all_to_all x1, blocking collectives, shards(): lax.all_to_all(packed_grad, LON, 0, 0, tiled=True).reshape(ROWS, 128)  8.45 us
    ppermute x1, waiting for transfers between devices, shards(): out_back = lax.ppermute(out_low, LAT, backward)  8.27 us
    all_to_all x1, waiting for transfers between devices, shards(): heads = lax.all_to_all(packed, LON, 0, 0, tiled=True).reshape(ROWS, 384)  6.43 us
    ppermute x1, starting transfers between devices, shards(): low = lax.ppermute(low, LAT, forward)  4.99 us
  transfers between devices with their start and end apart: 13, of which 7 were waited for; matrix products, arithmetic and copies ran while one was open for 3% of the time, Pallas kernels for 14%

profile of v2, /device:TPU:1, one launch (start us, length us, event | category | flops | bytes accessed | tf_op | source)
XLA Modules:
  0.0 138.4 jit_solution(10453333800070474103)
XLA Ops:
  8.1 0.9 copy-done.11
  9.0 0.9 copy-done.12
  12.0 5.0 %collective-permute-start = (bf16[192,512]{1,0:T(8,128)(2,1)S(1)}, bf16[192,512]{1,0:T(8,128)(2,1)S(1)}, u32[]{:S(2)}, u32[]{:S(2)}) collective-permute-start(bf16[192,512]{1,0:T(8,128)(2,1)S(1)} %get-tuple-element.42), channel_id=1, source_target_pairs={{0,8},{8,16},{16,24},{24,32},{32,40},{40,48},{48,56},{56,64},{64,7... | collective-permute-start | bytes 589832 | tf_op jit(solution)/shard_map/ppermute | solution.py:419
  17.0 2.6 %collective-permute-done.low_ref = bf16[192,512]{1,0:T(8,128)(2,1)S(1)} collective-permute-done((bf16[192,512]{1,0:T(8,128)(2,1)S(1)}, bf16[192,512]{1,0:T(8,128)(2,1)S(1)}, u32[]{:S(2)}, u32[]{:S(2)}) %collective-permute-start) | collective-permute-done | bytes 196640 | tf_op jit(solution)/shard_map/ppermute | solution.py:419
  19.6 1.4 %copy-done = bf16[512,1536]{1,0:T(8,128)(2,1)S(1)} copy-done((bf16[512,1536]{1,0:T(8,128)(2,1)S(1)}, bf16[512,1536]{1,0:T(8,128)(2,1)}, u32[]{:S(2)}) %copy-start) | copy-done | bytes 1572888
  21.7 1.5 %shard_map.154 = (bf16[2,96,512]{2,1,0:T(8,128)(2,1)}, bf16[8,96,384]{2,1,0:T(8,128)(2,1)}) custom-call(bf16[192,512]{1,0:T(8,128)(2,1)S(1)} %collective-permute-done.low_ref, bf16[96,512]{1,0:T(8,128)(2,1)S(1)} %get-tuple-element.43.up_ref, f32[2,512]{1,0:T(2,128)S(1)} %copy-done.15, bf16[512,1536]{1,0:T(8,128)(2,1)S(1)} %copy-done), custom_call_target="tpu_custom_call" | custom-call | bytes 8000000 | tf_op jit(solution)/shard_map/pallas_call | solution.py:429
  24.7 4.6 %all-to-all-start = ((bf16[8,96,384]{2,1,0:T(8,128)(2,1)}), bf16[8,96,384]{2,1,0:T(8,128)(2,1)S(1)}, u32[]{:S(2)}, u32[]{:S(2)}) async-start(bf16[8,96,384]{2,1,0:T(8,128)(2,1)} %get-tuple-element.44), calls=%async_computation | async-start | bytes 1179648 | tf_op jit(solution)/shard_map/all_to_all | solution.py:437
  30.9 6.4 %all-to-all-done = bf16[8,96,384]{2,1,0:T(8,128)(2,1)S(1)} async-done(((bf16[8,96,384]{2,1,0:T(8,128)(2,1)}), bf16[8,96,384]{2,1,0:T(8,128)(2,1)S(1)}, u32[]{:S(2)}, u32[]{:S(2)}) %all-to-all-start) | async-done | bytes 589856 | tf_op jit(solution)/shard_map/all_to_all | solution.py:437
  37.3 3.7 %shard_map.155 = (bf16[768,128]{1,0:T(8,128)(2,1)S(1)}, f32[768,128]{1,0:T(8,128)S(1)}) custom-call(f32[3]{0:T(128)S(1)} %pad_maximum_fusion.2.scal_ref, bf16[768,384]{1,0:T(8,128)(2,1)S(1)} %bitcast.12), custom_call_target="tpu_custom_call" | custom-call | bytes 20000000 | tf_op jit(solution)/shard_map/pallas_call | solution.py:440
  41.1 9.4 %all_to_all.25.att_ref = bf16[8,96,128]{2,1,0:T(8,128)(2,1)S(1)} all-to-all(bf16[8,96,128]{2,1,0:T(8,128)(2,1)S(1)} %bitcast.15), channel_id=1, replica_groups=mesh['x'=4,'zh'=2,'c'=2,'zl'=2,'y'=4] {'zl','y'}, dimensions={0} | all-to-all | bytes 393216 | tf_op jit(solution)/shard_map/all_to_all | solution.py:452
  50.5 1.6 %copy-done.2 = bf16[512,2048]{1,0:T(8,128)(2,1)S(1)} copy-done((bf16[512,2048]{1,0:T(8,128)(2,1)S(1)}, bf16[512,2048]{1,0:T(8,128)(2,1)}, u32[]{:S(2)}) %copy-start.2) | copy-done | bytes 2097176
  52.1 1.6 %copy-done.3 = bf16[2048,512]{1,0:T(8,128)(2,1)S(1)} copy-done((bf16[2048,512]{1,0:T(8,128)(2,1)S(1)}, bf16[2048,512]{1,0:T(8,128)(2,1)}, u32[]{:S(2)}) %copy-start.3) | copy-done | bytes 2097176
  54.6 3.4 %shard_map.156 = (bf16[96,512]{1,0:T(8,128)(2,1)S(1)}, bf16[96,512]{1,0:T(8,128)(2,1)S(1)}, bf16[8,96,128]{2,1,0:T(8,128)(2,1)S(1)}, f32[192,512]{1,0:T(8,128)S(...) custom-call(s32[1]{0:T(128)} %bitcast.core_ref, bf16[8,96,128]{2,1,0:T(8,128)(2,1)S(1)} %all_to_all.25.att_ref, ...), custom_call_target="tpu_custom_call" | custom-call | tf_op jit(solution)/shard_map/pallas_call | solution.py:454
  59.4 9.9 %collective-permute-start.2 = (bf16[192,4608]{1,0:T(8,128)(2,1)S(1)}, bf16[192,4608]{1,0:T(8,128)(2,1)S(1)}, u32[]{:S(2)}, u32[]{:S(2)}) collective-permute-start(bf16[192,4608]{1,0:T(8,128)(2,1)S(1)} %get-tuple-element.50.sent_ref), channel_id=1, source_target_pairs={{0,8},{8,0},{1,9},{9,1},{2,10},{10,2},{3,11},{11,3},{4,12},{12,4},... | collective-permute-start | bytes 5308424 | tf_op jit(solution)/shard_map/ppermute | solution.py:468
  69.3 3.3 %collective-permute-done.2.got_ref = bf16[192,4608]{1,0:T(8,128)(2,1)S(1)} collective-permute-done((bf16[192,4608]{1,0:T(8,128)(2,1)S(1)}, bf16[192,4608]{1,0:T(8,128)(2,1)S(1)}, u32[]{:S(2)}, u32[]{:S(2)}) %collective-permute-start.2) | collective-permute-done | bytes 1769504 | tf_op jit(solution)/shard_map/ppermute | solution.py:468
  72.6 2.8 %shard_map.157 = bf16[8,32,4608]{2,1,0:T(8,128)(2,1)} custom-call(bf16[192,1536]{1,0:T(8,128)(2,1)S(1)} %get-tuple-element.49.keep_ref, bf16[192,4608]{1,0:T(8,128)(2,1)S(1)} %get-tuple-element.50.sent_ref, bf16[192,4608]{1,0:T(8,128)(2,1)S(1)} %collective-permute-done.2.got_ref), custom_call_target="tpu_custom_call" | custom-call | tf_op jit(solution)/shard_map/pallas_call | solution.py:470
  75.5 8.4 %all_to_all.26 = bf16[8,96,128]{2,1,0:T(8,128)(2,1)S(1)} all-to-all(bf16[8,96,128]{2,1,0:T(8,128)(2,1)S(1)} %get-tuple-element.51), channel_id=1, replica_groups=mesh['x'=4,'zh'=2,'c'=2,'zl'=2,'y'=4] {'zl','y'}, dimensions={0} | all-to-all | bytes 393216 | tf_op jit(solution)/shard_map/all_to_all | solution.py:467
  84.0 1.4 %copy-done.4 = bf16[16,96,512]{2,1,0:T(8,128)(2,1)S(1)} copy-done((bf16[16,96,512]{2,1,0:T(8,128)(2,1)S(1)}, bf16[16,96,512]{2,1,0:T(8,128)(2,1)}, u32[]{:S(2)}) %copy-start.4) | copy-done | bytes 1572888
  85.4 1.0 copy-done.10
  86.4 8.5 %shard_map.158 = (bf16[768,384]{1,0:T(8,128)(2,1)}, bf16[8,32,192]{2,1,0:T(8,128)(2,1)S(1)}, bf16[8,32,192]{2,1,0:T(8,128)(2,1)S(1)}) custom-call(f32[3]{0:T(128)S(1)} %pad_maximum_fusion.2.scal_ref, s32[1]{0:T(128)} %bitcast.core_ref, bf16[768,384]{1,0:T(8,128)(2,1)S(1)} %bitcast.13, bf16[768,128]{1,0:T(8,128)(2,1)S(1)} %bitcast.16, ...), custom_call_target="tpu_custom_call" | custom-call | bytes 1000000000 | tf_op jit(solution)/shard_map/pallas_call | solution.py:476
  95.5 3.5 %all-to-all-start.3 = ((bf16[8,96,384]{2,1,0:T(8,128)(2,1)}), bf16[8,96,384]{2,1,0:T(8,128)(2,1)S(1)}, u32[]{:S(2)}, u32[]{:S(2)}) async-start(bf16[8,96,384]{2,1,0:T(8,128)(2,1)} %bitcast.8), calls=%async_computation.4 | async-start | bytes 1179648 | tf_op jit(solution)/shard_map/all_to_all | solution.py:490
  99.0 1.9 %collective-permute-start.4 = (bf16[8,32,192]{2,1,0:T(8,128)(2,1)}, bf16[8,32,192]{2,1,0:T(8,128)(2,1)S(1)}, u32[]{:S(2)}, u32[]{:S(2)}) collective-permute-start(bf16[8,32,192]{2,1,0:T(8,128)(2,1)} %copy-done.19), channel_id=1, source_target_pairs={{0,8},{8,0},{1,9},{9,1},{2,10},{10,2},{3,11},{11,3},{4,12},{12,4},... | collective-permute-start | bytes 294920 | tf_op jit(solution)/shard_map/ppermute | solution.py:493
  100.9 1.2 collective-permute-done.4.theirs_ref
  102.2 1.8 %collective-permute-start.6 = (bf16[2,32,192]{2,1,0:T(8,128)(2,1)S(1)}, bf16[2,32,192]{2,1,0:T(8,128)(2,1)S(1)}, u32[]{:S(2)}, u32[]{:S(2)}) collective-permute-start(bf16[2,32,192]{2,1,0:T(8,128)(2,1)S(1)} %get-tuple-element.65), channel_id=1, source_target_pairs={{0,64},{32,96},{64,0},{96,32},{1,65},{33,97},{65,1},{97,33},{2,66}... | collective-permute-start | bytes 73736 | tf_op jit(solution)/shard_map/ppermute | solution.py:498
  104.0 0.9 collective-permute-start.7
  104.9 4.7 %all-to-all-done.3.packed_ref = bf16[8,96,384]{2,1,0:T(8,128)(2,1)S(1)} async-done(((bf16[8,96,384]{2,1,0:T(8,128)(2,1)}), bf16[8,96,384]{2,1,0:T(8,128)(2,1)S(1)}, u32[]{:S(2)}, u32[]{:S(2)}) %all-to-all-start.3) | async-done | bytes 589856 | tf_op jit(solution)/shard_map/all_to_all | solution.py:490
  110.4 1.1 copy-done.5
  111.5 0.9 shard_map.161
  112.4 3.6 %all-to-all-start.4 = ((bf16[16,4,4864]{2,1,0:T(4,128)(2,1)}), bf16[16,4,4864]{2,1,0:T(4,128)(2,1)S(1)}, u32[]{:S(2)}, u32[]{:S(2)}) async-start(bf16[16,4,4864]{2,1,0:T(4,128)(2,1)} %shard_map.161), calls=%async_computation.5 | async-start | bytes 1245184 | tf_op jit(solution)/shard_map/all_to_all | solution.py:510
  116.0 1.2 collective-permute-start.1
  117.2 2.8 %collective-permute-start.3 = (bf16[96,512]{1,0:T(8,128)(2,1)S(1)}, bf16[96,512]{1,0:T(8,128)(2,1)S(1)}, u32[]{:S(2)}, u32[]{:S(2)}) collective-permute-start(bf16[96,512]{1,0:T(8,128)(2,1)S(1)} %get-tuple-element.59), channel_id=1, source_target_pairs={{8,0},{16,8},{24,16},{32,24},{40,32},{48,40},{56,48},{64,56},{72,6... | collective-permute-start | bytes 294920 | tf_op jit(solution)/shard_map/ppermute | solution.py:508
  120.0 8.3 %collective-permute-done.1 = bf16[96,512]{1,0:T(8,128)(2,1)S(1)} collective-permute-done((bf16[96,512]{1,0:T(8,128)(2,1)S(1)}, bf16[96,512]{1,0:T(8,128)(2,1)S(1)}, u32[]{:S(2)}, u32[]{:S(2)}) %collective-permute-start.1) | collective-permute-done | bytes 98336 | tf_op jit(solution)/shard_map/ppermute | solution.py:469
  (61 shorter events, 11.6 us)
Async XLA Ops:
  8.0 76.0 %all-gather.3.cloned.1.call-start = ((), (), s32[]{:S(2)}) async-start(), calls=%async_computation.7 | async-start | bytes 1769472 | tf_op jit(solution)/shard_map/all_gather | solution.py:436
  8.0 0.9 copy-start.11
  9.0 0.9 copy-start.12
  9.9 0.7 copy-start.17
  11.3 12.1 %copy-start.22 = (f32[8]{0:T(128)S(1)}, f32[8]{0:T(128)}, u32[]{:S(2)}) copy-start(f32[8]{0:T(128)} %param.15) | copy-start | bytes 100
  11.3 13.3 %copy-start.16 = (f32[2,512]{1,0:T(2,128)S(1)}, f32[2,512]{1,0:T(2,128)}, u32[]{:S(2)}) copy-start(f32[2,512]{1,0:T(2,128)} %gain_ref.5) | copy-start | bytes 12292
  12.0 7.6 %collective-permute-start = (bf16[192,512]{1,0:T(8,128)(2,1)S(1)}, bf16[192,512]{1,0:T(8,128)(2,1)S(1)}, u32[]{:S(2)}, u32[]{:S(2)}) collective-permute-start(bf16[192,512]{1,0:T(8,128)(2,1)S(1)} %get-tuple-element.42), channel_id=1, source_target_pairs={{0,8},{8,16},{16,24},{24,32},{32,40},{40,48},{48,56},{56,64},{64,7... | collective-permute-start | bytes 589832 | tf_op jit(solution)/shard_map/ppermute | solution.py:419
  19.6 1.4 %copy-start = (bf16[512,1536]{1,0:T(8,128)(2,1)S(1)}, bf16[512,1536]{1,0:T(8,128)(2,1)}, u32[]{:S(2)}) copy-start(bf16[512,1536]{1,0:T(8,128)(2,1)} %w_ref.3) | copy-start | bytes 4718596
  21.0 0.7 copy-start.15
  21.7 8.3 %copy-start.1 = (bf16[512,1536]{1,0:T(8,128)(2,1)S(1)}, bf16[512,1536]{1,0:T(8,128)(2,1)}, u32[]{:S(2)}) copy-start(bf16[512,1536]{1,0:T(8,128)(2,1)} %w_ref.3) | copy-start | bytes 4718596
  21.7 28.7 %copy-start.6 = (bf16[512,512]{1,0:T(8,128)(2,1)S(1)}, bf16[512,512]{1,0:T(8,128)(2,1)}, u32[]{:S(2)}) copy-start(bf16[512,512]{1,0:T(8,128)(2,1)} %w_out_ref.1) | copy-start | bytes 1572868
  24.7 12.6 %all-to-all-start = ((bf16[8,96,384]{2,1,0:T(8,128)(2,1)}), bf16[8,96,384]{2,1,0:T(8,128)(2,1)S(1)}, u32[]{:S(2)}, u32[]{:S(2)}) async-start(bf16[8,96,384]{2,1,0:T(8,128)(2,1)} %get-tuple-element.44), calls=%async_computation | async-start | bytes 1179648 | tf_op jit(solution)/shard_map/all_to_all | solution.py:437
  29.3 81.1 %reduce-scatter.2.cloned.1.call-start = ((), (), s32[]{:S(2)}) async-start(), calls=%async_computation.6 | async-start | bytes 2949120 | tf_op jit(solution)/shard_map/reduce_scatter | solution.py:473
  41.1 9.4 %copy-start.9 = (f32[768,128]{1,0:T(8,128)}, f32[768,128]{1,0:T(8,128)S(1)}, u32[]{:S(2)}) copy-start(f32[768,128]{1,0:T(8,128)S(1)} %get-tuple-element.52.inv_ref) | copy-start | bytes 1179652
  50.5 1.6 %copy-start.2 = (bf16[512,2048]{1,0:T(8,128)(2,1)S(1)}, bf16[512,2048]{1,0:T(8,128)(2,1)}, u32[]{:S(2)}) copy-start(bf16[512,2048]{1,0:T(8,128)(2,1)} %w_up_ref.1) | copy-start | bytes 6291460
  52.1 1.6 %copy-start.3 = (bf16[2048,512]{1,0:T(8,128)(2,1)S(1)}, bf16[2048,512]{1,0:T(8,128)(2,1)}, u32[]{:S(2)}) copy-start(bf16[2048,512]{1,0:T(8,128)(2,1)} %w_down_ref.1) | copy-start | bytes 6291460
  53.7 0.9 copy-start.14
  58.0 0.8 copy-start.7
  59.4 13.2 %collective-permute-start.2 = (bf16[192,4608]{1,0:T(8,128)(2,1)S(1)}, bf16[192,4608]{1,0:T(8,128)(2,1)S(1)}, u32[]{:S(2)}, u32[]{:S(2)}) collective-permute-start(bf16[192,4608]{1,0:T(8,128)(2,1)S(1)} %get-tuple-element.50.sent_ref), channel_id=1, source_target_pairs={{0,8},{8,0},{1,9},{9,1},{2,10},{10,2},{3,11},{11,3},{4,12},{12,4},... | collective-permute-start | bytes 5308424 | tf_op jit(solution)/shard_map/ppermute | solution.py:468
  84.0 1.4 %copy-start.4 = (bf16[16,96,512]{2,1,0:T(8,128)(2,1)S(1)}, bf16[16,96,512]{2,1,0:T(8,128)(2,1)}, u32[]{:S(2)}) copy-start(bf16[16,96,512]{2,1,0:T(8,128)(2,1)} %all-gather.3.cloned.1.call-done) | copy-start | bytes 4718596
  85.4 1.0 copy-start.10
  86.4 23.2 %copy-start.8 = (f32[192,512]{1,0:T(8,128)S(1)}, f32[192,512]{1,0:T(8,128)}, u32[]{:S(2)}) copy-start(f32[192,512]{1,0:T(8,128)} %copy-done.7) | copy-start | bytes 1179652
  95.5 14.1 %all-to-all-start.3 = ((bf16[8,96,384]{2,1,0:T(8,128)(2,1)}), bf16[8,96,384]{2,1,0:T(8,128)(2,1)S(1)}, u32[]{:S(2)}, u32[]{:S(2)}) async-start(bf16[8,96,384]{2,1,0:T(8,128)(2,1)} %bitcast.8), calls=%async_computation.4 | async-start | bytes 1179648 | tf_op jit(solution)/shard_map/all_to_all | solution.py:490
  99.0 3.1 %collective-permute-start.4 = (bf16[8,32,192]{2,1,0:T(8,128)(2,1)}, bf16[8,32,192]{2,1,0:T(8,128)(2,1)S(1)}, u32[]{:S(2)}, u32[]{:S(2)}) collective-permute-start(bf16[8,32,192]{2,1,0:T(8,128)(2,1)} %copy-done.19), channel_id=1, source_target_pairs={{0,8},{8,0},{1,9},{9,1},{2,10},{10,2},{3,11},{11,3},{4,12},{12,4},... | collective-permute-start | bytes 294920 | tf_op jit(solution)/shard_map/ppermute | solution.py:493
  102.1 8.2 %collective-permute-start.5 = (bf16[2,32,192]{2,1,0:T(8,128)(2,1)S(1)}, bf16[2,32,192]{2,1,0:T(8,128)(2,1)S(1)}, u32[]{:S(2)}, u32[]{:S(2)}) collective-permute-start(bf16[2,32,192]{2,1,0:T(8,128)(2,1)S(1)} %get-tuple-element.64), channel_id=1, source_target_pairs={{0,32},{32,64},{64,96},{96,0},{1,33},{33,65},{65,97},{97,1},{2,34}... | collective-permute-start | bytes 73736 | tf_op jit(solution)/shard_map/ppermute | solution.py:498
  102.2 8.2 %collective-permute-start.6 = (bf16[2,32,192]{2,1,0:T(8,128)(2,1)S(1)}, bf16[2,32,192]{2,1,0:T(8,128)(2,1)S(1)}, u32[]{:S(2)}, u32[]{:S(2)}) collective-permute-start(bf16[2,32,192]{2,1,0:T(8,128)(2,1)S(1)} %get-tuple-element.65), channel_id=1, source_target_pairs={{0,64},{32,96},{64,0},{96,32},{1,65},{33,97},{65,1},{97,33},{2,66}... | collective-permute-start | bytes 73736 | tf_op jit(solution)/shard_map/ppermute | solution.py:498
  104.0 6.4 %collective-permute-start.7 = (bf16[2,32,192]{2,1,0:T(8,128)(2,1)S(1)}, bf16[2,32,192]{2,1,0:T(8,128)(2,1)S(1)}, u32[]{:S(2)}, u32[]{:S(2)}) collective-permute-start(bf16[2,32,192]{2,1,0:T(8,128)(2,1)S(1)} %get-tuple-element.66), channel_id=1, source_target_pairs={{0,96},{32,0},{64,32},{96,64},{1,97},{33,1},{65,33},{97,65},{2,98}... | collective-permute-start | bytes 73736 | tf_op jit(solution)/shard_map/ppermute | solution.py:498
  109.6 6.4 %copy-start.21 = (bf16[96,512]{1,0:T(8,128)(2,1)S(1)}, bf16[96,512]{1,0:T(8,128)(2,1)}, u32[]{:S(2)}) copy-start(bf16[96,512]{1,0:T(8,128)(2,1)} %copy-done.20) | copy-start | bytes 294916
  110.4 1.1 copy-start.5
  112.4 17.8 %all-to-all-start.4 = ((bf16[16,4,4864]{2,1,0:T(4,128)(2,1)}), bf16[16,4,4864]{2,1,0:T(4,128)(2,1)S(1)}, u32[]{:S(2)}, u32[]{:S(2)}) async-start(bf16[16,4,4864]{2,1,0:T(4,128)(2,1)} %shard_map.161), calls=%async_computation.5 | async-start | bytes 1245184 | tf_op jit(solution)/shard_map/all_to_all | solution.py:510
  116.0 12.3 %collective-permute-start.1 = (bf16[96,512]{1,0:T(8,128)(2,1)S(1)}, bf16[96,512]{1,0:T(8,128)(2,1)S(1)}, u32[]{:S(2)}, u32[]{:S(2)}) collective-permute-start(bf16[96,512]{1,0:T(8,128)(2,1)S(1)} %copy-done.21), channel_id=1, source_target_pairs={{8,0},{16,8},{24,16},{32,24},{40,32},{48,40},{56,48},{64,56},{72,6... | collective-permute-start | bytes 294920 | tf_op jit(solution)/shard_map/ppermute | solution.py:469
  117.2 12.3 %collective-permute-start.3 = (bf16[96,512]{1,0:T(8,128)(2,1)S(1)}, bf16[96,512]{1,0:T(8,128)(2,1)S(1)}, u32[]{:S(2)}, u32[]{:S(2)}) collective-permute-start(bf16[96,512]{1,0:T(8,128)(2,1)S(1)} %get-tuple-element.59), channel_id=1, source_target_pairs={{8,0},{16,8},{24,16},{32,24},{40,32},{48,40},{56,48},{64,56},{72,6... | collective-permute-start | bytes 294920 | tf_op jit(solution)/shard_map/ppermute | solution.py:508
  (4 other events, 2.6 us)
Sparse Core Ops, SparseCore 0:
  23.4 40.5 all-gather.2
Sparse Core Ops, SparseCore 1:
  75.6 28.0 reduce-scatter.1

commit v3 on v2

--- a/solution.py
+++ b/solution.py
@@ -103,7 +103,7 @@
 
 
 def project_kernel(low_ref, up_ref, gain_ref, w_ref, normed_ref, packed_ref):
-    hidden = jnp.concatenate([low_ref[:HALF], up_ref[...]], axis=0).astype(F32)
+    hidden = jnp.concatenate([low_ref[:HALF], up_ref[:HALF]], axis=0).astype(F32)
     unit, _ = norm_stats(hidden)
     normed = (unit * gain_ref[0:1, :]).astype(BF16)
     normed_ref[0] = normed[:HALF]
@@ -150,8 +150,7 @@
 
 
 def attend_back_kernel(
-    scal_ref, core_ref, x_ref, grad_ref, att_ref, inv_ref, normed_ref, out_ref, mine_ref,
-    other_ref, q_s, k_s, v_s, g_s, gd_s,
+    scal_ref, x_ref, grad_ref, att_ref, inv_ref, out_ref, q_s, k_s, v_s, g_s, gd_s
 ):
     factor = scal_ref[0]
     scale = scal_ref[1]
@@ -207,12 +206,15 @@
     out_ref[:, : 2 * HEAD] = unit_back(dq_pair, query_unit, query_inverse).astype(BF16)
     out_ref[:, 2 * HEAD : 4 * HEAD] = unit_back(dk_pair, key_unit, key_inverse).astype(BF16)
     out_ref[:, 4 * HEAD :] = jnp.where(left, dv[0], dv[1]).astype(BF16)
+
+
+def weight_kernel(core_ref, packed_ref, normed_ref, mine_ref, other_ref):
     product = None
     for a in range(2):
         pieces = []
         for part in range(3):
             start = part * 2 * HEAD + a * HEAD
-            pieces.append(out_ref[:, start : start + HEAD])
+            pieces.append(packed_ref[:, start : start + HEAD])
         normed = jnp.concatenate([normed_ref[i, a] for i in range(8)], axis=0)
         term = dot_tn(normed, jnp.concatenate(pieces, axis=1))
         product = term if product is None else product + term
@@ -278,9 +280,37 @@
         gain_ref[i : i + 1] = row / gains_ref[i : i + 1]
 
 
+def load_all(pairs, sems):
+    loads = [
+        pltpu.make_async_copy(source, target, sems.at[i])
+        for i, (source, target) in enumerate(pairs)
+    ]
+    for load in loads:
+        load.start()
+    return loads
+
+
+def near_kernel(*refs):
+    count = (len(refs) - 1) // 2
+    for load in load_all(tuple(zip(refs[:count], refs[count:-1])), refs[-1]):
+        load.wait()
+
+
 def enter_kernel(
-    field_ref, mask_ref, embed_ref, cot_ref, low_ref, up_ref, cup_ref
+    field_hbm, mask_hbm, embed_hbm, cot_hbm, low_ref, up_ref,
+    field_ref, mask_ref, embed_ref, cot_ref, sems,
 ):
+    loads = load_all(
+        (
+            (mask_hbm, mask_ref),
+            (embed_hbm, embed_ref),
+            (field_hbm, field_ref),
+            (cot_hbm, cot_ref),
+        ),
+        sems,
+    )
+    for load in loads:
+        load.wait()
     sea = embed_ref[0:1].astype(F32)
     land = embed_ref[1:2].astype(F32)
     mask = (mask_ref[...] == 1).astype(F32)
@@ -290,13 +320,12 @@
     for row in range(4):
         column = jnp.sum(jnp.where(eye, mask[row : row + 1], 0.0), axis=1, keepdims=True)
         chosen = jnp.where(column > 0.5, land, sea)
-        hidden_ref, grad_ref = (up_ref, cup_ref) if row < 2 else (low_ref, low_ref)
-        offset = 0 if row < 2 else HALF
+        ref = up_ref if row < 2 else low_ref
         for level in range(3):
             start = (level * 2 + row % 2) * 16
             rows = slice(start, start + 16)
-            hidden_ref[rows] = (field_ref[level, row].astype(F32) + chosen).astype(BF16)
-            grad_ref[offset + start : offset + start + 16] = cot_ref[level, row]
+            ref[rows] = (field_ref[level, row].astype(F32) + chosen).astype(BF16)
+            ref[HALF + start : HALF + start + 16] = cot_ref[level, row]
 
 
 def core_columns(array, width, core):
@@ -307,13 +336,13 @@
 
 
 def middle_kernel(
-    core_ref, att_ref, low_ref, up_ref, cup_ref, gain_ref, w_out_ref, w_up_ref, w_down_ref,
+    core_ref, att_ref, low_ref, up_ref, gain_ref, w_out_ref, w_up_ref, w_down_ref,
     out_low_ref, out_up_ref, packed_ref, gm_ref, send_ref, keep_ref,
 ):
     first = core_ref[0] == 0
     attended = jnp.concatenate([unpack_heads(att_ref, 0), unpack_heads(att_ref, HEAD)], axis=0)
-    hidden = jnp.concatenate([low_ref[:HALF], up_ref[...]], axis=0).astype(F32)
-    cot = jnp.concatenate([low_ref[HALF:], cup_ref[...]], axis=0)
+    hidden = jnp.concatenate([low_ref[:HALF], up_ref[:HALF]], axis=0).astype(F32)
+    cot = jnp.concatenate([low_ref[HALF:], up_ref[HALF:]], axis=0)
     gain = gain_ref[1:2, :]
     mixed = (hidden + dot(attended, w_out_ref[...])).astype(BF16).astype(F32)
     unit, inverse = norm_stats(mixed)
@@ -375,7 +404,7 @@
         parts = [unpack_heads(packed_ref, place * 128 + a * HEAD) for place in range(3)]
         halves.append(jnp.concatenate(parts, axis=1))
     grad_projected = jnp.concatenate(halves, axis=0)
-    hidden = jnp.concatenate([low_ref[:HALF], up_ref[...]], axis=0).astype(F32)
+    hidden = jnp.concatenate([low_ref[:HALF], up_ref[:HALF]], axis=0).astype(F32)
     unit, inverse = norm_stats(hidden)
     grad_normed = dot_nt(grad_projected, w_ref[...])
     grad = gm_ref[...] + norm_back(grad_normed, unit, inverse, gain_ref[0:1, :])
@@ -386,9 +415,10 @@
 
 VMEM = pl.BlockSpec(memory_space=pltpu.VMEM)
 SMEM = pl.BlockSpec(memory_space=pltpu.SMEM)
-
-
-def call(kernel, outs, specs, scratch=(), vmem=12, cost=0):
+ANY = pl.BlockSpec(memory_space=pl.ANY)
+
+
+def call(kernel, outs, specs, scratch=(), vmem=12, cost=3_000_000):
     shapes = tuple(jax.ShapeDtypeStruct(shape, dtype) for shape, dtype in outs)
     return pl.pallas_call(
         kernel,
@@ -413,10 +443,27 @@
     backward = [(j, i) for i, j in forward]
     across = [(0, 1), (1, 0)]
     half = ((HALF, D), BF16)
-    low, up, cot_up = call(enter_kernel, [((OWN, D), BF16), half, half], [VMEM] * 4, cost=20_000_000)(
-        fields, land_sea, surface_embed, cotangent
-    )
+    low, up = call(
+        enter_kernel,
+        [((OWN, D), BF16)] * 2,
+        [ANY] * 4,
+        [
+            pltpu.VMEM((3, 4, 16, D), BF16),
+            pltpu.VMEM((4, 16), jnp.int32),
+            pltpu.VMEM((2, D), BF16),
+            pltpu.VMEM((3, 4, 16, D), BF16),
+            pltpu.SemaphoreType.DMA((4,)),
+        ],
+        vmem=60,
+    )(fields, land_sea, surface_embed, cotangent)
     low = lax.ppermute(low, LAT, forward)
+    w_qkv_near, gains_near = call(
+        near_kernel,
+        [((D, 3 * D), BF16), ((2, D), F32)],
+        [ANY] * 2,
+        [pltpu.SemaphoreType.DMA((2,))],
+    )(w_qkv, norm_gains)
+    low, w_qkv_near, gains_near = lax.optimization_barrier((low, w_qkv_near, gains_near))
 
     scale = head_scales[lon]
     valid = jnp.where(lat == 0, 0.0, 1.0)
@@ -424,7 +471,6 @@
     rows_qkv = lax.dynamic_slice_in_dim(w_qkv, device * 4, 4, axis=0)
     rows_up = lax.dynamic_slice_in_dim(w_up, device * 4, 4, axis=0)
     gains = lax.dynamic_slice_in_dim(norm_gains, device * 4, 4, axis=1)
-    scal, rows_qkv, rows_up, gains = lax.optimization_barrier((scal, rows_qkv, rows_up, gains))
 
     normed, packed = call(
         project_kernel,
@@ -432,9 +478,13 @@
         [VMEM] * 4,
         vmem=12,
         cost=8_000_000,
-    )(low, up, norm_gains, w_qkv)
+    )(low, up, gains_near, w_qkv_near)
+    heads = lax.all_to_all(packed, LON, 0, 0, tiled=True).reshape(ROWS, 384)
+    heads, scal, rows_qkv, rows_up, gains = lax.optimization_barrier(
+        (heads, scal, rows_qkv, rows_up, gains)
+    )
+    heads, normed = lax.optimization_barrier((heads, normed))
     normed_all = lax.all_gather(normed, LON, axis=0, tiled=False)
-    heads = lax.all_to_all(packed, LON, 0, 0, tiled=True).reshape(ROWS, 384)
 
     wide = 2 * ROWS
     att, inv = call(
@@ -461,9 +511,9 @@
             ((OWN, 9 * D), BF16),
             ((OWN, 3 * D), BF16),
         ],
-        [SMEM] + [VMEM] * 8,
+        [SMEM] + [VMEM] * 7,
         vmem=24,
-    )(core, att_rows, low, up, cot_up, norm_gains, w_out, w_up, w_down)
+    )(core, att_rows, low, up, gains_near, w_out, w_up, w_down)
     grad_heads = lax.all_to_all(packed_grad, LON, 0, 0, tiled=True).reshape(ROWS, 128)
     received = lax.ppermute(sent, "c", across)
     out_back = lax.ppermute(out_low, LAT, backward)
@@ -473,10 +523,10 @@
     part = lax.psum_scatter(pair, "x", scatter_dimension=0, tiled=True)
 
     block = ((8, 32, 192), BF16)
-    packed_back, mine, other = call(
+    (packed_back,) = call(
         attend_back_kernel,
-        [((ROWS, 384), BF16), block, block],
-        [SMEM] * 2 + [VMEM] * 5,
+        [((ROWS, 384), BF16)],
+        [SMEM] + [VMEM] * 4,
         [
             pltpu.VMEM((wide, 128), BF16),
             pltpu.VMEM((wide, 128), BF16),
@@ -486,9 +536,13 @@
         ],
         vmem=32,
         cost=1_000_000_000,
-    )(scal, core, heads, grad_heads, att, inv, normed_all)
+    )(scal, heads, grad_heads, att, inv)
+    packed_back, out_back = lax.optimization_barrier((packed_back, out_back))
     grad_packed = lax.all_to_all(
         packed_back.reshape(HEADS, HALF, 384), LON, 0, 0, tiled=True
+    )
+    mine, other = call(weight_kernel, [block] * 2, [SMEM] + [VMEM] * 2)(
+        core, packed_back, normed_all
     )
     theirs = lax.ppermute(other, "c", across)
     blocks = call(pair_kernel, [((2, 32, 192), BF16)] * 4, [SMEM, VMEM, VMEM])(
@@ -502,7 +556,7 @@
         [half] * 2,
         [VMEM] * 6,
         vmem=12,
-    )(grad_packed, low, up, norm_gains, grad_mixed, w_qkv)
+    )(grad_packed, low, up, gains_near, grad_mixed, w_qkv_near)
 
     part, grad_low, grad_up = lax.optimization_barrier((part, grad_low, grad_up))
     grad_back = lax.ppermute(grad_low, LAT, backward)

time: 139 us -> 132 us (0.950)
  blocking collectives: 17.8 us -> 9.46 us
  local copies, waits for them, and re-layouts: 17 us -> 12.7 us
  Pallas kernels: 22.6 us -> 26.8 us
  waiting for transfers between devices: 27 us -> 28.8 us
  starting transfers between devices: 35.4 us -> 33.9 us
    ppermute x1, waiting for transfers between devices: 0.48 us -> 9.19 us  [shards(): grad_back = lax.ppermute(grad_low, LAT, backward)]
    all_to_all x1 -> x0, blocking collectives: 8.45 us -> none  [shards(): lax.all_to_all(packed_grad, LON, 0, 0, tiled=True).reshape(ROWS, 128)]
    ppermute x1, waiting for transfers between devices: 8.27 us -> 0.01 us  [shards(): out_back = lax.ppermute(out_low, LAT, backward)]
    ppermute x1, starting transfers between devices: 9.92 us -> 2.14 us  [shards(): received = lax.ppermute(sent, 'c', across)]
    unnamed x46 -> x26, local copies, waits for them, and re-layouts: 15.6 us -> 9.16 us
    all_to_all x0 -> x1, waiting for transfers between devices: none -> 5.64 us  [shards(): lax.all_to_all(packed_grad, LON, 0, 0, tiled=True).reshape(ROWS, 128)]
    all_to_all x1, waiting for transfers between devices: 4.67 us -> 0.01 us  [shards(): lax.all_to_all(packed_back.reshape(HEADS, HALF, 384), LON, 0, 0, tiled=True)]
    pallas_call x2 -> x4, Pallas kernels: 8.57 us -> 12.1 us  [the longest x1 8.21 us: shards(): call(attend_back_kernel, [((ROWS, 384), BF16)], [SMEM] + [VMEM] * 4, [plt...]
  transfers between devices with their start and end apart: 13 -> 14, of which waited for: 7 -> 7; matrix products, arithmetic and copies ran while one was open for 3% -> 5% of each run, Pallas kernels for 14% -> 17%
where the time goes in v3:
time: 132 us; the launch traced here: 131 us
  starting transfers between devices  33.9 us (26%)
  waiting for transfers between devices  28.8 us (22%)
  Pallas kernels  26.8 us (20%)
  between operations  16.3 us (12%)
  local copies, waits for them, and re-layouts  12.7 us (10%)
  blocking collectives  9.46 us (7%)
  other arithmetic  3.01 us (2%)
    all_to_all x1, blocking collectives, shards(): lax.all_to_all(att.reshape(HEADS, HALF, 128), LON, 0, 0, tiled=True)  9.46 us
    ppermute x1, waiting for transfers between devices, shards(): grad_back = lax.ppermute(grad_low, LAT, backward)  9.19 us
    unnamed x26, local copies, waits for them, and re-layouts  9.16 us
    all_to_all x1, waiting for transfers between devices, shards(): heads = lax.all_to_all(packed, LON, 0, 0, tiled=True).reshape(ROWS, 384)  8.37 us
    pallas_call x1, Pallas kernels, shards(): call(attend_back_kernel, [((ROWS, 384), BF16)], [SMEM] + [VMEM] * 4, [plt...  8.21 us
    all_to_all x1, waiting for transfers between devices, shards(): lax.all_to_all(packed_grad, LON, 0, 0, tiled=True).reshape(ROWS, 128)  5.64 us
    all_to_all x1, starting transfers between devices, shards(): got = lax.all_to_all(joined, ('zh',) + LON, 0, 0, tiled=True)  5.46 us
    ppermute x1, starting transfers between devices, shards(): low = lax.ppermute(low, LAT, forward)  5.06 us
  transfers between devices with their start and end apart: 14, of which 7 were waited for; matrix products, arithmetic and copies ran while one was open for 5% of the time, Pallas kernels for 17%

profile of v3, /device:TPU:1, one launch (start us, length us, event | category | flops | bytes accessed | tf_op | source)
XLA Modules:
  0.0 131.0 jit_solution(3035262606205195114)
XLA Ops:
  8.0 1.9 %shard_map.153 = (bf16[192,512]{1,0:T(8,128)(2,1)}, bf16[192,512]{1,0:T(8,128)(2,1)}) custom-call(bf16[3,4,16,512]{3,2,1,0:T(8,128)(2,1)} %field_hbm.1, s32[4,16]{1,0:T(4,128)} %mask_hbm.1, bf16[2,512]{1,0:T(2,128)(2,1)} %embed_hbm.1, bf16[3,4,16,512]{3,2,1,0:T(8,128)(2,1)} %cot_hbm.1), custom_call_target="tpu_custom_call" | custom-call | bytes 3000000 | tf_op jit(solution)/shard_map/pallas_call | solution.py:446
  9.9 5.1 %collective-permute-start = (bf16[192,512]{1,0:T(8,128)(2,1)}, bf16[192,512]{1,0:T(8,128)(2,1)S(1)}, u32[]{:S(2)}, u32[]{:S(2)}) collective-permute-start(bf16[192,512]{1,0:T(8,128)(2,1)} %get-tuple-element.49), channel_id=1, source_target_pairs={{0,8},{8,16},{16,24},{24,32},{32,40},{40,48},{48,56},{56,64},{64,7... | collective-permute-start | bytes 589832 | tf_op jit(solution)/shard_map/ppermute | solution.py:459
  15.0 1.2 dynamic_slice.12
  16.9 1.4 %copy-done.3 = bf16[512,1536]{1,0:T(8,128)(2,1)S(1)} copy-done((bf16[512,1536]{1,0:T(8,128)(2,1)S(1)}, bf16[512,1536]{1,0:T(8,128)(2,1)}, u32[]{:S(2)}) %copy-start.3) | copy-done | bytes 1572888
  19.9 1.5 %shard_map.155 = (bf16[2,96,512]{2,1,0:T(8,128)(2,1)}, bf16[8,96,384]{2,1,0:T(8,128)(2,1)}) custom-call(bf16[192,512]{1,0:T(8,128)(2,1)S(1)} %collective-permute-done.low_ref, bf16[192,512]{1,0:T(8,128)(2,1)S(1)} %copy-done.2, f32[2,512]{1,0:T(2,128)S(1)} %get-tuple-element.54.gain_ref, bf16[512,1536]{1,0:T(8,128)(2,1)S(1)} %get-tuple-element.55.w_ref), custom_call_target="tpu_custom_call" | custom-call | bytes 8000000 | tf_op jit(solution)/shard_map/pallas_call | solution.py:475
  21.4 4.6 %all-to-all-start = ((bf16[8,96,384]{2,1,0:T(8,128)(2,1)}), bf16[8,96,384]{2,1,0:T(8,128)(2,1)S(1)}, u32[]{:S(2)}, u32[]{:S(2)}) async-start(bf16[8,96,384]{2,1,0:T(8,128)(2,1)} %get-tuple-element.56), calls=%async_computation | async-start | bytes 1179648 | tf_op jit(solution)/shard_map/all_to_all | solution.py:482
  28.4 8.4 %all-to-all-done = bf16[8,96,384]{2,1,0:T(8,128)(2,1)S(1)} async-done(((bf16[8,96,384]{2,1,0:T(8,128)(2,1)}), bf16[8,96,384]{2,1,0:T(8,128)(2,1)S(1)}, u32[]{:S(2)}, u32[]{:S(2)}) %all-to-all-start) | async-done | bytes 589856 | tf_op jit(solution)/shard_map/all_to_all | solution.py:482
  36.8 3.7 %shard_map.156 = (bf16[768,128]{1,0:T(8,128)(2,1)S(1)}, f32[768,128]{1,0:T(8,128)S(1)}) custom-call(f32[3]{0:T(128)S(1)} %pad_maximum_fusion.2.scal_ref, bf16[768,384]{1,0:T(8,128)(2,1)S(1)} %bitcast.12), custom_call_target="tpu_custom_call" | custom-call | bytes 20000000 | tf_op jit(solution)/shard_map/pallas_call | solution.py:490
  40.6 9.5 %all_to_all.25.att_ref = bf16[8,96,128]{2,1,0:T(8,128)(2,1)S(1)} all-to-all(bf16[8,96,128]{2,1,0:T(8,128)(2,1)S(1)} %bitcast.15), channel_id=1, replica_groups=mesh['x'=4,'zh'=2,'c'=2,'zl'=2,'y'=4] {'zl','y'}, dimensions={0} | all-to-all | bytes 393216 | tf_op jit(solution)/shard_map/all_to_all | solution.py:502
  50.1 1.6 %copy-done = bf16[512,2048]{1,0:T(8,128)(2,1)S(1)} copy-done((bf16[512,2048]{1,0:T(8,128)(2,1)S(1)}, bf16[512,2048]{1,0:T(8,128)(2,1)}, u32[]{:S(2)}) %copy-start) | copy-done | bytes 2097176
  51.7 1.6 %copy-done.1 = bf16[2048,512]{1,0:T(8,128)(2,1)S(1)} copy-done((bf16[2048,512]{1,0:T(8,128)(2,1)S(1)}, bf16[2048,512]{1,0:T(8,128)(2,1)}, u32[]{:S(2)}) %copy-start.1) | copy-done | bytes 2097176
  53.3 4.0 %shard_map.157 = (bf16[96,512]{1,0:T(8,128)(2,1)S(1)}, bf16[96,512]{1,0:T(8,128)(2,1)S(1)}, bf16[8,96,128]{2,1,0:T(8,128)(2,1)}, f32[192,512]{1,0:T(8,128)S(1)},...) custom-call(s32[1]{0:T(128)} %bitcast.core_ref, bf16[8,96,128]{2,1,0:T(8,128)(2,1)S(1)} %all_to_all.25.att_ref, ...), custom_call_target="tpu_custom_call" | custom-call | bytes 3000000 | tf_op jit(solution)/shard_map/pallas_call | solution.py:504
  58.7 2.1 %collective-permute-start.2 = (bf16[192,4608]{1,0:T(8,128)(2,1)S(1)}, bf16[192,4608]{1,0:T(8,128)(2,1)S(1)}, u32[]{:S(2)}, u32[]{:S(2)}) collective-permute-start(bf16[192,4608]{1,0:T(8,128)(2,1)S(1)} %get-tuple-element.68.sent_ref), channel_id=1, source_target_pairs={{0,8},{8,0},{1,9},{9,1},{2,10},{10,2},{3,11},{11,3},{4,12},{12,4},... | collective-permute-start | bytes 5308424 | tf_op jit(solution)/shard_map/ppermute | solution.py:518
  60.8 3.3 %collective-permute-done.2.got_ref = bf16[192,4608]{1,0:T(8,128)(2,1)S(1)} collective-permute-done((bf16[192,4608]{1,0:T(8,128)(2,1)S(1)}, bf16[192,4608]{1,0:T(8,128)(2,1)S(1)}, u32[]{:S(2)}, u32[]{:S(2)}) %collective-permute-start.2) | collective-permute-done | bytes 1769504 | tf_op jit(solution)/shard_map/ppermute | solution.py:518
  64.1 2.8 %shard_map.159 = bf16[8,32,4608]{2,1,0:T(8,128)(2,1)} custom-call(bf16[192,1536]{1,0:T(8,128)(2,1)S(1)} %get-tuple-element.67.keep_ref, bf16[192,4608]{1,0:T(8,128)(2,1)S(1)} %get-tuple-element.68.sent_ref, bf16[192,4608]{1,0:T(8,128)(2,1)S(1)} %collective-permute-done.2.got_ref), custom_call_target="tpu_custom_call" | custom-call | bytes 3000000 | tf_op jit(solution)/shard_map/pallas_call | solution.py:520
  67.0 3.5 %all-to-all-start.2 = ((bf16[8,96,128]{2,1,0:T(8,128)(2,1)}), bf16[8,96,128]{2,1,0:T(8,128)(2,1)S(1)}, u32[]{:S(2)}, u32[]{:S(2)}) async-start(bf16[8,96,128]{2,1,0:T(8,128)(2,1)} %get-tuple-element.63), calls=%async_computation.2 | async-start | bytes 393216 | tf_op jit(solution)/shard_map/all_to_all | solution.py:517
  71.3 5.6 %all-to-all-done.2 = bf16[8,96,128]{2,1,0:T(8,128)(2,1)S(1)} async-done(((bf16[8,96,128]{2,1,0:T(8,128)(2,1)}), bf16[8,96,128]{2,1,0:T(8,128)(2,1)S(1)}, u32[]{:S(2)}, u32[]{:S(2)}) %all-to-all-start.2) | async-done | bytes 196640 | tf_op jit(solution)/shard_map/all_to_all | solution.py:517
  76.9 8.2 %shard_map.158.packed_ref = bf16[768,384]{1,0:T(8,128)(2,1)} custom-call(f32[3]{0:T(128)S(1)} %pad_maximum_fusion.2.scal_ref, bf16[768,384]{1,0:T(8,128)(2,1)S(1)} %bitcast.13, bf16[768,128]{1,0:T(8,128)(2,1)S(1)} %bitcast.16, bf16[768,128]{1,0:T(8,128)(2,1)S(1)} %get-tuple-element.61.att_ref, f32[768,128]{1,0:T(8,128)S(1)} %copy-done.8), custom_call_target="tpu_custom_call" | custom-call | bytes 1000000000 | tf_op jit(solution)/shard_map/pallas_call | solution.py:526
  85.1 3.7 %all-to-all-start.3 = ((bf16[8,96,384]{2,1,0:T(8,128)(2,1)}), bf16[8,96,384]{2,1,0:T(8,128)(2,1)S(1)}, u32[]{:S(2)}, u32[]{:S(2)}) async-start(bf16[8,96,384]{2,1,0:T(8,128)(2,1)} %bitcast.7), calls=%async_computation.4 | async-start | bytes 1179648 | tf_op jit(solution)/shard_map/all_to_all | solution.py:541
  88.9 1.4 %copy-done.4 = bf16[16,96,512]{2,1,0:T(8,128)(2,1)S(1)} copy-done((bf16[16,96,512]{2,1,0:T(8,128)(2,1)S(1)}, bf16[16,96,512]{2,1,0:T(8,128)(2,1)}, u32[]{:S(2)}) %copy-start.4) | copy-done | bytes 1572888
  90.3 1.9 %shard_map.161 = (bf16[8,32,192]{2,1,0:T(8,128)(2,1)S(1)}, bf16[8,32,192]{2,1,0:T(8,128)(2,1)S(1)}) custom-call(s32[1]{0:T(128)} %bitcast.core_ref, bf16[768,384]{1,0:T(8,128)(2,1)} %shard_map.158.packed_ref, bf16[8,2,96,512]{3,2,1,0:T(8,128)(2,1)S(1)} %bitcast.14), custom_call_target="tpu_custom_call" | custom-call | bytes 3000000 | tf_op jit(solution)/shard_map/pallas_call | solution.py:544
  92.2 1.7 %collective-permute-start.4 = (bf16[8,32,192]{2,1,0:T(8,128)(2,1)S(1)}, bf16[8,32,192]{2,1,0:T(8,128)(2,1)S(1)}, u32[]{:S(2)}, u32[]{:S(2)}) collective-permute-start(bf16[8,32,192]{2,1,0:T(8,128)(2,1)S(1)} %get-tuple-element.78), channel_id=1, source_target_pairs={{0,8},{8,0},{1,9},{9,1},{2,10},{10,2},{3,11},{11,3},{4,12},{12,4},... | collective-permute-start | bytes 294920 | tf_op jit(solution)/shard_map/ppermute | solution.py:547
  93.9 1.0 collective-permute-done.4.theirs_ref
  94.9 1.5 %collective-permute-start.5 = (bf16[2,32,192]{2,1,0:T(8,128)(2,1)S(1)}, bf16[2,32,192]{2,1,0:T(8,128)(2,1)S(1)}, u32[]{:S(2)}, u32[]{:S(2)}) collective-permute-start(bf16[2,32,192]{2,1,0:T(8,128)(2,1)S(1)} %get-tuple-element.80), channel_id=1, source_target_pairs={{0,32},{32,64},{64,96},{96,0},{1,33},{33,65},{65,97},{97,1},{2,34}... | collective-permute-start | bytes 73736 | tf_op jit(solution)/shard_map/ppermute | solution.py:552
  96.3 2.3 %collective-permute-start.6 = (bf16[2,32,192]{2,1,0:T(8,128)(2,1)S(1)}, bf16[2,32,192]{2,1,0:T(8,128)(2,1)S(1)}, u32[]{:S(2)}, u32[]{:S(2)}) collective-permute-start(bf16[2,32,192]{2,1,0:T(8,128)(2,1)S(1)} %get-tuple-element.81), channel_id=1, source_target_pairs={{0,64},{32,96},{64,0},{96,32},{1,65},{33,97},{65,1},{97,33},{2,66}... | collective-permute-start | bytes 73736 | tf_op jit(solution)/shard_map/ppermute | solution.py:552
  98.7 1.0 collective-permute-start.7
  100.8 0.9 collective-permute-done.7.three_ref
  101.7 1.1 copy-done.5
  103.7 5.5 %all-to-all-start.4 = ((bf16[16,4,4864]{2,1,0:T(4,128)(2,1)}), bf16[16,4,4864]{2,1,0:T(4,128)(2,1)S(1)}, u32[]{:S(2)}, u32[]{:S(2)}) async-start(bf16[16,4,4864]{2,1,0:T(4,128)(2,1)} %shard_map.163), calls=%async_computation.5 | async-start | bytes 1245184 | tf_op jit(solution)/shard_map/all_to_all | solution.py:564
  109.2 2.1 %collective-permute-start.3 = (bf16[96,512]{1,0:T(8,128)(2,1)S(1)}, bf16[96,512]{1,0:T(8,128)(2,1)S(1)}, u32[]{:S(2)}, u32[]{:S(2)}) collective-permute-start(bf16[96,512]{1,0:T(8,128)(2,1)S(1)} %get-tuple-element.74), channel_id=1, source_target_pairs={{8,0},{16,8},{24,16},{32,24},{40,32},{48,40},{56,48},{64,56},{72,6... | collective-permute-start | bytes 294920 | tf_op jit(solution)/shard_map/ppermute | solution.py:562
  111.3 1.6 %pad_maximum_fusion = bf16[3,4,16,512]{3,2,1,0:T(8,128)(2,1)} fusion(bf16[3,2,16,512]{3,2,1,0:T(8,128)(2,1)} %bitcast.6, bf16[3,2,16,512]{3,2,1,0:T(8,128)(2,1)S(1)} %bitcast.17), kind=kLoop, calls=%fused_computation | loop fusion | flops 98304 | bytes 393216 | tf_op jit(solution)/shard_map/concatenate | solution.py:579
  112.9 9.2 %collective-permute-done.3 = bf16[96,512]{1,0:T(8,128)(2,1)S(1)} collective-permute-done((bf16[96,512]{1,0:T(8,128)(2,1)S(1)}, bf16[96,512]{1,0:T(8,128)(2,1)S(1)}, u32[]{:S(2)}, u32[]{:S(2)}) %collective-permute-start.3) | collective-permute-done | bytes 98336 | tf_op jit(solution)/shard_map/ppermute | solution.py:562
  (44 shorter events, 9.6 us)
Async XLA Ops:
  9.9 10.0 %copy-start.2 = (bf16[192,512]{1,0:T(8,128)(2,1)S(1)}, bf16[192,512]{1,0:T(8,128)(2,1)}, u32[]{:S(2)}) copy-start(bf16[192,512]{1,0:T(8,128)(2,1)} %get-tuple-element.53.up_ref) | copy-start | bytes 589828
  9.9 9.9 %collective-permute-start = (bf16[192,512]{1,0:T(8,128)(2,1)}, bf16[192,512]{1,0:T(8,128)(2,1)S(1)}, u32[]{:S(2)}, u32[]{:S(2)}) collective-permute-start(bf16[192,512]{1,0:T(8,128)(2,1)} %get-tuple-element.49), channel_id=1, source_target_pairs={{0,8},{8,16},{16,24},{24,32},{32,40},{40,48},{48,56},{56,64},{64,7... | collective-permute-start | bytes 589832 | tf_op jit(solution)/shard_map/ppermute | solution.py:459
  16.9 1.4 %copy-start.3 = (bf16[512,1536]{1,0:T(8,128)(2,1)S(1)}, bf16[512,1536]{1,0:T(8,128)(2,1)}, u32[]{:S(2)}) copy-start(bf16[512,1536]{1,0:T(8,128)(2,1)} %refs_0_.1) | copy-start | bytes 4718596
  18.3 0.7 copy-start.11
  19.9 30.2 %copy-start.6 = (bf16[512,512]{1,0:T(8,128)(2,1)S(1)}, bf16[512,512]{1,0:T(8,128)(2,1)}, u32[]{:S(2)}) copy-start(bf16[512,512]{1,0:T(8,128)(2,1)} %w_out_ref.1) | copy-start | bytes 1572868
  21.4 15.3 %all-to-all-start = ((bf16[8,96,384]{2,1,0:T(8,128)(2,1)}), bf16[8,96,384]{2,1,0:T(8,128)(2,1)S(1)}, u32[]{:S(2)}, u32[]{:S(2)}) async-start(bf16[8,96,384]{2,1,0:T(8,128)(2,1)} %get-tuple-element.56), calls=%async_computation | async-start | bytes 1179648 | tf_op jit(solution)/shard_map/all_to_all | solution.py:482
  26.1 62.8 %all-gather.3.cloned.1.call-start = ((), (), s32[]{:S(2)}) async-start(), calls=%async_computation.7 | async-start | bytes 1769472 | tf_op jit(solution)/shard_map/all_gather | solution.py:487
  36.8 63.7 %reduce-scatter.2.cloned.1.call-start = ((), (), s32[]{:S(2)}) async-start(), calls=%async_computation.6 | async-start | bytes 2949120 | tf_op jit(solution)/shard_map/reduce_scatter | solution.py:523
  40.6 9.5 %copy-start.7 = (f32[768,128]{1,0:T(8,128)}, f32[768,128]{1,0:T(8,128)S(1)}, u32[]{:S(2)}) copy-start(f32[768,128]{1,0:T(8,128)S(1)} %get-tuple-element.64.inv_ref) | copy-start | bytes 1179652
  50.1 1.6 %copy-start = (bf16[512,2048]{1,0:T(8,128)(2,1)S(1)}, bf16[512,2048]{1,0:T(8,128)(2,1)}, u32[]{:S(2)}) copy-start(bf16[512,2048]{1,0:T(8,128)(2,1)} %w_up_ref.1) | copy-start | bytes 6291460
  51.6 1.6 %copy-start.1 = (bf16[2048,512]{1,0:T(8,128)(2,1)S(1)}, bf16[2048,512]{1,0:T(8,128)(2,1)}, u32[]{:S(2)}) copy-start(bf16[2048,512]{1,0:T(8,128)(2,1)} %w_down_ref.1) | copy-start | bytes 6291460
  57.3 0.7 copy-start.9
  58.1 0.6 copy-start.12
  58.7 5.5 %collective-permute-start.2 = (bf16[192,4608]{1,0:T(8,128)(2,1)S(1)}, bf16[192,4608]{1,0:T(8,128)(2,1)S(1)}, u32[]{:S(2)}, u32[]{:S(2)}) collective-permute-start(bf16[192,4608]{1,0:T(8,128)(2,1)S(1)} %get-tuple-element.68.sent_ref), channel_id=1, source_target_pairs={{0,8},{8,0},{1,9},{9,1},{2,10},{10,2},{3,11},{11,3},{4,12},{12,4},... | collective-permute-start | bytes 5308424 | tf_op jit(solution)/shard_map/ppermute | solution.py:518
  67.0 9.9 %copy-start.8 = (f32[768,128]{1,0:T(8,128)S(1)}, f32[768,128]{1,0:T(8,128)}, u32[]{:S(2)}) copy-start(f32[768,128]{1,0:T(8,128)} %copy-done.7) | copy-start | bytes 1179652
  67.0 9.9 %all-to-all-start.2 = ((bf16[8,96,128]{2,1,0:T(8,128)(2,1)}), bf16[8,96,128]{2,1,0:T(8,128)(2,1)S(1)}, u32[]{:S(2)}, u32[]{:S(2)}) async-start(bf16[8,96,128]{2,1,0:T(8,128)(2,1)} %get-tuple-element.63), calls=%async_computation.2 | async-start | bytes 393216 | tf_op jit(solution)/shard_map/all_to_all | solution.py:517
  70.5 14.6 %collective-permute-start.1 = (bf16[96,512]{1,0:T(8,128)(2,1)}, bf16[96,512]{1,0:T(8,128)(2,1)}, u32[]{:S(2)}, u32[]{:S(2)}) collective-permute-start(bf16[96,512]{1,0:T(8,128)(2,1)} %copy-done.12), channel_id=1, source_target_pairs={{8,0},{16,8},{24,16},{32,24},{40,32},{48,40},{56,48},{64,56},{72,6... | collective-permute-start | bytes 294920 | tf_op jit(solution)/shard_map/ppermute | solution.py:519
  85.1 14.5 %copy-start.10 = (f32[192,512]{1,0:T(8,128)S(1)}, f32[192,512]{1,0:T(8,128)}, u32[]{:S(2)}) copy-start(f32[192,512]{1,0:T(8,128)} %copy-done.9) | copy-start | bytes 1179652
  85.1 14.5 %all-to-all-start.3 = ((bf16[8,96,384]{2,1,0:T(8,128)(2,1)}), bf16[8,96,384]{2,1,0:T(8,128)(2,1)S(1)}, u32[]{:S(2)}, u32[]{:S(2)}) async-start(bf16[8,96,384]{2,1,0:T(8,128)(2,1)} %bitcast.7), calls=%async_computation.4 | async-start | bytes 1179648 | tf_op jit(solution)/shard_map/all_to_all | solution.py:541
  88.8 1.4 %copy-start.4 = (bf16[16,96,512]{2,1,0:T(8,128)(2,1)S(1)}, bf16[16,96,512]{2,1,0:T(8,128)(2,1)}, u32[]{:S(2)}) copy-start(bf16[16,96,512]{2,1,0:T(8,128)(2,1)} %all-gather.3.cloned.1.call-done) | copy-start | bytes 4718596
  92.2 2.7 %collective-permute-start.4 = (bf16[8,32,192]{2,1,0:T(8,128)(2,1)S(1)}, bf16[8,32,192]{2,1,0:T(8,128)(2,1)S(1)}, u32[]{:S(2)}, u32[]{:S(2)}) collective-permute-start(bf16[8,32,192]{2,1,0:T(8,128)(2,1)S(1)} %get-tuple-element.78), channel_id=1, source_target_pairs={{0,8},{8,0},{1,9},{9,1},{2,10},{10,2},{3,11},{11,3},{4,12},{12,4},... | collective-permute-start | bytes 294920 | tf_op jit(solution)/shard_map/ppermute | solution.py:547
  94.9 5.6 %collective-permute-start.5 = (bf16[2,32,192]{2,1,0:T(8,128)(2,1)S(1)}, bf16[2,32,192]{2,1,0:T(8,128)(2,1)S(1)}, u32[]{:S(2)}, u32[]{:S(2)}) collective-permute-start(bf16[2,32,192]{2,1,0:T(8,128)(2,1)S(1)} %get-tuple-element.80), channel_id=1, source_target_pairs={{0,32},{32,64},{64,96},{96,0},{1,33},{33,65},{65,97},{97,1},{2,34}... | collective-permute-start | bytes 73736 | tf_op jit(solution)/shard_map/ppermute | solution.py:552
  96.3 4.4 %collective-permute-start.6 = (bf16[2,32,192]{2,1,0:T(8,128)(2,1)S(1)}, bf16[2,32,192]{2,1,0:T(8,128)(2,1)S(1)}, u32[]{:S(2)}, u32[]{:S(2)}) collective-permute-start(bf16[2,32,192]{2,1,0:T(8,128)(2,1)S(1)} %get-tuple-element.81), channel_id=1, source_target_pairs={{0,64},{32,96},{64,0},{96,32},{1,65},{33,97},{65,1},{97,33},{2,66}... | collective-permute-start | bytes 73736 | tf_op jit(solution)/shard_map/ppermute | solution.py:552
  98.7 3.1 %collective-permute-start.7 = (bf16[2,32,192]{2,1,0:T(8,128)(2,1)S(1)}, bf16[2,32,192]{2,1,0:T(8,128)(2,1)S(1)}, u32[]{:S(2)}, u32[]{:S(2)}) collective-permute-start(bf16[2,32,192]{2,1,0:T(8,128)(2,1)S(1)} %get-tuple-element.82), channel_id=1, source_target_pairs={{0,96},{32,0},{64,32},{96,64},{1,97},{33,1},{65,33},{97,65},{2,98}... | collective-permute-start | bytes 73736 | tf_op jit(solution)/shard_map/ppermute | solution.py:552
  101.7 1.1 copy-start.5
  103.7 19.1 %all-to-all-start.4 = ((bf16[16,4,4864]{2,1,0:T(4,128)(2,1)}), bf16[16,4,4864]{2,1,0:T(4,128)(2,1)S(1)}, u32[]{:S(2)}, u32[]{:S(2)}) async-start(bf16[16,4,4864]{2,1,0:T(4,128)(2,1)} %shard_map.163), calls=%async_computation.5 | async-start | bytes 1245184 | tf_op jit(solution)/shard_map/all_to_all | solution.py:564
  109.2 12.9 %collective-permute-start.3 = (bf16[96,512]{1,0:T(8,128)(2,1)S(1)}, bf16[96,512]{1,0:T(8,128)(2,1)S(1)}, u32[]{:S(2)}, u32[]{:S(2)}) collective-permute-start(bf16[96,512]{1,0:T(8,128)(2,1)S(1)} %get-tuple-element.74), channel_id=1, source_target_pairs={{8,0},{16,8},{24,16},{32,24},{40,32},{48,40},{56,48},{64,56},{72,6... | collective-permute-start | bytes 294920 | tf_op jit(solution)/shard_map/ppermute | solution.py:562
Sparse Core Ops, SparseCore 0:
  36.9 35.0 all-gather.2
Sparse Core Ops, SparseCore 1:
  67.1 29.8 reduce-scatter.1

commit v4 on v3

--- a/solution.py
+++ b/solution.py
@@ -558,7 +558,6 @@
         vmem=12,
     )(grad_packed, low, up, gains_near, grad_mixed, w_qkv_near)
 
-    part, grad_low, grad_up = lax.optimization_barrier((part, grad_low, grad_up))
     grad_back = lax.ppermute(grad_low, LAT, backward)
     (joined,) = call(join_kernel, [((16, 4, 9 * D + 256), BF16)], [VMEM] * 5)(part, *blocks)
     got = lax.all_to_all(joined, ("zh",) + LON, 0, 0, tiled=True)

time: 132 us -> 131 us (level)
  waiting for transfers between devices: 28.8 us -> 26.1 us
  starting transfers between devices: 33.9 us -> 36.1 us
    ppermute x1, starting transfers between devices: 2.14 us -> 4.69 us  [shards(): received = lax.ppermute(sent, 'c', across)]
    all_to_all x1, waiting for transfers between devices: 8.37 us -> 6.38 us  [shards(): heads = lax.all_to_all(packed, LON, 0, 0, tiled=True).reshape(ROWS, 384)]
    ppermute x1, waiting for transfers between devices: 9.19 us -> 7.4 us  [shards(): grad_back = lax.ppermute(grad_low, LAT, backward)]
    unnamed x26 -> x28, local copies, waits for them, and re-layouts: 9.16 us -> 10.2 us
where the time goes in v4:
time: 131 us; the launch traced here: 130 us
  starting transfers between devices  36.1 us (28%)
  Pallas kernels  26.8 us (20%)
  waiting for transfers between devices  26.1 us (20%)
  between operations  16.3 us (12%)
  local copies, waits for them, and re-layouts  13 us (10%)
  blocking collectives  8.79 us (7%)
  other arithmetic  3.01 us (2%)
    unnamed x28, local copies, waits for them, and re-layouts  10.2 us
    all_to_all x1, blocking collectives, shards(): lax.all_to_all(att.reshape(HEADS, HALF, 128), LON, 0, 0, tiled=True)  8.79 us
    pallas_call x1, Pallas kernels, shards(): call(attend_back_kernel, [((ROWS, 384), BF16)], [SMEM] + [VMEM] * 4, [plt...  8.23 us
    ppermute x1, waiting for transfers between devices, shards(): grad_back = lax.ppermute(grad_low, LAT, backward)  7.4 us
    all_to_all x1, waiting for transfers between devices, shards(): heads = lax.all_to_all(packed, LON, 0, 0, tiled=True).reshape(ROWS, 384)  6.38 us
    all_to_all x1, waiting for transfers between devices, shards(): lax.all_to_all(packed_grad, LON, 0, 0, tiled=True).reshape(ROWS, 128)  5.96 us
    all_to_all x1, starting transfers between devices, shards(): got = lax.all_to_all(joined, ('zh',) + LON, 0, 0, tiled=True)  5.44 us
    ppermute x3, starting transfers between devices, shards(): lax.ppermute(blocks[k], 'x', [(i, (i + k) % 4) for i in range(4)])  5.06 us
  transfers between devices with their start and end apart: 14, of which 7 were waited for; matrix products, arithmetic and copies ran while one was open for 5% of the time, Pallas kernels for 17%

profile of v4, /device:TPU:1, one launch (start us, length us, event | category | flops | bytes accessed | tf_op | source)
XLA Modules:
  0.0 130.2 jit_solution(12920067620710156337)
XLA Ops:
  8.0 1.9 %shard_map.153 = (bf16[192,512]{1,0:T(8,128)(2,1)}, bf16[192,512]{1,0:T(8,128)(2,1)}) custom-call(bf16[3,4,16,512]{3,2,1,0:T(8,128)(2,1)} %field_hbm.1, s32[4,16]{1,0:T(4,128)} %mask_hbm.1, bf16[2,512]{1,0:T(2,128)(2,1)} %embed_hbm.1, bf16[3,4,16,512]{3,2,1,0:T(8,128)(2,1)} %cot_hbm.1), custom_call_target="tpu_custom_call" | custom-call | bytes 3000000 | tf_op jit(solution)/shard_map/pallas_call | solution.py:446
  10.0 5.1 %collective-permute-start = (bf16[192,512]{1,0:T(8,128)(2,1)}, bf16[192,512]{1,0:T(8,128)(2,1)S(1)}, u32[]{:S(2)}, u32[]{:S(2)}) collective-permute-start(bf16[192,512]{1,0:T(8,128)(2,1)} %get-tuple-element.46), channel_id=1, source_target_pairs={{0,8},{8,16},{16,24},{24,32},{32,40},{40,48},{48,56},{56,64},{64,7... | collective-permute-start | bytes 589832 | tf_op jit(solution)/shard_map/ppermute | solution.py:459
  15.0 1.4 %copy-done.3 = bf16[512,1536]{1,0:T(8,128)(2,1)S(1)} copy-done((bf16[512,1536]{1,0:T(8,128)(2,1)S(1)}, bf16[512,1536]{1,0:T(8,128)(2,1)}, u32[]{:S(2)}) %copy-start.3) | copy-done | bytes 1572888
  19.3 1.6 %shard_map.155 = (bf16[2,96,512]{2,1,0:T(8,128)(2,1)}, bf16[8,96,384]{2,1,0:T(8,128)(2,1)}) custom-call(bf16[192,512]{1,0:T(8,128)(2,1)S(1)} %collective-permute-done.low_ref, bf16[192,512]{1,0:T(8,128)(2,1)S(1)} %copy-done.2, f32[2,512]{1,0:T(2,128)S(1)} %get-tuple-element.51.gain_ref, bf16[512,1536]{1,0:T(8,128)(2,1)S(1)} %get-tuple-element.52.w_ref), custom_call_target="tpu_custom_call" | custom-call | bytes 8000000 | tf_op jit(solution)/shard_map/pallas_call | solution.py:475
  20.8 4.7 %all-to-all-start = ((bf16[8,96,384]{2,1,0:T(8,128)(2,1)}), bf16[8,96,384]{2,1,0:T(8,128)(2,1)S(1)}, u32[]{:S(2)}, u32[]{:S(2)}) async-start(bf16[8,96,384]{2,1,0:T(8,128)(2,1)} %get-tuple-element.53), calls=%async_computation | async-start | bytes 1179648 | tf_op jit(solution)/shard_map/all_to_all | solution.py:482
  27.8 6.4 %all-to-all-done = bf16[8,96,384]{2,1,0:T(8,128)(2,1)S(1)} async-done(((bf16[8,96,384]{2,1,0:T(8,128)(2,1)}), bf16[8,96,384]{2,1,0:T(8,128)(2,1)S(1)}, u32[]{:S(2)}, u32[]{:S(2)}) %all-to-all-start) | async-done | bytes 589856 | tf_op jit(solution)/shard_map/all_to_all | solution.py:482
  34.2 3.8 %shard_map.156 = (bf16[768,128]{1,0:T(8,128)(2,1)S(1)}, f32[768,128]{1,0:T(8,128)S(1)}) custom-call(f32[3]{0:T(128)S(1)} %pad_maximum_fusion.2.scal_ref, bf16[768,384]{1,0:T(8,128)(2,1)S(1)} %bitcast.12), custom_call_target="tpu_custom_call" | custom-call | bytes 20000000 | tf_op jit(solution)/shard_map/pallas_call | solution.py:490
  38.0 8.8 %all_to_all.25.att_ref = bf16[8,96,128]{2,1,0:T(8,128)(2,1)S(1)} all-to-all(bf16[8,96,128]{2,1,0:T(8,128)(2,1)S(1)} %bitcast.15), channel_id=1, replica_groups=mesh['x'=4,'zh'=2,'c'=2,'zl'=2,'y'=4] {'zl','y'}, dimensions={0} | all-to-all | bytes 393216 | tf_op jit(solution)/shard_map/all_to_all | solution.py:502
  46.8 1.6 %copy-done = bf16[512,2048]{1,0:T(8,128)(2,1)S(1)} copy-done((bf16[512,2048]{1,0:T(8,128)(2,1)S(1)}, bf16[512,2048]{1,0:T(8,128)(2,1)}, u32[]{:S(2)}) %copy-start) | copy-done | bytes 2097176
  48.4 1.6 %copy-done.1 = bf16[2048,512]{1,0:T(8,128)(2,1)S(1)} copy-done((bf16[2048,512]{1,0:T(8,128)(2,1)S(1)}, bf16[2048,512]{1,0:T(8,128)(2,1)}, u32[]{:S(2)}) %copy-start.1) | copy-done | bytes 2097176
  50.0 4.0 %shard_map.157 = (bf16[96,512]{1,0:T(8,128)(2,1)S(1)}, bf16[96,512]{1,0:T(8,128)(2,1)S(1)}, bf16[8,96,128]{2,1,0:T(8,128)(2,1)}, f32[192,512]{1,0:T(8,128)S(1)},...) custom-call(s32[1]{0:T(128)} %bitcast.core_ref, bf16[8,96,128]{2,1,0:T(8,128)(2,1)S(1)} %all_to_all.25.att_ref, ...), custom_call_target="tpu_custom_call" | custom-call | bytes 3000000 | tf_op jit(solution)/shard_map/pallas_call | solution.py:504
  55.4 4.7 %collective-permute-start.3 = (bf16[192,4608]{1,0:T(8,128)(2,1)S(1)}, bf16[192,4608]{1,0:T(8,128)(2,1)S(1)}, u32[]{:S(2)}, u32[]{:S(2)}) collective-permute-start(bf16[192,4608]{1,0:T(8,128)(2,1)S(1)} %get-tuple-element.69.sent_ref), channel_id=1, source_target_pairs={{0,8},{8,0},{1,9},{9,1},{2,10},{10,2},{3,11},{11,3},{4,12},{12,4},... | collective-permute-start | bytes 5308424 | tf_op jit(solution)/shard_map/ppermute | solution.py:518
  60.1 3.3 %collective-permute-done.3.got_ref = bf16[192,4608]{1,0:T(8,128)(2,1)S(1)} collective-permute-done((bf16[192,4608]{1,0:T(8,128)(2,1)S(1)}, bf16[192,4608]{1,0:T(8,128)(2,1)S(1)}, u32[]{:S(2)}, u32[]{:S(2)}) %collective-permute-start.3) | collective-permute-done | bytes 1769504 | tf_op jit(solution)/shard_map/ppermute | solution.py:518
  63.4 2.8 %shard_map.160 = bf16[8,32,4608]{2,1,0:T(8,128)(2,1)} custom-call(bf16[192,1536]{1,0:T(8,128)(2,1)S(1)} %get-tuple-element.68.keep_ref, bf16[192,4608]{1,0:T(8,128)(2,1)S(1)} %get-tuple-element.69.sent_ref, bf16[192,4608]{1,0:T(8,128)(2,1)S(1)} %collective-permute-done.3.got_ref), custom_call_target="tpu_custom_call" | custom-call | bytes 3000000 | tf_op jit(solution)/shard_map/pallas_call | solution.py:520
  66.3 3.5 %all-to-all-start.2 = ((bf16[8,96,128]{2,1,0:T(8,128)(2,1)}), bf16[8,96,128]{2,1,0:T(8,128)(2,1)S(1)}, u32[]{:S(2)}, u32[]{:S(2)}) async-start(bf16[8,96,128]{2,1,0:T(8,128)(2,1)} %get-tuple-element.60), calls=%async_computation.2 | async-start | bytes 393216 | tf_op jit(solution)/shard_map/all_to_all | solution.py:517
  70.5 6.0 %all-to-all-done.2 = bf16[8,96,128]{2,1,0:T(8,128)(2,1)S(1)} async-done(((bf16[8,96,128]{2,1,0:T(8,128)(2,1)}), bf16[8,96,128]{2,1,0:T(8,128)(2,1)S(1)}, u32[]{:S(2)}, u32[]{:S(2)}) %all-to-all-start.2) | async-done | bytes 196640 | tf_op jit(solution)/shard_map/all_to_all | solution.py:517
  76.4 8.2 %shard_map.158.packed_ref = bf16[768,384]{1,0:T(8,128)(2,1)} custom-call(f32[3]{0:T(128)S(1)} %pad_maximum_fusion.2.scal_ref, bf16[768,384]{1,0:T(8,128)(2,1)S(1)} %bitcast.13, bf16[768,128]{1,0:T(8,128)(2,1)S(1)} %bitcast.16, bf16[768,128]{1,0:T(8,128)(2,1)S(1)} %get-tuple-element.58.att_ref, f32[768,128]{1,0:T(8,128)S(1)} %copy-done.8), custom_call_target="tpu_custom_call" | custom-call | bytes 1000000000 | tf_op jit(solution)/shard_map/pallas_call | solution.py:526
  84.7 3.5 %all-to-all-start.3 = ((bf16[8,96,384]{2,1,0:T(8,128)(2,1)}), bf16[8,96,384]{2,1,0:T(8,128)(2,1)S(1)}, u32[]{:S(2)}, u32[]{:S(2)}) async-start(bf16[8,96,384]{2,1,0:T(8,128)(2,1)} %bitcast.7), calls=%async_computation.3 | async-start | bytes 1179648 | tf_op jit(solution)/shard_map/all_to_all | solution.py:541
  88.3 1.4 %copy-done.4 = bf16[16,96,512]{2,1,0:T(8,128)(2,1)S(1)} copy-done((bf16[16,96,512]{2,1,0:T(8,128)(2,1)S(1)}, bf16[16,96,512]{2,1,0:T(8,128)(2,1)}, u32[]{:S(2)}) %copy-start.4) | copy-done | bytes 1572888
  89.7 1.9 %shard_map.161 = (bf16[8,32,192]{2,1,0:T(8,128)(2,1)S(1)}, bf16[8,32,192]{2,1,0:T(8,128)(2,1)S(1)}) custom-call(s32[1]{0:T(128)} %bitcast.core_ref, bf16[768,384]{1,0:T(8,128)(2,1)} %shard_map.158.packed_ref, bf16[8,2,96,512]{3,2,1,0:T(8,128)(2,1)S(1)} %bitcast.14), custom_call_target="tpu_custom_call" | custom-call | bytes 3000000 | tf_op jit(solution)/shard_map/pallas_call | solution.py:544
  91.6 1.3 %collective-permute-start.4 = (bf16[8,32,192]{2,1,0:T(8,128)(2,1)S(1)}, bf16[8,32,192]{2,1,0:T(8,128)(2,1)S(1)}, u32[]{:S(2)}, u32[]{:S(2)}) collective-permute-start(bf16[8,32,192]{2,1,0:T(8,128)(2,1)S(1)} %get-tuple-element.72), channel_id=1, source_target_pairs={{0,8},{8,0},{1,9},{9,1},{2,10},{10,2},{3,11},{11,3},{4,12},{12,4},... | collective-permute-start | bytes 294920 | tf_op jit(solution)/shard_map/ppermute | solution.py:547
  92.9 1.0 collective-permute-done.4.theirs_ref
  93.9 1.6 %collective-permute-start.5 = (bf16[2,32,192]{2,1,0:T(8,128)(2,1)S(1)}, bf16[2,32,192]{2,1,0:T(8,128)(2,1)S(1)}, u32[]{:S(2)}, u32[]{:S(2)}) collective-permute-start(bf16[2,32,192]{2,1,0:T(8,128)(2,1)S(1)} %get-tuple-element.74), channel_id=1, source_target_pairs={{0,32},{32,64},{64,96},{96,0},{1,33},{33,65},{65,97},{97,1},{2,34}... | collective-permute-start | bytes 73736 | tf_op jit(solution)/shard_map/ppermute | solution.py:552
  95.5 2.4 %collective-permute-start.6 = (bf16[2,32,192]{2,1,0:T(8,128)(2,1)S(1)}, bf16[2,32,192]{2,1,0:T(8,128)(2,1)S(1)}, u32[]{:S(2)}, u32[]{:S(2)}) collective-permute-start(bf16[2,32,192]{2,1,0:T(8,128)(2,1)S(1)} %get-tuple-element.75), channel_id=1, source_target_pairs={{0,64},{32,96},{64,0},{96,32},{1,65},{33,97},{65,1},{97,33},{2,66}... | collective-permute-start | bytes 73736 | tf_op jit(solution)/shard_map/ppermute | solution.py:552
  97.9 1.0 collective-permute-start.7
  99.8 1.2 collective-permute-done.7.three_ref
  101.0 1.1 copy-done.5
  103.0 5.4 %all-to-all-start.4 = ((bf16[16,4,4864]{2,1,0:T(4,128)(2,1)}), bf16[16,4,4864]{2,1,0:T(4,128)(2,1)S(1)}, u32[]{:S(2)}, u32[]{:S(2)}) async-start(bf16[16,4,4864]{2,1,0:T(4,128)(2,1)} %shard_map.163), calls=%async_computation.5 | async-start | bytes 1245184 | tf_op jit(solution)/shard_map/all_to_all | solution.py:563
  108.4 1.0 copy-done.10
  110.2 2.1 %collective-permute-start.2 = (bf16[96,512]{1,0:T(8,128)(2,1)S(1)}, bf16[96,512]{1,0:T(8,128)(2,1)S(1)}, u32[]{:S(2)}, u32[]{:S(2)}) collective-permute-start(bf16[96,512]{1,0:T(8,128)(2,1)S(1)} %get-tuple-element.67), channel_id=1, source_target_pairs={{8,0},{16,8},{24,16},{32,24},{40,32},{48,40},{56,48},{64,56},{72,6... | collective-permute-start | bytes 294920 | tf_op jit(solution)/shard_map/ppermute | solution.py:561
  112.3 1.6 %pad_maximum_fusion = bf16[3,4,16,512]{3,2,1,0:T(8,128)(2,1)} fusion(bf16[3,2,16,512]{3,2,1,0:T(8,128)(2,1)} %bitcast.6, bf16[3,2,16,512]{3,2,1,0:T(8,128)(2,1)S(1)} %bitcast.17), kind=kLoop, calls=%fused_computation | loop fusion | flops 98304 | bytes 393216 | tf_op jit(solution)/shard_map/concatenate | solution.py:578
  113.9 7.4 %collective-permute-done.2 = bf16[96,512]{1,0:T(8,128)(2,1)S(1)} collective-permute-done((bf16[96,512]{1,0:T(8,128)(2,1)S(1)}, bf16[96,512]{1,0:T(8,128)(2,1)S(1)}, u32[]{:S(2)}, u32[]{:S(2)}) %collective-permute-start.2) | collective-permute-done | bytes 98336 | tf_op jit(solution)/shard_map/ppermute | solution.py:561
  (46 shorter events, 10.6 us)
Async XLA Ops:
  8.0 9.2 %copy-start.13 = (f32[8]{0:T(128)S(1)}, f32[8]{0:T(128)}, u32[]{:S(2)}) copy-start(f32[8]{0:T(128)} %param.15) | copy-start | bytes 100
  9.9 9.3 %copy-start.2 = (bf16[192,512]{1,0:T(8,128)(2,1)S(1)}, bf16[192,512]{1,0:T(8,128)(2,1)}, u32[]{:S(2)}) copy-start(bf16[192,512]{1,0:T(8,128)(2,1)} %get-tuple-element.50.up_ref) | copy-start | bytes 589828
  10.0 9.3 %collective-permute-start = (bf16[192,512]{1,0:T(8,128)(2,1)}, bf16[192,512]{1,0:T(8,128)(2,1)S(1)}, u32[]{:S(2)}, u32[]{:S(2)}) collective-permute-start(bf16[192,512]{1,0:T(8,128)(2,1)} %get-tuple-element.46), channel_id=1, source_target_pairs={{0,8},{8,16},{16,24},{24,32},{32,40},{40,48},{48,56},{56,64},{64,7... | collective-permute-start | bytes 589832 | tf_op jit(solution)/shard_map/ppermute | solution.py:459
  15.0 1.4 %copy-start.3 = (bf16[512,1536]{1,0:T(8,128)(2,1)S(1)}, bf16[512,1536]{1,0:T(8,128)(2,1)}, u32[]{:S(2)}) copy-start(bf16[512,1536]{1,0:T(8,128)(2,1)} %refs_0_.1) | copy-start | bytes 4718596
  16.4 0.7 copy-start.11
  19.3 27.5 %copy-start.6 = (bf16[512,512]{1,0:T(8,128)(2,1)S(1)}, bf16[512,512]{1,0:T(8,128)(2,1)}, u32[]{:S(2)}) copy-start(bf16[512,512]{1,0:T(8,128)(2,1)} %w_out_ref.1) | copy-start | bytes 1572868
  20.8 13.3 %all-to-all-start = ((bf16[8,96,384]{2,1,0:T(8,128)(2,1)}), bf16[8,96,384]{2,1,0:T(8,128)(2,1)S(1)}, u32[]{:S(2)}, u32[]{:S(2)}) async-start(bf16[8,96,384]{2,1,0:T(8,128)(2,1)} %get-tuple-element.53), calls=%async_computation | async-start | bytes 1179648 | tf_op jit(solution)/shard_map/all_to_all | solution.py:482
  25.5 62.7 %all-gather.3.cloned.1.call-start = ((), (), s32[]{:S(2)}) async-start(), calls=%async_computation.7 | async-start | bytes 1769472 | tf_op jit(solution)/shard_map/all_gather | solution.py:487
  34.2 66.8 %reduce-scatter.2.cloned.1.call-start = ((), (), s32[]{:S(2)}) async-start(), calls=%async_computation.6 | async-start | bytes 2949120 | tf_op jit(solution)/shard_map/reduce_scatter | solution.py:523
  38.0 8.8 %copy-start.7 = (f32[768,128]{1,0:T(8,128)}, f32[768,128]{1,0:T(8,128)S(1)}, u32[]{:S(2)}) copy-start(f32[768,128]{1,0:T(8,128)S(1)} %get-tuple-element.61.inv_ref) | copy-start | bytes 1179652
  46.8 1.6 %copy-start = (bf16[512,2048]{1,0:T(8,128)(2,1)S(1)}, bf16[512,2048]{1,0:T(8,128)(2,1)}, u32[]{:S(2)}) copy-start(bf16[512,2048]{1,0:T(8,128)(2,1)} %w_up_ref.1) | copy-start | bytes 6291460
  48.4 1.6 %copy-start.1 = (bf16[2048,512]{1,0:T(8,128)(2,1)S(1)}, bf16[2048,512]{1,0:T(8,128)(2,1)}, u32[]{:S(2)}) copy-start(bf16[2048,512]{1,0:T(8,128)(2,1)} %w_down_ref.1) | copy-start | bytes 6291460
  54.0 0.8 copy-start.9
  54.8 0.6 copy-start.12
  55.4 8.0 %collective-permute-start.3 = (bf16[192,4608]{1,0:T(8,128)(2,1)S(1)}, bf16[192,4608]{1,0:T(8,128)(2,1)S(1)}, u32[]{:S(2)}, u32[]{:S(2)}) collective-permute-start(bf16[192,4608]{1,0:T(8,128)(2,1)S(1)} %get-tuple-element.69.sent_ref), channel_id=1, source_target_pairs={{0,8},{8,0},{1,9},{9,1},{2,10},{10,2},{3,11},{11,3},{4,12},{12,4},... | collective-permute-start | bytes 5308424 | tf_op jit(solution)/shard_map/ppermute | solution.py:518
  66.3 10.2 %copy-start.8 = (f32[768,128]{1,0:T(8,128)S(1)}, f32[768,128]{1,0:T(8,128)}, u32[]{:S(2)}) copy-start(f32[768,128]{1,0:T(8,128)} %copy-done.7) | copy-start | bytes 1179652
  66.3 10.1 %all-to-all-start.2 = ((bf16[8,96,128]{2,1,0:T(8,128)(2,1)}), bf16[8,96,128]{2,1,0:T(8,128)(2,1)S(1)}, u32[]{:S(2)}, u32[]{:S(2)}) async-start(bf16[8,96,128]{2,1,0:T(8,128)(2,1)} %get-tuple-element.60), calls=%async_computation.2 | async-start | bytes 393216 | tf_op jit(solution)/shard_map/all_to_all | solution.py:517
  69.8 14.8 %collective-permute-start.1 = (bf16[96,512]{1,0:T(8,128)(2,1)}, bf16[96,512]{1,0:T(8,128)(2,1)}, u32[]{:S(2)}, u32[]{:S(2)}) collective-permute-start(bf16[96,512]{1,0:T(8,128)(2,1)} %copy-done.12), channel_id=1, source_target_pairs={{8,0},{16,8},{24,16},{32,24},{40,32},{48,40},{56,48},{64,56},{72,6... | collective-permute-start | bytes 294920 | tf_op jit(solution)/shard_map/ppermute | solution.py:519
  84.7 18.3 %all-to-all-start.3 = ((bf16[8,96,384]{2,1,0:T(8,128)(2,1)}), bf16[8,96,384]{2,1,0:T(8,128)(2,1)S(1)}, u32[]{:S(2)}, u32[]{:S(2)}) async-start(bf16[8,96,384]{2,1,0:T(8,128)(2,1)} %bitcast.7), calls=%async_computation.3 | async-start | bytes 1179648 | tf_op jit(solution)/shard_map/all_to_all | solution.py:541
  88.2 1.4 %copy-start.4 = (bf16[16,96,512]{2,1,0:T(8,128)(2,1)S(1)}, bf16[16,96,512]{2,1,0:T(8,128)(2,1)}, u32[]{:S(2)}) copy-start(bf16[16,96,512]{2,1,0:T(8,128)(2,1)} %all-gather.3.cloned.1.call-done) | copy-start | bytes 4718596
  91.6 2.3 %collective-permute-start.4 = (bf16[8,32,192]{2,1,0:T(8,128)(2,1)S(1)}, bf16[8,32,192]{2,1,0:T(8,128)(2,1)S(1)}, u32[]{:S(2)}, u32[]{:S(2)}) collective-permute-start(bf16[8,32,192]{2,1,0:T(8,128)(2,1)S(1)} %get-tuple-element.72), channel_id=1, source_target_pairs={{0,8},{8,0},{1,9},{9,1},{2,10},{10,2},{3,11},{11,3},{4,12},{12,4},... | collective-permute-start | bytes 294920 | tf_op jit(solution)/shard_map/ppermute | solution.py:547
  93.9 5.1 %collective-permute-start.5 = (bf16[2,32,192]{2,1,0:T(8,128)(2,1)S(1)}, bf16[2,32,192]{2,1,0:T(8,128)(2,1)S(1)}, u32[]{:S(2)}, u32[]{:S(2)}) collective-permute-start(bf16[2,32,192]{2,1,0:T(8,128)(2,1)S(1)} %get-tuple-element.74), channel_id=1, source_target_pairs={{0,32},{32,64},{64,96},{96,0},{1,33},{33,65},{65,97},{97,1},{2,34}... | collective-permute-start | bytes 73736 | tf_op jit(solution)/shard_map/ppermute | solution.py:552
  95.5 4.3 %collective-permute-start.6 = (bf16[2,32,192]{2,1,0:T(8,128)(2,1)S(1)}, bf16[2,32,192]{2,1,0:T(8,128)(2,1)S(1)}, u32[]{:S(2)}, u32[]{:S(2)}) collective-permute-start(bf16[2,32,192]{2,1,0:T(8,128)(2,1)S(1)} %get-tuple-element.75), channel_id=1, source_target_pairs={{0,64},{32,96},{64,0},{96,32},{1,65},{33,97},{65,1},{97,33},{2,66}... | collective-permute-start | bytes 73736 | tf_op jit(solution)/shard_map/ppermute | solution.py:552
  97.9 3.1 %collective-permute-start.7 = (bf16[2,32,192]{2,1,0:T(8,128)(2,1)S(1)}, bf16[2,32,192]{2,1,0:T(8,128)(2,1)S(1)}, u32[]{:S(2)}, u32[]{:S(2)}) collective-permute-start(bf16[2,32,192]{2,1,0:T(8,128)(2,1)S(1)} %get-tuple-element.76), channel_id=1, source_target_pairs={{0,96},{32,0},{64,32},{96,64},{1,97},{33,1},{65,33},{97,65},{2,98}... | collective-permute-start | bytes 73736 | tf_op jit(solution)/shard_map/ppermute | solution.py:552
  101.0 1.1 copy-start.5
  103.0 19.1 %all-to-all-start.4 = ((bf16[16,4,4864]{2,1,0:T(4,128)(2,1)}), bf16[16,4,4864]{2,1,0:T(4,128)(2,1)S(1)}, u32[]{:S(2)}, u32[]{:S(2)}) async-start(bf16[16,4,4864]{2,1,0:T(4,128)(2,1)} %shard_map.163), calls=%async_computation.5 | async-start | bytes 1245184 | tf_op jit(solution)/shard_map/all_to_all | solution.py:563
  108.4 1.0 copy-start.10
  110.2 11.1 %collective-permute-start.2 = (bf16[96,512]{1,0:T(8,128)(2,1)S(1)}, bf16[96,512]{1,0:T(8,128)(2,1)S(1)}, u32[]{:S(2)}, u32[]{:S(2)}) collective-permute-start(bf16[96,512]{1,0:T(8,128)(2,1)S(1)} %get-tuple-element.67), channel_id=1, source_target_pairs={{8,0},{16,8},{24,16},{32,24},{40,32},{48,40},{56,48},{64,56},{72,6... | collective-permute-start | bytes 294920 | tf_op jit(solution)/shard_map/ppermute | solution.py:561
Sparse Core Ops, SparseCore 0:
  34.3 35.6 all-gather.2
Sparse Core Ops, SparseCore 1:
  66.4 29.9 reduce-scatter.1

commit v5 on v4

--- a/solution.py
+++ b/solution.py
@@ -483,9 +483,6 @@
     heads, scal, rows_qkv, rows_up, gains = lax.optimization_barrier(
         (heads, scal, rows_qkv, rows_up, gains)
     )
-    heads, normed = lax.optimization_barrier((heads, normed))
-    normed_all = lax.all_gather(normed, LON, axis=0, tiled=False)
-
     wide = 2 * ROWS
     att, inv = call(
         attend_kernel,
@@ -499,6 +496,8 @@
         vmem=20,
         cost=20_000_000,
     )(scal, heads)
+    att, normed = lax.optimization_barrier((att, normed))
+    normed_all = lax.all_gather(normed, LON, axis=0, tiled=False)
     att_rows = lax.all_to_all(att.reshape(HEADS, HALF, 128), LON, 0, 0, tiled=True)
 
     out_low, out_up, packed_grad, grad_mixed, sent, keep = call(

time: 131 us -> 131 us (level)
  transfers between devices with their start and end apart: 14 -> 14, of which waited for: 7 -> 7; matrix products, arithmetic and copies ran while one was open for 5% -> 5% of each run, Pallas kernels for 17% -> 14%
where the time goes in v5:
time: 131 us; the launch traced here: 130 us
  starting transfers between devices  35.4 us (27%)
  Pallas kernels  26.8 us (20%)
  waiting for transfers between devices  26 us (20%)
  between operations  16.3 us (12%)
  local copies, waits for them, and re-layouts  13.7 us (10%)
  blocking collectives  8.79 us (7%)
  other arithmetic  3.01 us (2%)
    unnamed x28, local copies, waits for them, and re-layouts  10.9 us
    all_to_all x1, blocking collectives, shards(): lax.all_to_all(att.reshape(HEADS, HALF, 128), LON, 0, 0, tiled=True)  8.79 us
    pallas_call x1, Pallas kernels, shards(): call(attend_back_kernel, [((ROWS, 384), BF16)], [SMEM] + [VMEM] * 4, [plt...  8.23 us
    ppermute x1, waiting for transfers between devices, shards(): grad_back = lax.ppermute(grad_low, LAT, backward)  7.7 us
    all_to_all x1, waiting for transfers between devices, shards(): heads = lax.all_to_all(packed, LON, 0, 0, tiled=True).reshape(ROWS, 384)  6.38 us
    all_to_all x1, waiting for transfers between devices, shards(): lax.all_to_all(packed_grad, LON, 0, 0, tiled=True).reshape(ROWS, 128)  6.09 us
    all_to_all x1, starting transfers between devices, shards(): got = lax.all_to_all(joined, ('zh',) + LON, 0, 0, tiled=True)  5.45 us
    ppermute x1, starting transfers between devices, shards(): low = lax.ppermute(low, LAT, forward)  5.06 us
  transfers between devices with their start and end apart: 14, of which 7 were waited for; matrix products, arithmetic and copies ran while one was open for 5% of the time, Pallas kernels for 14%

profile of v5, /device:TPU:1, one launch (start us, length us, event | category | flops | bytes accessed | tf_op | source)
XLA Modules:
  0.0 130.1 jit_solution(3865550262022644257)
XLA Ops:
  8.0 1.9 %shard_map.153 = (bf16[192,512]{1,0:T(8,128)(2,1)}, bf16[192,512]{1,0:T(8,128)(2,1)}) custom-call(bf16[3,4,16,512]{3,2,1,0:T(8,128)(2,1)} %field_hbm.1, s32[4,16]{1,0:T(4,128)} %mask_hbm.1, bf16[2,512]{1,0:T(2,128)(2,1)} %embed_hbm.1, bf16[3,4,16,512]{3,2,1,0:T(8,128)(2,1)} %cot_hbm.1), custom_call_target="tpu_custom_call" | custom-call | bytes 3000000 | tf_op jit(solution)/shard_map/pallas_call | solution.py:446
  10.0 5.1 %collective-permute-start = (bf16[192,512]{1,0:T(8,128)(2,1)}, bf16[192,512]{1,0:T(8,128)(2,1)S(1)}, u32[]{:S(2)}, u32[]{:S(2)}) collective-permute-start(bf16[192,512]{1,0:T(8,128)(2,1)} %get-tuple-element.46), channel_id=1, source_target_pairs={{0,8},{8,16},{16,24},{24,32},{32,40},{40,48},{48,56},{56,64},{64,7... | collective-permute-start | bytes 589832 | tf_op jit(solution)/shard_map/ppermute | solution.py:459
  15.0 1.4 %copy-done.3 = bf16[512,1536]{1,0:T(8,128)(2,1)S(1)} copy-done((bf16[512,1536]{1,0:T(8,128)(2,1)S(1)}, bf16[512,1536]{1,0:T(8,128)(2,1)}, u32[]{:S(2)}) %copy-start.3) | copy-done | bytes 1572888
  19.3 1.6 %shard_map.155 = (bf16[2,96,512]{2,1,0:T(8,128)(2,1)}, bf16[8,96,384]{2,1,0:T(8,128)(2,1)}) custom-call(bf16[192,512]{1,0:T(8,128)(2,1)S(1)} %collective-permute-done.low_ref, bf16[192,512]{1,0:T(8,128)(2,1)S(1)} %copy-done.2, f32[2,512]{1,0:T(2,128)S(1)} %get-tuple-element.51.gain_ref, bf16[512,1536]{1,0:T(8,128)(2,1)S(1)} %get-tuple-element.52.w_ref), custom_call_target="tpu_custom_call" | custom-call | bytes 8000000 | tf_op jit(solution)/shard_map/pallas_call | solution.py:475
  20.8 4.7 %all-to-all-start = ((bf16[8,96,384]{2,1,0:T(8,128)(2,1)}), bf16[8,96,384]{2,1,0:T(8,128)(2,1)S(1)}, u32[]{:S(2)}, u32[]{:S(2)}) async-start(bf16[8,96,384]{2,1,0:T(8,128)(2,1)} %get-tuple-element.53), calls=%async_computation | async-start | bytes 1179648 | tf_op jit(solution)/shard_map/all_to_all | solution.py:482
  27.8 6.4 %all-to-all-done = bf16[8,96,384]{2,1,0:T(8,128)(2,1)S(1)} async-done(((bf16[8,96,384]{2,1,0:T(8,128)(2,1)}), bf16[8,96,384]{2,1,0:T(8,128)(2,1)S(1)}, u32[]{:S(2)}, u32[]{:S(2)}) %all-to-all-start) | async-done | bytes 589856 | tf_op jit(solution)/shard_map/all_to_all | solution.py:482
  34.2 3.7 %shard_map.156 = (bf16[768,128]{1,0:T(8,128)(2,1)S(1)}, f32[768,128]{1,0:T(8,128)S(1)}) custom-call(f32[3]{0:T(128)S(1)} %pad_maximum_fusion.2.scal_ref, bf16[768,384]{1,0:T(8,128)(2,1)S(1)} %bitcast.12), custom_call_target="tpu_custom_call" | custom-call | bytes 20000000 | tf_op jit(solution)/shard_map/pallas_call | solution.py:487
  38.7 8.8 %all_to_all.25.att_ref = bf16[8,96,128]{2,1,0:T(8,128)(2,1)S(1)} all-to-all(bf16[8,96,128]{2,1,0:T(8,128)(2,1)S(1)} %bitcast.15), channel_id=1, replica_groups=mesh['x'=4,'zh'=2,'c'=2,'zl'=2,'y'=4] {'zl','y'}, dimensions={0} | all-to-all | bytes 393216 | tf_op jit(solution)/shard_map/all_to_all | solution.py:501
  47.5 1.6 %copy-done = bf16[512,2048]{1,0:T(8,128)(2,1)S(1)} copy-done((bf16[512,2048]{1,0:T(8,128)(2,1)S(1)}, bf16[512,2048]{1,0:T(8,128)(2,1)}, u32[]{:S(2)}) %copy-start) | copy-done | bytes 2097176
  49.1 1.6 %copy-done.1 = bf16[2048,512]{1,0:T(8,128)(2,1)S(1)} copy-done((bf16[2048,512]{1,0:T(8,128)(2,1)S(1)}, bf16[2048,512]{1,0:T(8,128)(2,1)}, u32[]{:S(2)}) %copy-start.1) | copy-done | bytes 2097176
  50.7 4.0 %shard_map.157 = (bf16[96,512]{1,0:T(8,128)(2,1)S(1)}, bf16[96,512]{1,0:T(8,128)(2,1)S(1)}, bf16[8,96,128]{2,1,0:T(8,128)(2,1)}, f32[192,512]{1,0:T(8,128)S(1)},...) custom-call(s32[1]{0:T(128)} %bitcast.core_ref, bf16[8,96,128]{2,1,0:T(8,128)(2,1)S(1)} %all_to_all.25.att_ref, ...), custom_call_target="tpu_custom_call" | custom-call | bytes 3000000 | tf_op jit(solution)/shard_map/pallas_call | solution.py:503
  56.1 3.8 %collective-permute-start.3 = (bf16[192,4608]{1,0:T(8,128)(2,1)S(1)}, bf16[192,4608]{1,0:T(8,128)(2,1)S(1)}, u32[]{:S(2)}, u32[]{:S(2)}) collective-permute-start(bf16[192,4608]{1,0:T(8,128)(2,1)S(1)} %get-tuple-element.69.sent_ref), channel_id=1, source_target_pairs={{0,8},{8,0},{1,9},{9,1},{2,10},{10,2},{3,11},{11,3},{4,12},{12,4},... | collective-permute-start | bytes 5308424 | tf_op jit(solution)/shard_map/ppermute | solution.py:517
  59.9 3.3 %collective-permute-done.3.got_ref = bf16[192,4608]{1,0:T(8,128)(2,1)S(1)} collective-permute-done((bf16[192,4608]{1,0:T(8,128)(2,1)S(1)}, bf16[192,4608]{1,0:T(8,128)(2,1)S(1)}, u32[]{:S(2)}, u32[]{:S(2)}) %collective-permute-start.3) | collective-permute-done | bytes 1769504 | tf_op jit(solution)/shard_map/ppermute | solution.py:517
  63.2 2.8 %shard_map.160 = bf16[8,32,4608]{2,1,0:T(8,128)(2,1)} custom-call(bf16[192,1536]{1,0:T(8,128)(2,1)S(1)} %get-tuple-element.68.keep_ref, bf16[192,4608]{1,0:T(8,128)(2,1)S(1)} %get-tuple-element.69.sent_ref, bf16[192,4608]{1,0:T(8,128)(2,1)S(1)} %collective-permute-done.3.got_ref), custom_call_target="tpu_custom_call" | custom-call | bytes 3000000 | tf_op jit(solution)/shard_map/pallas_call | solution.py:519
  66.1 3.5 %all-to-all-start.2 = ((bf16[8,96,128]{2,1,0:T(8,128)(2,1)}), bf16[8,96,128]{2,1,0:T(8,128)(2,1)S(1)}, u32[]{:S(2)}, u32[]{:S(2)}) async-start(bf16[8,96,128]{2,1,0:T(8,128)(2,1)} %get-tuple-element.60), calls=%async_computation.2 | async-start | bytes 393216 | tf_op jit(solution)/shard_map/all_to_all | solution.py:516
  70.3 6.1 %all-to-all-done.2 = bf16[8,96,128]{2,1,0:T(8,128)(2,1)S(1)} async-done(((bf16[8,96,128]{2,1,0:T(8,128)(2,1)}), bf16[8,96,128]{2,1,0:T(8,128)(2,1)S(1)}, u32[]{:S(2)}, u32[]{:S(2)}) %all-to-all-start.2) | async-done | bytes 196640 | tf_op jit(solution)/shard_map/all_to_all | solution.py:516
  76.3 8.2 %shard_map.158.packed_ref = bf16[768,384]{1,0:T(8,128)(2,1)} custom-call(f32[3]{0:T(128)S(1)} %pad_maximum_fusion.2.scal_ref, bf16[768,384]{1,0:T(8,128)(2,1)S(1)} %bitcast.13, bf16[768,128]{1,0:T(8,128)(2,1)S(1)} %bitcast.16, bf16[768,128]{1,0:T(8,128)(2,1)S(1)} %get-tuple-element.58.att_ref, f32[768,128]{1,0:T(8,128)S(1)} %copy-done.8), custom_call_target="tpu_custom_call" | custom-call | bytes 1000000000 | tf_op jit(solution)/shard_map/pallas_call | solution.py:525
  84.6 3.5 %all-to-all-start.3 = ((bf16[8,96,384]{2,1,0:T(8,128)(2,1)}), bf16[8,96,384]{2,1,0:T(8,128)(2,1)S(1)}, u32[]{:S(2)}, u32[]{:S(2)}) async-start(bf16[8,96,384]{2,1,0:T(8,128)(2,1)} %bitcast.7), calls=%async_computation.3 | async-start | bytes 1179648 | tf_op jit(solution)/shard_map/all_to_all | solution.py:540
  88.2 1.4 %copy-done.4 = bf16[16,96,512]{2,1,0:T(8,128)(2,1)S(1)} copy-done((bf16[16,96,512]{2,1,0:T(8,128)(2,1)S(1)}, bf16[16,96,512]{2,1,0:T(8,128)(2,1)}, u32[]{:S(2)}) %copy-start.4) | copy-done | bytes 1572888
  89.6 1.9 %shard_map.161 = (bf16[8,32,192]{2,1,0:T(8,128)(2,1)S(1)}, bf16[8,32,192]{2,1,0:T(8,128)(2,1)S(1)}) custom-call(s32[1]{0:T(128)} %bitcast.core_ref, bf16[768,384]{1,0:T(8,128)(2,1)} %shard_map.158.packed_ref, bf16[8,2,96,512]{3,2,1,0:T(8,128)(2,1)S(1)} %bitcast.14), custom_call_target="tpu_custom_call" | custom-call | bytes 3000000 | tf_op jit(solution)/shard_map/pallas_call | solution.py:543
  91.5 2.0 %collective-permute-start.4 = (bf16[8,32,192]{2,1,0:T(8,128)(2,1)S(1)}, bf16[8,32,192]{2,1,0:T(8,128)(2,1)S(1)}, u32[]{:S(2)}, u32[]{:S(2)}) collective-permute-start(bf16[8,32,192]{2,1,0:T(8,128)(2,1)S(1)} %get-tuple-element.72), channel_id=1, source_target_pairs={{0,8},{8,0},{1,9},{9,1},{2,10},{10,2},{3,11},{11,3},{4,12},{12,4},... | collective-permute-start | bytes 294920 | tf_op jit(solution)/shard_map/ppermute | solution.py:546
  93.5 1.0 collective-permute-done.4.theirs_ref
  94.5 1.2 collective-permute-start.5
  95.7 1.8 %collective-permute-start.6 = (bf16[2,32,192]{2,1,0:T(8,128)(2,1)S(1)}, bf16[2,32,192]{2,1,0:T(8,128)(2,1)S(1)}, u32[]{:S(2)}, u32[]{:S(2)}) collective-permute-start(bf16[2,32,192]{2,1,0:T(8,128)(2,1)S(1)} %get-tuple-element.75), channel_id=1, source_target_pairs={{0,64},{32,96},{64,0},{96,32},{1,65},{33,97},{65,1},{97,33},{2,66}... | collective-permute-start | bytes 73736 | tf_op jit(solution)/shard_map/ppermute | solution.py:551
  97.4 1.9 %collective-permute-start.7 = (bf16[2,32,192]{2,1,0:T(8,128)(2,1)S(1)}, bf16[2,32,192]{2,1,0:T(8,128)(2,1)S(1)}, u32[]{:S(2)}, u32[]{:S(2)}) collective-permute-start(bf16[2,32,192]{2,1,0:T(8,128)(2,1)S(1)} %get-tuple-element.76), channel_id=1, source_target_pairs={{0,96},{32,0},{64,32},{96,64},{1,97},{33,1},{65,33},{97,65},{2,98}... | collective-permute-start | bytes 73736 | tf_op jit(solution)/shard_map/ppermute | solution.py:551
  100.9 1.1 copy-done.5
  101.9 0.9 shard_map.163
  102.8 5.5 %all-to-all-start.4 = ((bf16[16,4,4864]{2,1,0:T(4,128)(2,1)}), bf16[16,4,4864]{2,1,0:T(4,128)(2,1)S(1)}, u32[]{:S(2)}, u32[]{:S(2)}) async-start(bf16[16,4,4864]{2,1,0:T(4,128)(2,1)} %shard_map.163), calls=%async_computation.5 | async-start | bytes 1245184 | tf_op jit(solution)/shard_map/all_to_all | solution.py:562
  108.3 1.0 copy-done.10
  110.1 1.8 %collective-permute-start.2 = (bf16[96,512]{1,0:T(8,128)(2,1)S(1)}, bf16[96,512]{1,0:T(8,128)(2,1)S(1)}, u32[]{:S(2)}, u32[]{:S(2)}) collective-permute-start(bf16[96,512]{1,0:T(8,128)(2,1)S(1)} %get-tuple-element.67), channel_id=1, source_target_pairs={{8,0},{16,8},{24,16},{32,24},{40,32},{48,40},{56,48},{64,56},{72,6... | collective-permute-start | bytes 294920 | tf_op jit(solution)/shard_map/ppermute | solution.py:560
  111.9 1.6 %pad_maximum_fusion = bf16[3,4,16,512]{3,2,1,0:T(8,128)(2,1)} fusion(bf16[3,2,16,512]{3,2,1,0:T(8,128)(2,1)} %bitcast.6, bf16[3,2,16,512]{3,2,1,0:T(8,128)(2,1)S(1)} %bitcast.17), kind=kLoop, calls=%fused_computation | loop fusion | flops 98304 | bytes 393216 | tf_op jit(solution)/shard_map/concatenate | solution.py:577
  113.5 7.7 %collective-permute-done.2 = bf16[96,512]{1,0:T(8,128)(2,1)S(1)} collective-permute-done((bf16[96,512]{1,0:T(8,128)(2,1)S(1)}, bf16[96,512]{1,0:T(8,128)(2,1)S(1)}, u32[]{:S(2)}, u32[]{:S(2)}) %collective-permute-start.2) | collective-permute-done | bytes 98336 | tf_op jit(solution)/shard_map/ppermute | solution.py:560
  (46 shorter events, 11.1 us)
Async XLA Ops:
  8.0 9.2 %copy-start.13 = (f32[8]{0:T(128)S(1)}, f32[8]{0:T(128)}, u32[]{:S(2)}) copy-start(f32[8]{0:T(128)} %param.15) | copy-start | bytes 100
  9.9 9.3 %copy-start.2 = (bf16[192,512]{1,0:T(8,128)(2,1)S(1)}, bf16[192,512]{1,0:T(8,128)(2,1)}, u32[]{:S(2)}) copy-start(bf16[192,512]{1,0:T(8,128)(2,1)} %get-tuple-element.50.up_ref) | copy-start | bytes 589828
  10.0 9.3 %collective-permute-start = (bf16[192,512]{1,0:T(8,128)(2,1)}, bf16[192,512]{1,0:T(8,128)(2,1)S(1)}, u32[]{:S(2)}, u32[]{:S(2)}) collective-permute-start(bf16[192,512]{1,0:T(8,128)(2,1)} %get-tuple-element.46), channel_id=1, source_target_pairs={{0,8},{8,16},{16,24},{24,32},{32,40},{40,48},{48,56},{56,64},{64,7... | collective-permute-start | bytes 589832 | tf_op jit(solution)/shard_map/ppermute | solution.py:459
  15.0 1.4 %copy-start.3 = (bf16[512,1536]{1,0:T(8,128)(2,1)S(1)}, bf16[512,1536]{1,0:T(8,128)(2,1)}, u32[]{:S(2)}) copy-start(bf16[512,1536]{1,0:T(8,128)(2,1)} %refs_0_.1) | copy-start | bytes 4718596
  16.4 0.7 copy-start.11
  19.3 28.3 %copy-start.6 = (bf16[512,512]{1,0:T(8,128)(2,1)S(1)}, bf16[512,512]{1,0:T(8,128)(2,1)}, u32[]{:S(2)}) copy-start(bf16[512,512]{1,0:T(8,128)(2,1)} %w_out_ref.1) | copy-start | bytes 1572868
  20.8 13.3 %all-to-all-start = ((bf16[8,96,384]{2,1,0:T(8,128)(2,1)}), bf16[8,96,384]{2,1,0:T(8,128)(2,1)S(1)}, u32[]{:S(2)}, u32[]{:S(2)}) async-start(bf16[8,96,384]{2,1,0:T(8,128)(2,1)} %get-tuple-element.53), calls=%async_computation | async-start | bytes 1179648 | tf_op jit(solution)/shard_map/all_to_all | solution.py:482
  25.5 62.7 %all-gather.3.cloned.1.call-start = ((), (), s32[]{:S(2)}) async-start(), calls=%async_computation.7 | async-start | bytes 1769472 | tf_op jit(solution)/shard_map/all_gather | solution.py:500
  37.9 0.7 copy-start.7
  38.7 62.2 %reduce-scatter.2.cloned.1.call-start = ((), (), s32[]{:S(2)}) async-start(), calls=%async_computation.6 | async-start | bytes 2949120 | tf_op jit(solution)/shard_map/reduce_scatter | solution.py:522
  47.5 1.6 %copy-start = (bf16[512,2048]{1,0:T(8,128)(2,1)S(1)}, bf16[512,2048]{1,0:T(8,128)(2,1)}, u32[]{:S(2)}) copy-start(bf16[512,2048]{1,0:T(8,128)(2,1)} %w_up_ref.1) | copy-start | bytes 6291460
  49.1 1.6 %copy-start.1 = (bf16[2048,512]{1,0:T(8,128)(2,1)S(1)}, bf16[2048,512]{1,0:T(8,128)(2,1)}, u32[]{:S(2)}) copy-start(bf16[2048,512]{1,0:T(8,128)(2,1)} %w_down_ref.1) | copy-start | bytes 6291460
  54.7 0.8 copy-start.9
  55.5 0.6 copy-start.12
  56.1 7.1 %collective-permute-start.3 = (bf16[192,4608]{1,0:T(8,128)(2,1)S(1)}, bf16[192,4608]{1,0:T(8,128)(2,1)S(1)}, u32[]{:S(2)}, u32[]{:S(2)}) collective-permute-start(bf16[192,4608]{1,0:T(8,128)(2,1)S(1)} %get-tuple-element.69.sent_ref), channel_id=1, source_target_pairs={{0,8},{8,0},{1,9},{9,1},{2,10},{10,2},{3,11},{11,3},{4,12},{12,4},... | collective-permute-start | bytes 5308424 | tf_op jit(solution)/shard_map/ppermute | solution.py:517
  66.1 10.3 %copy-start.8 = (f32[768,128]{1,0:T(8,128)S(1)}, f32[768,128]{1,0:T(8,128)}, u32[]{:S(2)}) copy-start(f32[768,128]{1,0:T(8,128)} %copy-done.7) | copy-start | bytes 1179652
  66.1 10.3 %all-to-all-start.2 = ((bf16[8,96,128]{2,1,0:T(8,128)(2,1)}), bf16[8,96,128]{2,1,0:T(8,128)(2,1)S(1)}, u32[]{:S(2)}, u32[]{:S(2)}) async-start(bf16[8,96,128]{2,1,0:T(8,128)(2,1)} %get-tuple-element.60), calls=%async_computation.2 | async-start | bytes 393216 | tf_op jit(solution)/shard_map/all_to_all | solution.py:516
  69.6 15.0 %collective-permute-start.1 = (bf16[96,512]{1,0:T(8,128)(2,1)}, bf16[96,512]{1,0:T(8,128)(2,1)}, u32[]{:S(2)}, u32[]{:S(2)}) collective-permute-start(bf16[96,512]{1,0:T(8,128)(2,1)} %copy-done.12), channel_id=1, source_target_pairs={{8,0},{16,8},{24,16},{32,24},{40,32},{48,40},{56,48},{64,56},{72,6... | collective-permute-start | bytes 294920 | tf_op jit(solution)/shard_map/ppermute | solution.py:518
  84.6 18.2 %all-to-all-start.3 = ((bf16[8,96,384]{2,1,0:T(8,128)(2,1)}), bf16[8,96,384]{2,1,0:T(8,128)(2,1)S(1)}, u32[]{:S(2)}, u32[]{:S(2)}) async-start(bf16[8,96,384]{2,1,0:T(8,128)(2,1)} %bitcast.7), calls=%async_computation.3 | async-start | bytes 1179648 | tf_op jit(solution)/shard_map/all_to_all | solution.py:540
  88.2 1.4 %copy-start.4 = (bf16[16,96,512]{2,1,0:T(8,128)(2,1)S(1)}, bf16[16,96,512]{2,1,0:T(8,128)(2,1)}, u32[]{:S(2)}) copy-start(bf16[16,96,512]{2,1,0:T(8,128)(2,1)} %all-gather.3.cloned.1.call-done) | copy-start | bytes 4718596
  91.5 3.0 %collective-permute-start.4 = (bf16[8,32,192]{2,1,0:T(8,128)(2,1)S(1)}, bf16[8,32,192]{2,1,0:T(8,128)(2,1)S(1)}, u32[]{:S(2)}, u32[]{:S(2)}) collective-permute-start(bf16[8,32,192]{2,1,0:T(8,128)(2,1)S(1)} %get-tuple-element.72), channel_id=1, source_target_pairs={{0,8},{8,0},{1,9},{9,1},{2,10},{10,2},{3,11},{11,3},{4,12},{12,4},... | collective-permute-start | bytes 294920 | tf_op jit(solution)/shard_map/ppermute | solution.py:546
  94.5 4.9 %collective-permute-start.5 = (bf16[2,32,192]{2,1,0:T(8,128)(2,1)S(1)}, bf16[2,32,192]{2,1,0:T(8,128)(2,1)S(1)}, u32[]{:S(2)}, u32[]{:S(2)}) collective-permute-start(bf16[2,32,192]{2,1,0:T(8,128)(2,1)S(1)} %get-tuple-element.74), channel_id=1, source_target_pairs={{0,32},{32,64},{64,96},{96,0},{1,33},{33,65},{65,97},{97,1},{2,34}... | collective-permute-start | bytes 73736 | tf_op jit(solution)/shard_map/ppermute | solution.py:551
  95.7 4.3 %collective-permute-start.6 = (bf16[2,32,192]{2,1,0:T(8,128)(2,1)S(1)}, bf16[2,32,192]{2,1,0:T(8,128)(2,1)S(1)}, u32[]{:S(2)}, u32[]{:S(2)}) collective-permute-start(bf16[2,32,192]{2,1,0:T(8,128)(2,1)S(1)} %get-tuple-element.75), channel_id=1, source_target_pairs={{0,64},{32,96},{64,0},{96,32},{1,65},{33,97},{65,1},{97,33},{2,66}... | collective-permute-start | bytes 73736 | tf_op jit(solution)/shard_map/ppermute | solution.py:551
  97.4 3.4 %collective-permute-start.7 = (bf16[2,32,192]{2,1,0:T(8,128)(2,1)S(1)}, bf16[2,32,192]{2,1,0:T(8,128)(2,1)S(1)}, u32[]{:S(2)}, u32[]{:S(2)}) collective-permute-start(bf16[2,32,192]{2,1,0:T(8,128)(2,1)S(1)} %get-tuple-element.76), channel_id=1, source_target_pairs={{0,96},{32,0},{64,32},{96,64},{1,97},{33,1},{65,33},{97,65},{2,98}... | collective-permute-start | bytes 73736 | tf_op jit(solution)/shard_map/ppermute | solution.py:551
  100.9 1.1 copy-start.5
  102.8 19.1 %all-to-all-start.4 = ((bf16[16,4,4864]{2,1,0:T(4,128)(2,1)}), bf16[16,4,4864]{2,1,0:T(4,128)(2,1)S(1)}, u32[]{:S(2)}, u32[]{:S(2)}) async-start(bf16[16,4,4864]{2,1,0:T(4,128)(2,1)} %shard_map.163), calls=%async_computation.5 | async-start | bytes 1245184 | tf_op jit(solution)/shard_map/all_to_all | solution.py:562
  108.3 1.0 copy-start.10
  110.1 11.1 %collective-permute-start.2 = (bf16[96,512]{1,0:T(8,128)(2,1)S(1)}, bf16[96,512]{1,0:T(8,128)(2,1)S(1)}, u32[]{:S(2)}, u32[]{:S(2)}) collective-permute-start(bf16[96,512]{1,0:T(8,128)(2,1)S(1)} %get-tuple-element.67), channel_id=1, source_target_pairs={{8,0},{16,8},{24,16},{32,24},{40,32},{48,40},{56,48},{64,56},{72,6... | collective-permute-start | bytes 294920 | tf_op jit(solution)/shard_map/ppermute | solution.py:560
Sparse Core Ops, SparseCore 0:
  38.8 34.6 all-gather.2
Sparse Core Ops, SparseCore 1:
  66.2 29.5 reduce-scatter.1
